TPU v7x, 512 devices: a whole 4x8x8 slice. The times are simulated.
512 devices in a mesh: inner: 32 (over y, x), outer: 16 (over z, core).
Axes of the slice: x: 4, y: 8, z: 8, core: 2. Of those that a mesh axis runs over, the one named last changes fastest.
Arguments:
- query: bfloat16 [65536, 768], P(('inner', 'outer')), may hold values from -8 to 8
- keys: bfloat16 [65536, 768], P(('inner', 'outer')), may hold values from -8 to 8
- values: bfloat16 [65536, 768], P(('inner', 'outer')), may hold values from -6 to 6
- dout: bfloat16 [65536, 768], P(('inner', 'outer')), may hold values from -6 to 6
- partners: int32 [512, 7], P(('inner', 'outer')), may hold values from 0 to 511, as said below
- counts: int32 [512], P(('inner', 'outer')), may hold values from 1 to 7, as said below
Outputs:
- dquery: bfloat16 [65536, 768], P(('inner', 'outer'))
- dkeys: bfloat16 [65536, 768], P(('inner', 'outer'))
- dvalues: bfloat16 [65536, 768], P(('inner', 'outer'))
Inputs may be any that keep to these rules, and one draw needn't show every extreme that they name: Block b has the coordinates z = b mod 16, x = (b div 16) mod 4, y = b div (64). partners[b, 0] is b; slots 1 to counts[b] - 1 hold distinct blocks that differ from b by one step in exactly one of x, y, z and lie in the volume (x below 4, y below 8, z below 16), in the order x+1, x-1, y+1, y-1, z+1, z-1 of those present; the remaining slots hold b. counts[b] is one more than the number of neighbours that block b lists; some block lists every neighbour it has in the volume.
All inputs are finite; a program needn't handle non-finite values.
Results may differ from a plain program's by a relative error of at most 0.011.
Values may be sent and summed in bfloat16 or wider, within the bound.
No kernel may reach another device: no remote copies, remote signals or barrier semaphores. Data moves between devices by JAX's collectives and lax.ppermute only.
A program may use at most 64 MiB of HBM per device.

v0:
```python
from functools import reduce

import jax
import jax.numpy as jnp
from jax import lax
from jax.sharding import PartitionSpec as P

HEADS = 6
HD = 128
ROW_W = 4


neg_large = -1e30


def passed_along(block, axis, distance):
    devices = range(lax.axis_size(axis))
    route = [(i - distance, i) for i in devices if i - distance in devices]
    return lax.ppermute(block, axis, route)


def head_view(matrix):
    return matrix.reshape(matrix.shape[0], HEADS, HD)


def block_scores(query_heads, key_heads):
    return jnp.einsum(
        "qhd,khd->hqk", query_heads, key_heads, preferred_element_type=jnp.float32
    ) * HD ** (-0.5)


def mix_rows(weights, row_heads):
    return jnp.einsum("hqk,khd->qhd", weights, row_heads, preferred_element_type=jnp.float32)


def back_rows(weights, row_heads):
    return jnp.einsum("hqk,qhd->khd", weights, row_heads, preferred_element_type=jnp.float32)


def guarded(action, operands):
    return action(*operands)


def on_device(query, keys, values, dout, partners, counts):
    outer_count = lax.axis_size("outer")
    block_id = lax.axis_index("inner") * outer_count + lax.axis_index("outer")
    live_slots = jnp.arange(partners.shape[1]) < counts[0]
    inner_steps = (1, -1, ROW_W, -ROW_W)
    outer_steps = (1, -1)

    def listed(offset):
        return jnp.any((partners[0] == block_id + offset) & live_slots)

    flags = (
        [jnp.array(True)]
        + [listed(step * outer_count) for step in inner_steps]
        + [listed(step) for step in outer_steps]
    )
    blocks = [(keys, values)]
    for step in inner_steps:
        blocks.append(passed_along((keys, values), "inner", -step))
    for step in outer_steps:
        blocks.append(passed_along((keys, values), "outer", -step))
    query_heads = head_view(query)
    dout_heads = head_view(dout)
    rows = query.shape[0]
    row_shape = (rows, HEADS, HD)
    score_list = []
    for index in range(len(blocks)):
        key_heads = head_view(blocks[index][0])
        if index == 0:
            score_list.append(block_scores(query_heads, key_heads))
        else:
            score_list.append(
                jnp.where(flags[index], block_scores(query_heads, key_heads), neg_large)
            )
    row_max = reduce(jnp.maximum, [scores.max(axis=2) for scores in score_list])
    total = sum((jnp.sum(jnp.exp(scores - row_max[:, :, None]), axis=2) for scores in score_list))
    log_total = row_max + jnp.log(total)
    probs = [jnp.exp(scores - log_total[:, :, None]) for scores in score_list]
    probs_low = [prob.astype(jnp.bfloat16) for prob in probs]
    attended = jnp.zeros(row_shape, jnp.float32)
    for index in range(len(blocks)):
        attended = attended + guarded(mix_rows, (probs_low[index], head_view(blocks[index][1])))
    delta = jnp.sum(dout_heads.astype(jnp.float32) * attended, axis=2).T

    def score_grad(prob, value_heads):
        grads = jnp.einsum(
            "qhd,khd->hqk", dout_heads, value_heads, preferred_element_type=jnp.float32
        )
        return prob * (grads - delta[:, :, None])

    query_grad = jnp.zeros(row_shape, jnp.float32)
    key_parts = []
    for index in range(len(blocks)):
        dscores = guarded(score_grad, (probs[index], head_view(blocks[index][1]))).astype(
            jnp.bfloat16
        )
        query_grad = query_grad + guarded(mix_rows, (dscores, head_view(blocks[index][0])))
        key_parts.append((dscores, probs_low[index]))
    key_grad = back_rows(key_parts[0][0], query_heads)
    value_grad = back_rows(key_parts[0][1], dout_heads)
    returned = []
    for index in range(1, len(blocks)):
        returned.append(
            (
                back_rows(key_parts[index][0], query_heads),
                back_rows(key_parts[index][1], dout_heads),
            )
        )
    for position, step in enumerate(inner_steps):
        terms = returned[position]
        arrived = passed_along((terms[0], terms[1]), "inner", step)
        key_grad = key_grad + arrived[0]
        value_grad = value_grad + arrived[1]
    for position, step in enumerate(outer_steps):
        terms = returned[4 + position]
        arrived = passed_along((terms[0], terms[1]), "outer", step)
        key_grad = key_grad + arrived[0]
        value_grad = value_grad + arrived[1]
    scale = HD ** (-0.5)
    width = query.shape[1]
    query_out = (query_grad * scale).astype(jnp.bfloat16).reshape(rows, width)
    key_out = (key_grad * scale).astype(jnp.bfloat16).reshape(rows, width)
    value_out = value_grad.astype(jnp.bfloat16).reshape(rows, width)
    return (query_out, key_out, value_out)


def solution(mesh):
    return jax.shard_map(
        on_device,
        mesh=mesh,
        in_specs=(
            P(("inner", "outer"), None),
            P(("inner", "outer"), None),
            P(("inner", "outer"), None),
            P(("inner", "outer"), None),
            P(("inner", "outer"), None),
            P(("inner", "outer")),
        ),
        out_specs=(
            P(("inner", "outer"), None),
            P(("inner", "outer"), None),
            P(("inner", "outer"), None),
        ),
        check_vma=False,
    )
```

profile of v0, /device:TPU:225, one launch (start us, length us, event | category | flops | bytes accessed | tf_op | source)
XLA Modules:
  0.0 156.7 jit_solution(348059217169590636)
XLA Ops:
  0.6 1.1 copy.98
  1.7 5.8 %collective-permute-start.5 = (bf16[128,768]{0,1:T(8,128)(2,1)S(1)}, bf16[128,768]{0,1:T(8,128)(2,1)S(1)}, u32[]{:S(2)}, u32[]{:S(2)}) collective-permute-start(bf16[128,768]{0,1:T(8,128)(2,1)S(1)} %copy.98), channel_id=1, source_target_pairs={{0,1},{1,2},{2,3},{3,4},{4,5},{5,6},{6,7},{7,8},{8,9},{9,10},{10,1... | collective-permute-start | bytes 589832 | tf_op jit(solution)/shard_map/ppermute | solution.py:19
  7.5 1.9 %collective-permute-start.4 = (bf16[128,768]{0,1:T(8,128)(2,1)S(1)}, bf16[128,768]{0,1:T(8,128)(2,1)S(1)}, u32[]{:S(2)}, u32[]{:S(2)}) collective-permute-start(bf16[128,768]{0,1:T(8,128)(2,1)S(1)} %copy.98), channel_id=1, source_target_pairs={{1,0},{2,1},{3,2},{4,3},{5,4},{6,5},{7,6},{8,7},{9,8},{10,9},{11,1... | collective-permute-start | bytes 589832 | tf_op jit(solution)/shard_map/ppermute | solution.py:19
  9.4 2.3 %collective-permute-start.3 = (bf16[128,768]{0,1:T(8,128)(2,1)S(1)}, bf16[128,768]{0,1:T(8,128)(2,1)S(1)}, u32[]{:S(2)}, u32[]{:S(2)}) collective-permute-start(bf16[128,768]{0,1:T(8,128)(2,1)S(1)} %copy.98), channel_id=1, source_target_pairs={{0,64},{16,80},{32,96},{48,112},{64,128},{80,144},{96,160},{112,17... | collective-permute-start | bytes 589832 | tf_op jit(solution)/shard_map/ppermute | solution.py:19
  11.7 4.2 %collective-permute-start.2 = (bf16[128,768]{0,1:T(8,128)(2,1)S(1)}, bf16[128,768]{0,1:T(8,128)(2,1)S(1)}, u32[]{:S(2)}, u32[]{:S(2)}) collective-permute-start(bf16[128,768]{0,1:T(8,128)(2,1)S(1)} %copy.98), channel_id=1, source_target_pairs={{64,0},{80,16},{96,32},{112,48},{128,64},{144,80},{160,96},{176,11... | collective-permute-start | bytes 589832 | tf_op jit(solution)/shard_map/ppermute | solution.py:19
  15.9 5.4 %collective-permute-start.11 = (bf16[128,768]{1,0:T(8,128)(2,1)}, bf16[128,768]{1,0:T(8,128)(2,1)}, u32[]{:S(2)}, u32[]{:S(2)}) collective-permute-start(bf16[128,768]{1,0:T(8,128)(2,1)} %param.8), channel_id=1, source_target_pairs={{0,1},{1,2},{2,3},{3,4},{4,5},{5,6},{6,7},{7,8},{8,9},{9,10},{10,1... | collective-permute-start | bytes 589832 | tf_op jit(solution)/shard_map/ppermute | solution.py:19
  21.4 1.1 copy.120
  22.7 0.8 copy-done.26
  24.9 0.8 fusion.79
  26.0 3.1 %collective-permute-start.1 = (bf16[128,768]{0,1:T(8,128)(2,1)S(1)}, bf16[128,768]{0,1:T(8,128)(2,1)S(1)}, u32[]{:S(2)}, u32[]{:S(2)}) collective-permute-start(bf16[128,768]{0,1:T(8,128)(2,1)S(1)} %copy.98), channel_id=1, source_target_pairs={{0,16},{16,32},{32,48},{48,64},{64,80},{80,96},{96,112},{112,128},... | collective-permute-start | bytes 589832 | tf_op jit(solution)/shard_map/ppermute | solution.py:19
  29.1 0.9 fusion.80
  30.1 5.5 %collective-permute-start = (bf16[128,768]{0,1:T(8,128)(2,1)S(1)}, bf16[128,768]{0,1:T(8,128)(2,1)S(1)}, u32[]{:S(2)}, u32[]{:S(2)}) collective-permute-start(bf16[128,768]{0,1:T(8,128)(2,1)S(1)} %copy.98), channel_id=1, source_target_pairs={{16,0},{32,16},{48,32},{64,48},{80,64},{96,80},{112,96},{128,112},... | collective-permute-start | bytes 589832 | tf_op jit(solution)/shard_map/ppermute | solution.py:19
  35.6 0.9 fusion.81
  36.5 1.9 %collective-permute-start.10 = (bf16[128,768]{1,0:T(8,128)(2,1)}, bf16[128,768]{1,0:T(8,128)(2,1)}, u32[]{:S(2)}, u32[]{:S(2)}) collective-permute-start(bf16[128,768]{1,0:T(8,128)(2,1)} %param.8), channel_id=1, source_target_pairs={{1,0},{2,1},{3,2},{4,3},{5,4},{6,5},{7,6},{8,7},{9,8},{10,9},{11,1... | collective-permute-start | bytes 589832 | tf_op jit(solution)/shard_map/ppermute | solution.py:19
  38.4 0.9 fusion.82
  39.4 1.9 %collective-permute-start.9 = (bf16[128,768]{1,0:T(8,128)(2,1)}, bf16[128,768]{1,0:T(8,128)(2,1)}, u32[]{:S(2)}, u32[]{:S(2)}) collective-permute-start(bf16[128,768]{1,0:T(8,128)(2,1)} %param.8), channel_id=1, source_target_pairs={{0,64},{16,80},{32,96},{48,112},{64,128},{80,144},{96,160},{112,17... | collective-permute-start | bytes 589832 | tf_op jit(solution)/shard_map/ppermute | solution.py:19
  41.3 0.9 fusion.83
  42.3 4.6 %collective-permute-start.8 = (bf16[128,768]{1,0:T(8,128)(2,1)}, bf16[128,768]{1,0:T(8,128)(2,1)}, u32[]{:S(2)}, u32[]{:S(2)}) collective-permute-start(bf16[128,768]{1,0:T(8,128)(2,1)} %param.8), channel_id=1, source_target_pairs={{64,0},{80,16},{96,32},{112,48},{128,64},{144,80},{160,96},{176,11... | collective-permute-start | bytes 589832 | tf_op jit(solution)/shard_map/ppermute | solution.py:19
  46.8 0.9 fusion.84
  47.8 1.9 %collective-permute-start.6 = (bf16[128,768]{1,0:T(8,128)(2,1)}, bf16[128,768]{1,0:T(8,128)(2,1)}, u32[]{:S(2)}, u32[]{:S(2)}) collective-permute-start(bf16[128,768]{1,0:T(8,128)(2,1)} %param.8), channel_id=1, source_target_pairs={{16,0},{32,16},{48,32},{64,48},{80,64},{96,80},{112,96},{128,112},... | collective-permute-start | bytes 589832 | tf_op jit(solution)/shard_map/ppermute | solution.py:19
  49.7 0.9 fusion.86
  51.3 1.0 fusion.72
  52.3 2.9 %collective-permute-done.6 = bf16[128,768]{1,0:T(8,128)(2,1)} collective-permute-done((bf16[128,768]{1,0:T(8,128)(2,1)}, bf16[128,768]{1,0:T(8,128)(2,1)}, u32[]{:S(2)}, u32[]{:S(2)}) %collective-permute-start.6) | collective-permute-done | bytes 196640 | tf_op jit(solution)/shard_map/ppermute | solution.py:19
  55.2 1.9 %collective-permute-start.7 = (bf16[128,768]{1,0:T(8,128)(2,1)}, bf16[128,768]{1,0:T(8,128)(2,1)}, u32[]{:S(2)}, u32[]{:S(2)}) collective-permute-start(bf16[128,768]{1,0:T(8,128)(2,1)} %param.8), channel_id=1, source_target_pairs={{0,16},{16,32},{32,48},{48,64},{64,80},{80,96},{96,112},{112,128},... | collective-permute-start | bytes 589832 | tf_op jit(solution)/shard_map/ppermute | solution.py:19
  57.1 1.7 %copy.124 = bf16[128,768]{0,1:T(8,128)(2,1)} copy(bf16[128,768]{1,0:T(8,128)(2,1)} %collective-permute-done.6) | data formatting | bytes 393216 | tf_op jit(solution)/shard_map/ppermute | solution.py:19
  58.9 2.1 %convolution_add_fusion.3 = f32[6,128,128]{1,2,0:T(8,128)} fusion(f32[6,128,128]{1,2,0:T(8,128)} %fusion.72, bf16[128,6,128]{0,2,1:T(8,128)(2,1)} %bitcast.215, f32[6,128,128]{1,2,0:T(8,128)S(1)} %get-tuple-element.35, f32[6,128]{1,0:T(8,128)S(1)} %log_add_fusion), kind=kOutput, calls=%fused_computation.3 | convolution fusion | flops 25460736 | bytes 1379328 | tf_op jit(solution)/shard_map/hqk,khd->qhd/dot_general | solution.py:33
  60.9 1.7 %copy.134 = bf16[128,768]{0,1:T(8,128)(2,1)} copy(bf16[128,768]{1,0:T(8,128)(2,1)} %collective-permute-done.11) | data formatting | bytes 393216 | tf_op jit(solution)/shard_map/ppermute | solution.py:19
  62.7 1.9 %fusion.56 = f32[6,128,128]{1,2,0:T(8,128)} fusion(bf16[128,6,128]{0,2,1:T(8,128)(2,1)} %bitcast.217, f32[6,128,128]{1,2,0:T(8,128)S(1)} %get-tuple-element.23, f32[6,128]{1,0:T(8,128)S(1)} %log_add_fusion), kind=kOutput, calls=%fused_computation.101 | convolution fusion | flops 25362432 | bytes 986112 | tf_op jit(solution)/shard_map/hqk,khd->qhd/dot_general | solution.py:33
  64.5 1.7 %copy.132 = bf16[128,768]{0,1:T(8,128)(2,1)} copy(bf16[128,768]{1,0:T(8,128)(2,1)} %collective-permute-done.10) | data formatting | bytes 393216 | tf_op jit(solution)/shard_map/ppermute | solution.py:19
  66.3 1.9 %fusion.59 = f32[6,128,128]{1,2,0:T(8,128)} fusion(bf16[128,6,128]{0,2,1:T(8,128)(2,1)} %bitcast.219, f32[6,128,128]{1,2,0:T(8,128)S(1)} %get-tuple-element.25, f32[6,128]{1,0:T(8,128)S(1)} %log_add_fusion), kind=kOutput, calls=%fused_computation.102 | convolution fusion | flops 25362432 | bytes 986112 | tf_op jit(solution)/shard_map/hqk,khd->qhd/dot_general | solution.py:33
  68.2 1.7 %copy.130 = bf16[128,768]{0,1:T(8,128)(2,1)} copy(bf16[128,768]{1,0:T(8,128)(2,1)} %collective-permute-done.9) | data formatting | bytes 393216 | tf_op jit(solution)/shard_map/ppermute | solution.py:19
  69.9 1.9 %fusion.62 = f32[6,128,128]{1,2,0:T(8,128)} fusion(bf16[128,6,128]{0,2,1:T(8,128)(2,1)} %bitcast.221, f32[6,128,128]{1,2,0:T(8,128)S(1)} %get-tuple-element.27, f32[6,128]{1,0:T(8,128)S(1)} %log_add_fusion), kind=kOutput, calls=%fused_computation.103 | convolution fusion | flops 25362432 | bytes 986112 | tf_op jit(solution)/shard_map/hqk,khd->qhd/dot_general | solution.py:33
  71.8 1.7 %copy.128 = bf16[128,768]{0,1:T(8,128)(2,1)} copy(bf16[128,768]{1,0:T(8,128)(2,1)} %collective-permute-done.8) | data formatting | bytes 393216 | tf_op jit(solution)/shard_map/ppermute | solution.py:19
  73.5 1.9 %fusion.65 = f32[6,128,128]{1,2,0:T(8,128)} fusion(bf16[128,6,128]{0,2,1:T(8,128)(2,1)} %bitcast.223, f32[6,128,128]{1,2,0:T(8,128)S(1)} %get-tuple-element.29, f32[6,128]{1,0:T(8,128)S(1)} %log_add_fusion), kind=kOutput, calls=%fused_computation.104 | convolution fusion | flops 25362432 | bytes 986112 | tf_op jit(solution)/shard_map/hqk,khd->qhd/dot_general | solution.py:33
  75.4 1.7 %copy.126 = bf16[128,768]{0,1:T(8,128)(2,1)} copy(bf16[128,768]{1,0:T(8,128)(2,1)} %collective-permute-done.7) | data formatting | bytes 393216 | tf_op jit(solution)/shard_map/ppermute | solution.py:19
  77.2 1.8 %fusion.47 = f32[128,6]{0,1:T(8,128)S(1)} fusion(f32[6,128,128]{1,2,0:T(8,128)} %fusion.56, f32[6,128,128]{1,2,0:T(8,128)} %fusion.59, f32[6,128,128]{1,2,0:T(8,128)} %fusion.62, f32[6,128,128]{1,2,0:T(8,128)} %fusion.65, f32[6,128,128]{1,2,0:T(8,128)} %convolution_add_fusion.3, bf16[128,6,128]{0,2,1:T(8,128)(2,1)} %bitcast.225, ...), kind=kOutput, calls=%fused_computation.79 | convolution fusion | flops 26148096 | bytes 2758656 | tf_op jit(solution)/shard_map/hqk,khd->qhd/dot_general | solution.py:33
  85.1 0.7 copy-done.13
  86.2 0.7 copy-done.15
  87.3 0.7 copy-done.17
  88.7 1.0 convolution_bitcast_fusion.1
  89.7 1.0 convolution_bitcast_fusion.2
  90.7 1.0 convolution_bitcast_fusion.3
  91.8 1.0 convolution_bitcast_fusion.4
  92.8 1.0 convolution_bitcast_fusion.5
  93.8 1.9 %collective-permute-start.17 = (f32[128,6,128]{0,2,1:T(8,128)S(1)}, f32[128,6,128]{0,2,1:T(8,128)S(1)}, u32[]{:S(2)}, u32[]{:S(2)}) collective-permute-start(f32[128,6,128]{0,2,1:T(8,128)S(1)} %convolution_bitcast_fusion.7), channel_id=1, source_target_pairs={{1,0},{2,1},{3,2},{4,3},{5,4},{6,5},{7,6},{8,7},{9,8},{10,9},{11,1... | collective-permute-start | bytes 1179656 | tf_op jit(solution)/shard_map/ppermute | solution.py:19
  95.7 5.9 %collective-permute-start.16 = (f32[128,6,128]{0,2,1:T(8,128)S(1)}, f32[128,6,128]{0,2,1:T(8,128)S(1)}, u32[]{:S(2)}, u32[]{:S(2)}) collective-permute-start(f32[128,6,128]{0,2,1:T(8,128)S(1)} %convolution_bitcast_fusion.8), channel_id=1, source_target_pairs={{0,1},{1,2},{2,3},{3,4},{4,5},{5,6},{6,7},{7,8},{8,9},{9,10},{10,1... | collective-permute-start | bytes 1179656 | tf_op jit(solution)/shard_map/ppermute | solution.py:19
  101.6 1.9 %collective-permute-start.15 = (f32[128,6,128]{0,2,1:T(8,128)S(1)}, f32[128,6,128]{0,2,1:T(8,128)S(1)}, u32[]{:S(2)}, u32[]{:S(2)}) collective-permute-start(f32[128,6,128]{0,2,1:T(8,128)S(1)} %convolution_bitcast_fusion.9), channel_id=1, source_target_pairs={{64,0},{80,16},{96,32},{112,48},{128,64},{144,80},{160,96},{176,11... | collective-permute-start | bytes 1179656 | tf_op jit(solution)/shard_map/ppermute | solution.py:19
  103.5 3.4 %collective-permute-start.14 = (f32[128,6,128]{0,2,1:T(8,128)S(1)}, f32[128,6,128]{0,2,1:T(8,128)S(1)}, u32[]{:S(2)}, u32[]{:S(2)}) collective-permute-start(f32[128,6,128]{0,2,1:T(8,128)S(1)} %convolution_bitcast_fusion.10), channel_id=1, source_target_pairs={{0,64},{16,80},{32,96},{48,112},{64,128},{80,144},{96,160},{112,17... | collective-permute-start | bytes 1179656 | tf_op jit(solution)/shard_map/ppermute | solution.py:19
  107.2 8.2 %collective-permute-start.13 = (f32[128,6,128]{0,2,1:T(8,128)S(1)}, f32[128,6,128]{0,2,1:T(8,128)S(1)}, u32[]{:S(2)}, u32[]{:S(2)}) collective-permute-start(f32[128,6,128]{0,2,1:T(8,128)S(1)} %convolution_bitcast_fusion.11), channel_id=1, source_target_pairs={{16,0},{32,16},{48,32},{64,48},{80,64},{96,80},{112,96},{128,112},... | collective-permute-start | bytes 1179656 | tf_op jit(solution)/shard_map/ppermute | solution.py:19
  115.9 2.1 %collective-permute-start.12 = (f32[128,6,128]{0,2,1:T(8,128)S(1)}, f32[128,6,128]{0,2,1:T(8,128)S(1)}, u32[]{:S(2)}, u32[]{:S(2)}) collective-permute-start(f32[128,6,128]{0,2,1:T(8,128)S(1)} %convolution_bitcast_fusion.12), channel_id=1, source_target_pairs={{0,16},{16,32},{32,48},{48,64},{64,80},{80,96},{96,112},{112,128},... | collective-permute-start | bytes 1179656 | tf_op jit(solution)/shard_map/ppermute | solution.py:19
  118.0 0.7 copy-done.20
  118.7 1.9 %collective-permute-start.23 = (f32[128,6,128]{0,2,1:T(8,128)S(1)}, f32[128,6,128]{0,2,1:T(8,128)S(1)}, u32[]{:S(2)}, u32[]{:S(2)}) collective-permute-start(f32[128,6,128]{0,2,1:T(8,128)S(1)} %convolution_bitcast_fusion), channel_id=1, source_target_pairs={{1,0},{2,1},{3,2},{4,3},{5,4},{6,5},{7,6},{8,7},{9,8},{10,9},{11,1... | collective-permute-start | bytes 1179656 | tf_op jit(solution)/shard_map/ppermute | solution.py:19
  121.1 4.9 %collective-permute-start.22 = (f32[128,6,128]{0,2,1:T(8,128)}, f32[128,6,128]{0,2,1:T(8,128)S(1)}, u32[]{:S(2)}, u32[]{:S(2)}) collective-permute-start(f32[128,6,128]{0,2,1:T(8,128)} %convolution_bitcast_fusion.1), channel_id=1, source_target_pairs={{0,1},{1,2},{2,3},{3,4},{4,5},{5,6},{6,7},{7,8},{8,9},{9,10},{10,1... | collective-permute-start | bytes 1179656 | tf_op jit(solution)/shard_map/ppermute | solution.py:19
  126.0 1.9 %collective-permute-start.21 = (f32[128,6,128]{0,2,1:T(8,128)}, f32[128,6,128]{0,2,1:T(8,128)S(1)}, u32[]{:S(2)}, u32[]{:S(2)}) collective-permute-start(f32[128,6,128]{0,2,1:T(8,128)} %convolution_bitcast_fusion.2), channel_id=1, source_target_pairs={{64,0},{80,16},{96,32},{112,48},{128,64},{144,80},{160,96},{176,11... | collective-permute-start | bytes 1179656 | tf_op jit(solution)/shard_map/ppermute | solution.py:19
  127.9 3.4 %collective-permute-start.20 = (f32[128,6,128]{0,2,1:T(8,128)}, f32[128,6,128]{0,2,1:T(8,128)S(1)}, u32[]{:S(2)}, u32[]{:S(2)}) collective-permute-start(f32[128,6,128]{0,2,1:T(8,128)} %convolution_bitcast_fusion.3), channel_id=1, source_target_pairs={{0,64},{16,80},{32,96},{48,112},{64,128},{80,144},{96,160},{112,17... | collective-permute-start | bytes 1179656 | tf_op jit(solution)/shard_map/ppermute | solution.py:19
  131.3 7.9 %collective-permute-start.19 = (f32[128,6,128]{0,2,1:T(8,128)}, f32[128,6,128]{0,2,1:T(8,128)}, u32[]{:S(2)}, u32[]{:S(2)}) collective-permute-start(f32[128,6,128]{0,2,1:T(8,128)} %convolution_bitcast_fusion.4), channel_id=1, source_target_pairs={{16,0},{32,16},{48,32},{64,48},{80,64},{96,80},{112,96},{128,112},... | collective-permute-start | bytes 1179656 | tf_op jit(solution)/shard_map/ppermute | solution.py:19
  139.2 1.9 %collective-permute-start.18 = (f32[128,6,128]{0,2,1:T(8,128)}, f32[128,6,128]{0,2,1:T(8,128)}, u32[]{:S(2)}, u32[]{:S(2)}) collective-permute-start(f32[128,6,128]{0,2,1:T(8,128)} %convolution_bitcast_fusion.5), channel_id=1, source_target_pairs={{0,16},{16,32},{32,48},{48,64},{64,80},{80,96},{96,112},{112,128},... | collective-permute-start | bytes 1179656 | tf_op jit(solution)/shard_map/ppermute | solution.py:19
  141.5 0.8 copy.188
  142.5 1.8 %fusion.46 = bf16[128,6,128]{0,2,1:T(8,128)(2,1)S(1)} fusion(f32[128,6,128]{0,2,1:T(8,128)S(1)} %copy-done.19, f32[128,6,128]{0,2,1:T(8,128)} %copy-done.20, f32[128,6,128]{0,2,1:T(8,128)} %copy-done.21, f32[128,6,128]{0,2,1:T(8,128)} %copy-done.22, f32[128,6,128]{0,2,1:T(8,128)} %copy-done.23, f32[128,6,128]{0,2,1:T(8,128)} %copy-done.24, ...), kind=kOutput, calls=%fused_computation.78 | convolution fusion | flops 25952256 | bytes 2949120 | tf_op jit(solution)/shard_map/hqk,qhd->khd/dot_general | solution.py:37
  144.3 0.8 copy.189
  145.1 2.0 %collective-permute-done.19 = f32[128,6,128]{0,2,1:T(8,128)} collective-permute-done((f32[128,6,128]{0,2,1:T(8,128)}, f32[128,6,128]{0,2,1:T(8,128)}, u32[]{:S(2)}, u32[]{:S(2)}) %collective-permute-start.19) | collective-permute-done | bytes 393248 | tf_op jit(solution)/shard_map/ppermute | solution.py:19
  147.1 7.4 %collective-permute-done.18 = f32[128,6,128]{0,2,1:T(8,128)} collective-permute-done((f32[128,6,128]{0,2,1:T(8,128)}, f32[128,6,128]{0,2,1:T(8,128)}, u32[]{:S(2)}, u32[]{:S(2)}) %collective-permute-start.18) | collective-permute-done | bytes 393248 | tf_op jit(solution)/shard_map/ppermute | solution.py:19
  154.5 1.4 fusion.38
  155.9 0.8 copy.190
  (99 shorter events, 11.2 us)
Async XLA Ops:
  1.7 24.3 %collective-permute-start.5 = (bf16[128,768]{0,1:T(8,128)(2,1)S(1)}, bf16[128,768]{0,1:T(8,128)(2,1)S(1)}, u32[]{:S(2)}, u32[]{:S(2)}) collective-permute-start(bf16[128,768]{0,1:T(8,128)(2,1)S(1)} %copy.98), channel_id=1, source_target_pairs={{0,1},{1,2},{2,3},{3,4},{4,5},{5,6},{6,7},{7,8},{8,9},{9,10},{10,1... | collective-permute-start | bytes 589832 | tf_op jit(solution)/shard_map/ppermute | solution.py:19
  7.5 22.6 %collective-permute-start.4 = (bf16[128,768]{0,1:T(8,128)(2,1)S(1)}, bf16[128,768]{0,1:T(8,128)(2,1)S(1)}, u32[]{:S(2)}, u32[]{:S(2)}) collective-permute-start(bf16[128,768]{0,1:T(8,128)(2,1)S(1)} %copy.98), channel_id=1, source_target_pairs={{1,0},{2,1},{3,2},{4,3},{5,4},{6,5},{7,6},{8,7},{9,8},{10,9},{11,1... | collective-permute-start | bytes 589832 | tf_op jit(solution)/shard_map/ppermute | solution.py:19
  9.4 27.1 %collective-permute-start.3 = (bf16[128,768]{0,1:T(8,128)(2,1)S(1)}, bf16[128,768]{0,1:T(8,128)(2,1)S(1)}, u32[]{:S(2)}, u32[]{:S(2)}) collective-permute-start(bf16[128,768]{0,1:T(8,128)(2,1)S(1)} %copy.98), channel_id=1, source_target_pairs={{0,64},{16,80},{32,96},{48,112},{64,128},{80,144},{96,160},{112,17... | collective-permute-start | bytes 589832 | tf_op jit(solution)/shard_map/ppermute | solution.py:19
  11.7 27.6 %collective-permute-start.2 = (bf16[128,768]{0,1:T(8,128)(2,1)S(1)}, bf16[128,768]{0,1:T(8,128)(2,1)S(1)}, u32[]{:S(2)}, u32[]{:S(2)}) collective-permute-start(bf16[128,768]{0,1:T(8,128)(2,1)S(1)} %copy.98), channel_id=1, source_target_pairs={{64,0},{80,16},{96,32},{112,48},{128,64},{144,80},{160,96},{176,11... | collective-permute-start | bytes 589832 | tf_op jit(solution)/shard_map/ppermute | solution.py:19
  15.9 45.0 %collective-permute-start.11 = (bf16[128,768]{1,0:T(8,128)(2,1)}, bf16[128,768]{1,0:T(8,128)(2,1)}, u32[]{:S(2)}, u32[]{:S(2)}) collective-permute-start(bf16[128,768]{1,0:T(8,128)(2,1)} %param.8), channel_id=1, source_target_pairs={{0,1},{1,2},{2,3},{3,4},{4,5},{5,6},{6,7},{7,8},{8,9},{9,10},{10,1... | collective-permute-start | bytes 589832 | tf_op jit(solution)/shard_map/ppermute | solution.py:19
  21.4 1.1 copy-start.25
  22.5 0.9 copy-start.26
  24.3 0.7 copy-start.27
  26.0 4.1 %copy-start.10 = (bf16[128,768]{0,1:T(8,128)(2,1)}, bf16[128,768]{0,1:T(8,128)(2,1)S(1)}, u32[]{:S(2)}) copy-start(bf16[128,768]{0,1:T(8,128)(2,1)S(1)} %collective-permute-done.5) | copy-start | bytes 589828
  26.0 16.2 %collective-permute-start.1 = (bf16[128,768]{0,1:T(8,128)(2,1)S(1)}, bf16[128,768]{0,1:T(8,128)(2,1)S(1)}, u32[]{:S(2)}, u32[]{:S(2)}) collective-permute-start(bf16[128,768]{0,1:T(8,128)(2,1)S(1)} %copy.98), channel_id=1, source_target_pairs={{0,16},{16,32},{32,48},{48,64},{64,80},{80,96},{96,112},{112,128},... | collective-permute-start | bytes 589832 | tf_op jit(solution)/shard_map/ppermute | solution.py:19
  30.1 6.4 %copy-start.12 = (bf16[128,768]{0,1:T(8,128)(2,1)}, bf16[128,768]{0,1:T(8,128)(2,1)S(1)}, u32[]{:S(2)}) copy-start(bf16[128,768]{0,1:T(8,128)(2,1)S(1)} %collective-permute-done.4) | copy-start | bytes 589828
  30.1 17.7 %collective-permute-start = (bf16[128,768]{0,1:T(8,128)(2,1)S(1)}, bf16[128,768]{0,1:T(8,128)(2,1)S(1)}, u32[]{:S(2)}, u32[]{:S(2)}) collective-permute-start(bf16[128,768]{0,1:T(8,128)(2,1)S(1)} %copy.98), channel_id=1, source_target_pairs={{16,0},{32,16},{48,32},{64,48},{80,64},{96,80},{112,96},{128,112},... | collective-permute-start | bytes 589832 | tf_op jit(solution)/shard_map/ppermute | solution.py:19
  36.5 2.9 %copy-start.14 = (bf16[128,768]{0,1:T(8,128)(2,1)}, bf16[128,768]{0,1:T(8,128)(2,1)S(1)}, u32[]{:S(2)}) copy-start(bf16[128,768]{0,1:T(8,128)(2,1)S(1)} %collective-permute-done.3) | copy-start | bytes 589828
  36.5 28.0 %collective-permute-start.10 = (bf16[128,768]{1,0:T(8,128)(2,1)}, bf16[128,768]{1,0:T(8,128)(2,1)}, u32[]{:S(2)}, u32[]{:S(2)}) collective-permute-start(bf16[128,768]{1,0:T(8,128)(2,1)} %param.8), channel_id=1, source_target_pairs={{1,0},{2,1},{3,2},{4,3},{5,4},{6,5},{7,6},{8,7},{9,8},{10,9},{11,1... | collective-permute-start | bytes 589832 | tf_op jit(solution)/shard_map/ppermute | solution.py:19
  39.4 2.9 %copy-start.16 = (bf16[128,768]{0,1:T(8,128)(2,1)}, bf16[128,768]{0,1:T(8,128)(2,1)S(1)}, u32[]{:S(2)}) copy-start(bf16[128,768]{0,1:T(8,128)(2,1)S(1)} %collective-permute-done.2) | copy-start | bytes 589828
  39.4 28.8 %collective-permute-start.9 = (bf16[128,768]{1,0:T(8,128)(2,1)}, bf16[128,768]{1,0:T(8,128)(2,1)}, u32[]{:S(2)}, u32[]{:S(2)}) collective-permute-start(bf16[128,768]{1,0:T(8,128)(2,1)} %param.8), channel_id=1, source_target_pairs={{0,64},{16,80},{32,96},{48,112},{64,128},{80,144},{96,160},{112,17... | collective-permute-start | bytes 589832 | tf_op jit(solution)/shard_map/ppermute | solution.py:19
  42.2 5.5 %copy-start.6 = (bf16[128,768]{0,1:T(8,128)(2,1)}, bf16[128,768]{0,1:T(8,128)(2,1)S(1)}, u32[]{:S(2)}) copy-start(bf16[128,768]{0,1:T(8,128)(2,1)S(1)} %collective-permute-done.1) | copy-start | bytes 589828
  42.3 29.5 %collective-permute-start.8 = (bf16[128,768]{1,0:T(8,128)(2,1)}, bf16[128,768]{1,0:T(8,128)(2,1)}, u32[]{:S(2)}, u32[]{:S(2)}) collective-permute-start(bf16[128,768]{1,0:T(8,128)(2,1)} %param.8), channel_id=1, source_target_pairs={{64,0},{80,16},{96,32},{112,48},{128,64},{144,80},{160,96},{176,11... | collective-permute-start | bytes 589832 | tf_op jit(solution)/shard_map/ppermute | solution.py:19
  47.8 2.9 %copy-start.8 = (bf16[128,768]{0,1:T(8,128)(2,1)}, bf16[128,768]{0,1:T(8,128)(2,1)S(1)}, u32[]{:S(2)}) copy-start(bf16[128,768]{0,1:T(8,128)(2,1)S(1)} %collective-permute-done) | copy-start | bytes 589828
  47.8 7.4 %collective-permute-start.6 = (bf16[128,768]{1,0:T(8,128)(2,1)}, bf16[128,768]{1,0:T(8,128)(2,1)}, u32[]{:S(2)}, u32[]{:S(2)}) collective-permute-start(bf16[128,768]{1,0:T(8,128)(2,1)} %param.8), channel_id=1, source_target_pairs={{16,0},{32,16},{48,32},{64,48},{80,64},{96,80},{112,96},{128,112},... | collective-permute-start | bytes 589832 | tf_op jit(solution)/shard_map/ppermute | solution.py:19
  55.2 20.2 %collective-permute-start.7 = (bf16[128,768]{1,0:T(8,128)(2,1)}, bf16[128,768]{1,0:T(8,128)(2,1)}, u32[]{:S(2)}, u32[]{:S(2)}) collective-permute-start(bf16[128,768]{1,0:T(8,128)(2,1)} %param.8), channel_id=1, source_target_pairs={{0,16},{16,32},{32,48},{48,64},{64,80},{80,96},{96,112},{112,128},... | collective-permute-start | bytes 589832 | tf_op jit(solution)/shard_map/ppermute | solution.py:19
  77.2 1.9 %copy-start.1 = (bf16[128,768]{0,1:T(8,128)(2,1)S(1)}, bf16[128,768]{0,1:T(8,128)(2,1)}, u32[]{:S(2)}) copy-start(bf16[128,768]{0,1:T(8,128)(2,1)} %copy.134) | copy-start | bytes 589828
  79.0 0.9 copy-start.2
  80.0 0.9 copy-start.3
  80.9 0.9 copy-start.4
  81.8 0.9 copy-start
  82.7 0.9 copy-start.5
  83.7 0.9 copy-start.11
  84.8 0.9 copy-start.13
  85.9 0.9 copy-start.15
  87.1 0.9 copy-start.17
  93.8 22.1 %collective-permute-start.17 = (f32[128,6,128]{0,2,1:T(8,128)S(1)}, f32[128,6,128]{0,2,1:T(8,128)S(1)}, u32[]{:S(2)}, u32[]{:S(2)}) collective-permute-start(f32[128,6,128]{0,2,1:T(8,128)S(1)} %convolution_bitcast_fusion.7), channel_id=1, source_target_pairs={{1,0},{2,1},{3,2},{4,3},{5,4},{6,5},{7,6},{8,7},{9,8},{10,9},{11,1... | collective-permute-start | bytes 1179656 | tf_op jit(solution)/shard_map/ppermute | solution.py:19
  95.7 22.3 %collective-permute-start.16 = (f32[128,6,128]{0,2,1:T(8,128)S(1)}, f32[128,6,128]{0,2,1:T(8,128)S(1)}, u32[]{:S(2)}, u32[]{:S(2)}) collective-permute-start(f32[128,6,128]{0,2,1:T(8,128)S(1)} %convolution_bitcast_fusion.8), channel_id=1, source_target_pairs={{0,1},{1,2},{2,3},{3,4},{4,5},{5,6},{6,7},{7,8},{8,9},{9,10},{10,1... | collective-permute-start | bytes 1179656 | tf_op jit(solution)/shard_map/ppermute | solution.py:19
  101.6 19.5 %collective-permute-start.15 = (f32[128,6,128]{0,2,1:T(8,128)S(1)}, f32[128,6,128]{0,2,1:T(8,128)S(1)}, u32[]{:S(2)}, u32[]{:S(2)}) collective-permute-start(f32[128,6,128]{0,2,1:T(8,128)S(1)} %convolution_bitcast_fusion.9), channel_id=1, source_target_pairs={{64,0},{80,16},{96,32},{112,48},{128,64},{144,80},{160,96},{176,11... | collective-permute-start | bytes 1179656 | tf_op jit(solution)/shard_map/ppermute | solution.py:19
  103.5 22.4 %collective-permute-start.14 = (f32[128,6,128]{0,2,1:T(8,128)S(1)}, f32[128,6,128]{0,2,1:T(8,128)S(1)}, u32[]{:S(2)}, u32[]{:S(2)}) collective-permute-start(f32[128,6,128]{0,2,1:T(8,128)S(1)} %convolution_bitcast_fusion.10), channel_id=1, source_target_pairs={{0,64},{16,80},{32,96},{48,112},{64,128},{80,144},{96,160},{112,17... | collective-permute-start | bytes 1179656 | tf_op jit(solution)/shard_map/ppermute | solution.py:19
  107.2 20.8 %collective-permute-start.13 = (f32[128,6,128]{0,2,1:T(8,128)S(1)}, f32[128,6,128]{0,2,1:T(8,128)S(1)}, u32[]{:S(2)}, u32[]{:S(2)}) collective-permute-start(f32[128,6,128]{0,2,1:T(8,128)S(1)} %convolution_bitcast_fusion.11), channel_id=1, source_target_pairs={{16,0},{32,16},{48,32},{64,48},{80,64},{96,80},{112,96},{128,112},... | collective-permute-start | bytes 1179656 | tf_op jit(solution)/shard_map/ppermute | solution.py:19
  115.9 5.0 %copy-start.9 = (bf16[128,768]{0,1:T(8,128)(2,1)S(1)}, bf16[128,768]{0,1:T(8,128)(2,1)}, u32[]{:S(2)}) copy-start(bf16[128,768]{0,1:T(8,128)(2,1)} %copy-done.8) | copy-start | bytes 589828
  115.9 4.7 %copy-start.18 = (f32[128,6,128]{0,2,1:T(8,128)}, f32[128,6,128]{0,2,1:T(8,128)S(1)}, u32[]{:S(2)}) copy-start(f32[128,6,128]{0,2,1:T(8,128)S(1)} %collective-permute-done.17) | copy-start | bytes 1179652
  115.9 15.4 %collective-permute-start.12 = (f32[128,6,128]{0,2,1:T(8,128)S(1)}, f32[128,6,128]{0,2,1:T(8,128)S(1)}, u32[]{:S(2)}, u32[]{:S(2)}) collective-permute-start(f32[128,6,128]{0,2,1:T(8,128)S(1)} %convolution_bitcast_fusion.12), channel_id=1, source_target_pairs={{0,16},{16,32},{32,48},{48,64},{64,80},{80,96},{96,112},{112,128},... | collective-permute-start | bytes 1179656 | tf_op jit(solution)/shard_map/ppermute | solution.py:19
  118.0 0.7 copy-start.20
  118.7 20.5 %collective-permute-start.23 = (f32[128,6,128]{0,2,1:T(8,128)S(1)}, f32[128,6,128]{0,2,1:T(8,128)S(1)}, u32[]{:S(2)}, u32[]{:S(2)}) collective-permute-start(f32[128,6,128]{0,2,1:T(8,128)S(1)} %convolution_bitcast_fusion), channel_id=1, source_target_pairs={{1,0},{2,1},{3,2},{4,3},{5,4},{6,5},{7,6},{8,7},{9,8},{10,9},{11,1... | collective-permute-start | bytes 1179656 | tf_op jit(solution)/shard_map/ppermute | solution.py:19
  120.9 20.3 %copy-start.7 = (bf16[128,768]{0,1:T(8,128)(2,1)S(1)}, bf16[128,768]{0,1:T(8,128)(2,1)}, u32[]{:S(2)}) copy-start(bf16[128,768]{0,1:T(8,128)(2,1)} %copy-done.6) | copy-start | bytes 589828
  121.1 4.9 %copy-start.21 = (f32[128,6,128]{0,2,1:T(8,128)}, f32[128,6,128]{0,2,1:T(8,128)S(1)}, u32[]{:S(2)}) copy-start(f32[128,6,128]{0,2,1:T(8,128)S(1)} %collective-permute-done.15) | copy-start | bytes 1179652
  121.1 24.0 %collective-permute-start.22 = (f32[128,6,128]{0,2,1:T(8,128)}, f32[128,6,128]{0,2,1:T(8,128)S(1)}, u32[]{:S(2)}, u32[]{:S(2)}) collective-permute-start(f32[128,6,128]{0,2,1:T(8,128)} %convolution_bitcast_fusion.1), channel_id=1, source_target_pairs={{0,1},{1,2},{2,3},{3,4},{4,5},{5,6},{6,7},{7,8},{8,9},{9,10},{10,1... | collective-permute-start | bytes 1179656 | tf_op jit(solution)/shard_map/ppermute | solution.py:19
  126.0 15.5 %copy-start.22 = (f32[128,6,128]{0,2,1:T(8,128)}, f32[128,6,128]{0,2,1:T(8,128)S(1)}, u32[]{:S(2)}) copy-start(f32[128,6,128]{0,2,1:T(8,128)S(1)} %collective-permute-done.14) | copy-start | bytes 1179652
  126.0 19.1 %collective-permute-start.21 = (f32[128,6,128]{0,2,1:T(8,128)}, f32[128,6,128]{0,2,1:T(8,128)S(1)}, u32[]{:S(2)}, u32[]{:S(2)}) collective-permute-start(f32[128,6,128]{0,2,1:T(8,128)} %convolution_bitcast_fusion.2), channel_id=1, source_target_pairs={{64,0},{80,16},{96,32},{112,48},{128,64},{144,80},{160,96},{176,11... | collective-permute-start | bytes 1179656 | tf_op jit(solution)/shard_map/ppermute | solution.py:19
  127.9 13.5 %copy-start.23 = (f32[128,6,128]{0,2,1:T(8,128)}, f32[128,6,128]{0,2,1:T(8,128)S(1)}, u32[]{:S(2)}) copy-start(f32[128,6,128]{0,2,1:T(8,128)S(1)} %collective-permute-done.13) | copy-start | bytes 1179652
  127.9 17.1 %collective-permute-start.20 = (f32[128,6,128]{0,2,1:T(8,128)}, f32[128,6,128]{0,2,1:T(8,128)S(1)}, u32[]{:S(2)}, u32[]{:S(2)}) collective-permute-start(f32[128,6,128]{0,2,1:T(8,128)} %convolution_bitcast_fusion.3), channel_id=1, source_target_pairs={{0,64},{16,80},{32,96},{48,112},{64,128},{80,144},{96,160},{112,17... | collective-permute-start | bytes 1179656 | tf_op jit(solution)/shard_map/ppermute | solution.py:19
  131.3 10.2 %copy-start.24 = (f32[128,6,128]{0,2,1:T(8,128)}, f32[128,6,128]{0,2,1:T(8,128)S(1)}, u32[]{:S(2)}) copy-start(f32[128,6,128]{0,2,1:T(8,128)S(1)} %collective-permute-done.12) | copy-start | bytes 1179652
  131.3 15.7 %collective-permute-start.19 = (f32[128,6,128]{0,2,1:T(8,128)}, f32[128,6,128]{0,2,1:T(8,128)}, u32[]{:S(2)}, u32[]{:S(2)}) collective-permute-start(f32[128,6,128]{0,2,1:T(8,128)} %convolution_bitcast_fusion.4), channel_id=1, source_target_pairs={{16,0},{32,16},{48,32},{64,48},{80,64},{96,80},{112,96},{128,112},... | collective-permute-start | bytes 1179656 | tf_op jit(solution)/shard_map/ppermute | solution.py:19
  139.2 15.2 %collective-permute-start.18 = (f32[128,6,128]{0,2,1:T(8,128)}, f32[128,6,128]{0,2,1:T(8,128)}, u32[]{:S(2)}, u32[]{:S(2)}) collective-permute-start(f32[128,6,128]{0,2,1:T(8,128)} %convolution_bitcast_fusion.5), channel_id=1, source_target_pairs={{0,16},{16,32},{32,48},{48,64},{64,80},{80,96},{96,112},{112,128},... | collective-permute-start | bytes 1179656 | tf_op jit(solution)/shard_map/ppermute | solution.py:19
  141.5 1.0 copy-start.19
where the time goes:
time: 158 us; the launch traced here: 157 us
  starting transfers between devices  85.6 us (54%)
  matrix products  31.5 us (20%)
  local copies, waits for them, and re-layouts  23.7 us (15%)
  waiting for transfers between devices  12.4 us (8%)
  between operations  2.15 us (1%)
    ppermute x24, starting transfers between devices, passed_along(): return lax.ppermute(block, axis, route)  85.6 us
    dot_general x14, matrix products, mix_rows(): jnp.einsum('hqk,khd->qhd', weights, row_heads, preferred_element_type=jnp...  13.8 us
    unnamed x63, local copies, waits for them, and re-layouts  13.3 us
    ppermute x24, waiting for transfers between devices, passed_along(): return lax.ppermute(block, axis, route)  12.4 us
    ppermute x6, local copies, waits for them, and re-layouts, passed_along(): return lax.ppermute(block, axis, route)  10.4 us
    dot_general x14, matrix products, back_rows(): jnp.einsum('hqk,qhd->khd', weights, row_heads, preferred_element_type=jnp...  10.1 us
    dot_general x7, matrix products, block_scores(): jnp.einsum('qhd,khd->hqk', query_heads, key_heads, preferred_element_type...  5.7 us
  transfers between devices with their start and end apart: 24, of which 3 were waited for; matrix products, arithmetic and copies ran while one was open for 21% of the time, Pallas kernels for 0%

commit v1 on v0

v1 whole, which is shorter than its diff:
```python
import functools

import jax
import jax.numpy as jnp
from jax import lax
from jax.experimental import pallas as pl
from jax.experimental.pallas import tpu as pltpu
from jax.sharding import PartitionSpec as P

HEADS = 6
HD = 128
BLOCK = 128
NX, NY, NZ = 4, 8, 16
AXES = ("inner", "outer")
SCALE = HD ** -0.5
LOG2E = 1.4426950408889634
NEG = -1e30
X_STEP, Y_STEP, Z_STEP = NZ, NZ * NX, 1
ROUTES = (("y", 1), ("y", -1), ("x", 1), ("x", -1), ("z", 1), ("z", -1))
STEP = {"x": X_STEP, "y": Y_STEP, "z": Z_STEP}
SIZE = {"x": NX, "y": NY, "z": NZ}


def coordinate(block, name):
    return (block // STEP[name]) % SIZE[name]


def pairs(name, direction):
    return [
        (b, b + direction * STEP[name])
        for b in range(NX * NY * NZ)
        if 0 <= coordinate(b, name) + direction < SIZE[name]
    ]


def moved(message, name, direction):
    return lax.ppermute(message, AXES, pairs(name, direction))


def rows_of(ref, half, head):
    return ref[pl.ds(half * BLOCK, BLOCK), pl.ds(head * HD, HD)]


def nt(a, b):
    return lax.dot_general(a, b, (((1,), (1,)), ((), ())), preferred_element_type=jnp.float32)


def nn(a, b):
    return lax.dot_general(a, b, (((1,), (0,)), ((), ())), preferred_element_type=jnp.float32)


def tn(a, b):
    return lax.dot_general(a, b, (((0,), (0,)), ((), ())), preferred_element_type=jnp.float32)


def pair_kernel(partners, counts, query, dout, own, *refs):
    others, outs = refs[:6], refs[6:]
    terms, query_out, own_out = outs[:6], outs[6], outs[7]
    blocks = (own,) + tuple(others)
    me = partners[0, 0]
    biases = [0.0]
    for name, direction in ROUTES:
        target = me - direction * STEP[name]
        listed = jnp.int32(0)
        for slot in range(1, 7):
            hit = (partners[0, slot] == target) & (slot < counts[0])
            listed = listed | hit.astype(jnp.int32)
        biases.append(jnp.where(listed > 0, jnp.float32(0.0), jnp.float32(NEG)))
    for head in range(HEADS):
        lanes = pl.ds(head * HD, HD)
        q = query[:, lanes]
        do = dout[:, lanes]
        scores = [nt(rows_of(block, 0, head), q) for block in blocks]
        tops = [
            jnp.max(s, axis=0, keepdims=True) * (SCALE * LOG2E) + bias
            for s, bias in zip(scores, biases)
        ]
        top = functools.reduce(jnp.maximum, tops)
        weights = [
            jnp.exp2(s * (SCALE * LOG2E) + (bias - top)) for s, bias in zip(scores, biases)
        ]
        grads = [nt(rows_of(block, 1, head), do) for block in blocks]
        total = functools.reduce(
            jnp.add, [jnp.sum(w, axis=0, keepdims=True) for w in weights]
        )
        delta = functools.reduce(
            jnp.add, [jnp.sum(w * g, axis=0, keepdims=True) for w, g in zip(weights, grads)]
        )
        inverse = 1.0 / total
        delta = delta * inverse
        query_grad = jnp.zeros((BLOCK, HD), jnp.float32)
        for index in range(7):
            probs = weights[index] * inverse
            dscores = (probs * (grads[index] - delta)).astype(jnp.bfloat16)
            query_grad = query_grad + tn(dscores, rows_of(blocks[index], 0, head))
            key_grad = nn(dscores, q) * SCALE
            value_grad = nn(probs.astype(jnp.bfloat16), do)
            out = own_out if index == 0 else terms[index - 1]
            out[pl.ds(0, BLOCK), lanes] = key_grad.astype(out.dtype)
            out[pl.ds(BLOCK, BLOCK), lanes] = value_grad.astype(out.dtype)
        query_out[:, lanes] = (query_grad * SCALE).astype(query_out.dtype)


def sum_kernel(own, *refs):
    parts, (key_out, value_out) = refs[:6], refs[6:]
    for half, out in ((0, key_out), (1, value_out)):
        rows = pl.ds(half * BLOCK, BLOCK)
        total = own[rows, :]
        for part in parts:
            total = total + part[rows, :].astype(jnp.float32)
        out[...] = total.astype(out.dtype)


VM = pl.BlockSpec(memory_space=pltpu.VMEM)
SM = pl.BlockSpec(memory_space=pltpu.SMEM)
WIDE = (2 * BLOCK, HEADS * HD)
NARROW = (BLOCK, HEADS * HD)


def on_device(query, keys, values, dout, partners, counts):
    own = jnp.concatenate([keys, values], axis=0)
    others = [moved(own, name, direction) for name, direction in ROUTES]
    outs = pl.pallas_call(
        pair_kernel,
        out_shape=[jax.ShapeDtypeStruct(WIDE, jnp.bfloat16)] * 6
        + [jax.ShapeDtypeStruct(NARROW, jnp.bfloat16), jax.ShapeDtypeStruct(WIDE, jnp.float32)],
        in_specs=[SM, SM] + [VM] * 9,
        out_specs=[VM] * 8,
        compiler_params=pltpu.CompilerParams(vmem_limit_bytes=40 * 1024 * 1024),
        name="pairs",
    )(partners, counts, query, dout, own, *others)
    terms, query_out, own_out = outs[:6], outs[6], outs[7]
    arrived = [
        moved(term, name, -direction) for term, (name, direction) in zip(terms, ROUTES)
    ]
    key_out, value_out = pl.pallas_call(
        sum_kernel,
        out_shape=[jax.ShapeDtypeStruct(NARROW, jnp.bfloat16)] * 2,
        in_specs=[VM] * 7,
        out_specs=[VM] * 2,
        compiler_params=pltpu.CompilerParams(vmem_limit_bytes=40 * 1024 * 1024),
        name="sums",
    )(own_out, *arrived)
    return query_out, key_out, value_out


def solution(mesh):
    tokens = P(AXES, None)
    return jax.shard_map(
        on_device,
        mesh=mesh,
        in_specs=(tokens, tokens, tokens, tokens, tokens, P(AXES)),
        out_specs=(tokens, tokens, tokens),
        check_vma=False,
    )
```

time: 158 us -> 61 us (0.39)
  the two profiles are of different devices: /device:TPU:225 before, /device:TPU:217 now
where the time goes in v1:
time: 61 us; the launch traced here: 60.6 us
  starting transfers between devices  39.7 us (65%)
  waiting for transfers between devices  11.5 us (19%)
  Pallas kernels  6.83 us (11%)
  between operations  1.46 us (2%)
  local copies, waits for them, and re-layouts  1.04 us (2%)
    ppermute x12, starting transfers between devices, moved(): return lax.ppermute(message, AXES, pairs(name, direction))  39.7 us
    ppermute x12, waiting for transfers between devices, moved(): return lax.ppermute(message, AXES, pairs(name, direction))  11.5 us
    pallas_call x1, Pallas kernels, on_device(): pl.pallas_call(pair_kernel, out_shape=[jax.ShapeDtypeStruct(WIDE, jnp.bfl...  5.81 us
  transfers between devices with their start and end apart: 12, of which 5 were waited for; matrix products, arithmetic and copies ran while one was open for 0% of the time, Pallas kernels for 0%

profile of v1, /device:TPU:217, one launch (start us, length us, event | category | flops | bytes accessed | tf_op | source)
XLA Modules:
  0.0 60.6 jit_solution(11254201681944488569)
XLA Ops:
  0.6 0.0 copy-start.3
  0.6 1.0 %constant_dynamic-update-slice_fusion.1 = bf16[256,768]{1,0:T(8,128)(2,1)S(1)} fusion(bf16[128,768]{1,0:T(8,128)(2,1)} %param.7), kind=kLoop, calls=%fused_computation.1 | loop fusion | bytes 393216
  1.6 0.0 copy-done.3
  1.7 0.0 copy-start
  1.7 0.0 copy-start.1
  1.7 0.0 copy-start.2
  1.7 2.7 %collective-permute-start.5 = (bf16[256,768]{1,0:T(8,128)(2,1)S(1)}, bf16[256,768]{1,0:T(8,128)(2,1)S(1)}, u32[]{:S(2)}, u32[]{:S(2)}) collective-permute-start(bf16[256,768]{1,0:T(8,128)(2,1)S(1)} %constant_dynamic-update-slice_fusion.own), channel_id=1, source_target_pairs={{1,0},{2,1},{3,2},{4,3},{5,4},{6,5},{7,6},{8,7},{9,8},{10,9},{11,1... | collective-permute-start | bytes 1179656 | tf_op jit(solution)/shard_map/ppermute | solution.py:37
  4.4 5.1 %collective-permute-start.4 = (bf16[256,768]{1,0:T(8,128)(2,1)S(1)}, bf16[256,768]{1,0:T(8,128)(2,1)S(1)}, u32[]{:S(2)}, u32[]{:S(2)}) collective-permute-start(bf16[256,768]{1,0:T(8,128)(2,1)S(1)} %constant_dynamic-update-slice_fusion.own), channel_id=1, source_target_pairs={{0,1},{1,2},{2,3},{3,4},{4,5},{5,6},{6,7},{7,8},{8,9},{9,10},{10,1... | collective-permute-start | bytes 1179656 | tf_op jit(solution)/shard_map/ppermute | solution.py:37
  9.5 1.3 %collective-permute-start.3 = (bf16[256,768]{1,0:T(8,128)(2,1)S(1)}, bf16[256,768]{1,0:T(8,128)(2,1)S(1)}, u32[]{:S(2)}, u32[]{:S(2)}) collective-permute-start(bf16[256,768]{1,0:T(8,128)(2,1)S(1)} %constant_dynamic-update-slice_fusion.own), channel_id=1, source_target_pairs={{16,0},{17,1},{18,2},{19,3},{20,4},{21,5},{22,6},{23,7},{24,8},{25... | collective-permute-start | bytes 1179656 | tf_op jit(solution)/shard_map/ppermute | solution.py:37
  10.8 4.0 %collective-permute-start.2 = (bf16[256,768]{1,0:T(8,128)(2,1)S(1)}, bf16[256,768]{1,0:T(8,128)(2,1)S(1)}, u32[]{:S(2)}, u32[]{:S(2)}) collective-permute-start(bf16[256,768]{1,0:T(8,128)(2,1)S(1)} %constant_dynamic-update-slice_fusion.own), channel_id=1, source_target_pairs={{0,16},{1,17},{2,18},{3,19},{4,20},{5,21},{6,22},{7,23},{8,24},{9,... | collective-permute-start | bytes 1179656 | tf_op jit(solution)/shard_map/ppermute | solution.py:37
  14.9 2.1 %collective-permute-start.1 = (bf16[256,768]{1,0:T(8,128)(2,1)S(1)}, bf16[256,768]{1,0:T(8,128)(2,1)S(1)}, u32[]{:S(2)}, u32[]{:S(2)}) collective-permute-start(bf16[256,768]{1,0:T(8,128)(2,1)S(1)} %constant_dynamic-update-slice_fusion.own), channel_id=1, source_target_pairs={{64,0},{65,1},{66,2},{67,3},{68,4},{69,5},{70,6},{71,7},{72,8},{73... | collective-permute-start | bytes 1179656 | tf_op jit(solution)/shard_map/ppermute | solution.py:37
  16.9 0.0 collective-permute-done.5.refs_5_
  16.9 4.4 %collective-permute-start = (bf16[256,768]{1,0:T(8,128)(2,1)S(1)}, bf16[256,768]{1,0:T(8,128)(2,1)S(1)}, u32[]{:S(2)}, u32[]{:S(2)}) collective-permute-start(bf16[256,768]{1,0:T(8,128)(2,1)S(1)} %constant_dynamic-update-slice_fusion.own), channel_id=1, source_target_pairs={{0,64},{1,65},{2,66},{3,67},{4,68},{5,69},{6,70},{7,71},{8,72},{9,... | collective-permute-start | bytes 1179656 | tf_op jit(solution)/shard_map/ppermute | solution.py:37
  22.0 0.0 collective-permute-done.4.refs_4_
  22.0 0.0 collective-permute-done.3.refs_3_
  22.0 0.0 collective-permute-done.2.refs_2_
  22.0 5.1 %collective-permute-done.1.refs_1_ = bf16[256,768]{1,0:T(8,128)(2,1)S(1)} collective-permute-done((bf16[256,768]{1,0:T(8,128)(2,1)S(1)}, bf16[256,768]{1,0:T(8,128)(2,1)S(1)}, u32[]{:S(2)}, u32[]{:S(2)}) %collective-permute-start.1) | collective-permute-done | bytes 393248 | tf_op jit(solution)/shard_map/ppermute | solution.py:37
  27.1 1.8 %collective-permute-done.refs_0_ = bf16[256,768]{1,0:T(8,128)(2,1)S(1)} collective-permute-done((bf16[256,768]{1,0:T(8,128)(2,1)S(1)}, bf16[256,768]{1,0:T(8,128)(2,1)S(1)}, u32[]{:S(2)}, u32[]{:S(2)}) %collective-permute-start) | collective-permute-done | bytes 393248 | tf_op jit(solution)/shard_map/ppermute | solution.py:37
  28.9 0.0 copy-done
  28.9 0.0 copy-done.1
  28.9 0.0 copy-done.2
  28.9 5.8 %pairs.1 = (bf16[256,768]{1,0:T(8,128)(2,1)S(1)}, bf16[256,768]{1,0:T(8,128)(2,1)S(1)}, bf16[256,768]{1,0:T(8,128)(2,1)S(1)}, bf16[256,768]{1,0:T(8,128)(2,1)S(1...) custom-call(s32[1,7]{1,0:T(1,128)S(1)} %copy-done.2, ...), custom_call_target="tpu_custom_call" | custom-call | tf_op jit(solution)/shard_map/pairs/pallas_call | solution.py:123
  34.7 1.9 %collective-permute-start.6 = (bf16[256,768]{1,0:T(8,128)(2,1)S(1)}, bf16[256,768]{1,0:T(8,128)(2,1)S(1)}, u32[]{:S(2)}, u32[]{:S(2)}) collective-permute-start(bf16[256,768]{1,0:T(8,128)(2,1)S(1)} %get-tuple-element.15), channel_id=1, source_target_pairs={{64,0},{65,1},{66,2},{67,3},{68,4},{69,5},{70,6},{71,7},{72,8},{73... | collective-permute-start | bytes 1179656 | tf_op jit(solution)/shard_map/ppermute | solution.py:37
  36.6 5.0 %collective-permute-start.7 = (bf16[256,768]{1,0:T(8,128)(2,1)S(1)}, bf16[256,768]{1,0:T(8,128)(2,1)S(1)}, u32[]{:S(2)}, u32[]{:S(2)}) collective-permute-start(bf16[256,768]{1,0:T(8,128)(2,1)S(1)} %get-tuple-element.16), channel_id=1, source_target_pairs={{0,64},{1,65},{2,66},{3,67},{4,68},{5,69},{6,70},{7,71},{8,72},{9,... | collective-permute-start | bytes 1179656 | tf_op jit(solution)/shard_map/ppermute | solution.py:37
  41.7 1.3 %collective-permute-start.8 = (bf16[256,768]{1,0:T(8,128)(2,1)S(1)}, bf16[256,768]{1,0:T(8,128)(2,1)S(1)}, u32[]{:S(2)}, u32[]{:S(2)}) collective-permute-start(bf16[256,768]{1,0:T(8,128)(2,1)S(1)} %get-tuple-element.17), channel_id=1, source_target_pairs={{16,0},{17,1},{18,2},{19,3},{20,4},{21,5},{22,6},{23,7},{24,8},{25... | collective-permute-start | bytes 1179656 | tf_op jit(solution)/shard_map/ppermute | solution.py:37
  43.0 4.0 %collective-permute-start.9 = (bf16[256,768]{1,0:T(8,128)(2,1)S(1)}, bf16[256,768]{1,0:T(8,128)(2,1)S(1)}, u32[]{:S(2)}, u32[]{:S(2)}) collective-permute-start(bf16[256,768]{1,0:T(8,128)(2,1)S(1)} %get-tuple-element.18), channel_id=1, source_target_pairs={{0,16},{1,17},{2,18},{3,19},{4,20},{5,21},{6,22},{7,23},{8,24},{9,... | collective-permute-start | bytes 1179656 | tf_op jit(solution)/shard_map/ppermute | solution.py:37
  47.0 2.0 %collective-permute-start.10 = (bf16[256,768]{1,0:T(8,128)(2,1)S(1)}, bf16[256,768]{1,0:T(8,128)(2,1)S(1)}, u32[]{:S(2)}, u32[]{:S(2)}) collective-permute-start(bf16[256,768]{1,0:T(8,128)(2,1)S(1)} %get-tuple-element.19), channel_id=1, source_target_pairs={{1,0},{2,1},{3,2},{4,3},{5,4},{6,5},{7,6},{8,7},{9,8},{10,9},{11,1... | collective-permute-start | bytes 1179656 | tf_op jit(solution)/shard_map/ppermute | solution.py:37
  49.0 0.0 collective-permute-done.6.refs_0_
  49.0 5.8 %collective-permute-start.11 = (bf16[256,768]{1,0:T(8,128)(2,1)S(1)}, bf16[256,768]{1,0:T(8,128)(2,1)S(1)}, u32[]{:S(2)}, u32[]{:S(2)}) collective-permute-start(bf16[256,768]{1,0:T(8,128)(2,1)S(1)} %get-tuple-element.20), channel_id=1, source_target_pairs={{0,1},{1,2},{2,3},{3,4},{4,5},{5,6},{6,7},{7,8},{8,9},{9,10},{10,1... | collective-permute-start | bytes 1179656 | tf_op jit(solution)/shard_map/ppermute | solution.py:37
  54.9 0.0 collective-permute-done.7.refs_1_
  54.9 0.0 collective-permute-done.8.refs_2_
  54.9 0.8 %collective-permute-done.9.refs_3_ = bf16[256,768]{1,0:T(8,128)(2,1)S(1)} collective-permute-done((bf16[256,768]{1,0:T(8,128)(2,1)S(1)}, bf16[256,768]{1,0:T(8,128)(2,1)S(1)}, u32[]{:S(2)}, u32[]{:S(2)}) %collective-permute-start.9) | collective-permute-done | bytes 393248 | tf_op jit(solution)/shard_map/ppermute | solution.py:37
  55.6 2.7 %collective-permute-done.10.refs_4_ = bf16[256,768]{1,0:T(8,128)(2,1)S(1)} collective-permute-done((bf16[256,768]{1,0:T(8,128)(2,1)S(1)}, bf16[256,768]{1,0:T(8,128)(2,1)S(1)}, u32[]{:S(2)}, u32[]{:S(2)}) %collective-permute-start.10) | collective-permute-done | bytes 393248 | tf_op jit(solution)/shard_map/ppermute | solution.py:37
  58.4 1.2 %collective-permute-done.11.refs_5_ = bf16[256,768]{1,0:T(8,128)(2,1)S(1)} collective-permute-done((bf16[256,768]{1,0:T(8,128)(2,1)S(1)}, bf16[256,768]{1,0:T(8,128)(2,1)S(1)}, u32[]{:S(2)}, u32[]{:S(2)}) %collective-permute-start.11) | collective-permute-done | bytes 393248 | tf_op jit(solution)/shard_map/ppermute | solution.py:37
  59.6 1.0 %sums.1 = (bf16[128,768]{1,0:T(8,128)(2,1)}, bf16[128,768]{1,0:T(8,128)(2,1)}) custom-call(f32[256,768]{1,0:T(8,128)S(1)} %get-tuple-element.14.own, bf16[256,768]{1,0:T(8,128)(2,1)S(1)} %collective-permute-done.6.refs_0_, bf16[256,768]{1,0:T(8,128)(2,1)S(1)} %collective-permute-done.7.refs_1_, bf16[256,768]{1,0:T(8,128)(2,1)S(1)} %collective-permute-done.8.refs_2_, ...), custom_call_target="tpu_custom_call" | custom-call | tf_op jit(solution)/shard_map/sums/pallas_call | solution.py:136
  (1 shorter events, 0.0 us)
Async XLA Ops:
  0.6 1.0 %copy-start.3 = (bf16[128,768]{1,0:T(8,128)(2,1)S(1)}, bf16[128,768]{1,0:T(8,128)(2,1)}, u32[]{:S(2)}) copy-start(bf16[128,768]{1,0:T(8,128)(2,1)} %param.8) | copy-start | bytes 589828
  1.7 27.2 %copy-start = (bf16[128,768]{1,0:T(8,128)(2,1)S(1)}, bf16[128,768]{1,0:T(8,128)(2,1)}, u32[]{:S(2)}) copy-start(bf16[128,768]{1,0:T(8,128)(2,1)} %query.1) | copy-start | bytes 589828
  1.7 27.2 %copy-start.1 = (bf16[128,768]{1,0:T(8,128)(2,1)S(1)}, bf16[128,768]{1,0:T(8,128)(2,1)}, u32[]{:S(2)}) copy-start(bf16[128,768]{1,0:T(8,128)(2,1)} %dout.1) | copy-start | bytes 589828
  1.7 27.2 %copy-start.2 = (s32[1,7]{1,0:T(1,128)S(1)}, s32[1,7]{1,0:T(1,128)}, u32[]{:S(2)}) copy-start(s32[1,7]{1,0:T(1,128)} %partners.1) | copy-start | bytes 88
  1.7 15.2 %collective-permute-start.5 = (bf16[256,768]{1,0:T(8,128)(2,1)S(1)}, bf16[256,768]{1,0:T(8,128)(2,1)S(1)}, u32[]{:S(2)}, u32[]{:S(2)}) collective-permute-start(bf16[256,768]{1,0:T(8,128)(2,1)S(1)} %constant_dynamic-update-slice_fusion.own), channel_id=1, source_target_pairs={{1,0},{2,1},{3,2},{4,3},{5,4},{6,5},{7,6},{8,7},{9,8},{10,9},{11,1... | collective-permute-start | bytes 1179656 | tf_op jit(solution)/shard_map/ppermute | solution.py:37
  4.4 17.6 %collective-permute-start.4 = (bf16[256,768]{1,0:T(8,128)(2,1)S(1)}, bf16[256,768]{1,0:T(8,128)(2,1)S(1)}, u32[]{:S(2)}, u32[]{:S(2)}) collective-permute-start(bf16[256,768]{1,0:T(8,128)(2,1)S(1)} %constant_dynamic-update-slice_fusion.own), channel_id=1, source_target_pairs={{0,1},{1,2},{2,3},{3,4},{4,5},{5,6},{6,7},{7,8},{8,9},{9,10},{10,1... | collective-permute-start | bytes 1179656 | tf_op jit(solution)/shard_map/ppermute | solution.py:37
  9.5 12.5 %collective-permute-start.3 = (bf16[256,768]{1,0:T(8,128)(2,1)S(1)}, bf16[256,768]{1,0:T(8,128)(2,1)S(1)}, u32[]{:S(2)}, u32[]{:S(2)}) collective-permute-start(bf16[256,768]{1,0:T(8,128)(2,1)S(1)} %constant_dynamic-update-slice_fusion.own), channel_id=1, source_target_pairs={{16,0},{17,1},{18,2},{19,3},{20,4},{21,5},{22,6},{23,7},{24,8},{25... | collective-permute-start | bytes 1179656 | tf_op jit(solution)/shard_map/ppermute | solution.py:37
  10.8 11.2 %collective-permute-start.2 = (bf16[256,768]{1,0:T(8,128)(2,1)S(1)}, bf16[256,768]{1,0:T(8,128)(2,1)S(1)}, u32[]{:S(2)}, u32[]{:S(2)}) collective-permute-start(bf16[256,768]{1,0:T(8,128)(2,1)S(1)} %constant_dynamic-update-slice_fusion.own), channel_id=1, source_target_pairs={{0,16},{1,17},{2,18},{3,19},{4,20},{5,21},{6,22},{7,23},{8,24},{9,... | collective-permute-start | bytes 1179656 | tf_op jit(solution)/shard_map/ppermute | solution.py:37
  14.9 12.3 %collective-permute-start.1 = (bf16[256,768]{1,0:T(8,128)(2,1)S(1)}, bf16[256,768]{1,0:T(8,128)(2,1)S(1)}, u32[]{:S(2)}, u32[]{:S(2)}) collective-permute-start(bf16[256,768]{1,0:T(8,128)(2,1)S(1)} %constant_dynamic-update-slice_fusion.own), channel_id=1, source_target_pairs={{64,0},{65,1},{66,2},{67,3},{68,4},{69,5},{70,6},{71,7},{72,8},{73... | collective-permute-start | bytes 1179656 | tf_op jit(solution)/shard_map/ppermute | solution.py:37
  16.9 11.9 %collective-permute-start = (bf16[256,768]{1,0:T(8,128)(2,1)S(1)}, bf16[256,768]{1,0:T(8,128)(2,1)S(1)}, u32[]{:S(2)}, u32[]{:S(2)}) collective-permute-start(bf16[256,768]{1,0:T(8,128)(2,1)S(1)} %constant_dynamic-update-slice_fusion.own), channel_id=1, source_target_pairs={{0,64},{1,65},{2,66},{3,67},{4,68},{5,69},{6,70},{7,71},{8,72},{9,... | collective-permute-start | bytes 1179656 | tf_op jit(solution)/shard_map/ppermute | solution.py:37
  34.7 14.3 %collective-permute-start.6 = (bf16[256,768]{1,0:T(8,128)(2,1)S(1)}, bf16[256,768]{1,0:T(8,128)(2,1)S(1)}, u32[]{:S(2)}, u32[]{:S(2)}) collective-permute-start(bf16[256,768]{1,0:T(8,128)(2,1)S(1)} %get-tuple-element.15), channel_id=1, source_target_pairs={{64,0},{65,1},{66,2},{67,3},{68,4},{69,5},{70,6},{71,7},{72,8},{73... | collective-permute-start | bytes 1179656 | tf_op jit(solution)/shard_map/ppermute | solution.py:37
  36.6 18.2 %collective-permute-start.7 = (bf16[256,768]{1,0:T(8,128)(2,1)S(1)}, bf16[256,768]{1,0:T(8,128)(2,1)S(1)}, u32[]{:S(2)}, u32[]{:S(2)}) collective-permute-start(bf16[256,768]{1,0:T(8,128)(2,1)S(1)} %get-tuple-element.16), channel_id=1, source_target_pairs={{0,64},{1,65},{2,66},{3,67},{4,68},{5,69},{6,70},{7,71},{8,72},{9,... | collective-permute-start | bytes 1179656 | tf_op jit(solution)/shard_map/ppermute | solution.py:37
  41.7 13.2 %collective-permute-start.8 = (bf16[256,768]{1,0:T(8,128)(2,1)S(1)}, bf16[256,768]{1,0:T(8,128)(2,1)S(1)}, u32[]{:S(2)}, u32[]{:S(2)}) collective-permute-start(bf16[256,768]{1,0:T(8,128)(2,1)S(1)} %get-tuple-element.17), channel_id=1, source_target_pairs={{16,0},{17,1},{18,2},{19,3},{20,4},{21,5},{22,6},{23,7},{24,8},{25... | collective-permute-start | bytes 1179656 | tf_op jit(solution)/shard_map/ppermute | solution.py:37
  43.0 12.7 %collective-permute-start.9 = (bf16[256,768]{1,0:T(8,128)(2,1)S(1)}, bf16[256,768]{1,0:T(8,128)(2,1)S(1)}, u32[]{:S(2)}, u32[]{:S(2)}) collective-permute-start(bf16[256,768]{1,0:T(8,128)(2,1)S(1)} %get-tuple-element.18), channel_id=1, source_target_pairs={{0,16},{1,17},{2,18},{3,19},{4,20},{5,21},{6,22},{7,23},{8,24},{9,... | collective-permute-start | bytes 1179656 | tf_op jit(solution)/shard_map/ppermute | solution.py:37
  47.0 11.4 %collective-permute-start.10 = (bf16[256,768]{1,0:T(8,128)(2,1)S(1)}, bf16[256,768]{1,0:T(8,128)(2,1)S(1)}, u32[]{:S(2)}, u32[]{:S(2)}) collective-permute-start(bf16[256,768]{1,0:T(8,128)(2,1)S(1)} %get-tuple-element.19), channel_id=1, source_target_pairs={{1,0},{2,1},{3,2},{4,3},{5,4},{6,5},{7,6},{8,7},{9,8},{10,9},{11,1... | collective-permute-start | bytes 1179656 | tf_op jit(solution)/shard_map/ppermute | solution.py:37
  49.0 10.6 %collective-permute-start.11 = (bf16[256,768]{1,0:T(8,128)(2,1)S(1)}, bf16[256,768]{1,0:T(8,128)(2,1)S(1)}, u32[]{:S(2)}, u32[]{:S(2)}) collective-permute-start(bf16[256,768]{1,0:T(8,128)(2,1)S(1)} %get-tuple-element.20), channel_id=1, source_target_pairs={{0,1},{1,2},{2,3},{3,4},{4,5},{5,6},{6,7},{7,8},{8,9},{9,10},{10,1... | collective-permute-start | bytes 1179656 | tf_op jit(solution)/shard_map/ppermute | solution.py:37

commit v2 on v1

v2 whole, which is shorter than its diff:
```python
import functools

import jax
import jax.numpy as jnp
from jax import lax
from jax.experimental import pallas as pl
from jax.experimental.pallas import tpu as pltpu
from jax.sharding import PartitionSpec as P

HEADS = 6
HD = 128
BLOCK = 128
AXES = ("inner", "outer")
SCALE = HD ** -0.5
SCALE2 = SCALE * 1.4426950408889634
NEG = -1e30
STEP = {"x": 16, "y": 64, "z": 1}
SIZE = {"x": 4, "y": 8, "z": 16}
BLOCKS = 512
ROUTES = (
    (("z", 1), ("z", 1)),
    (("y", 0), ("x", 0)),
    (("y", 1), ("x", 1)),
    (("x", 0), ("y", 0)),
    (("x", 1), ("y", 1)),
    (("z", 0), ("z", 0)),
)
EARLY = 4
BACK = (0, 1, 2, 3, 4, 5)
SUMMED = 4


def route_pairs(route):
    found = []
    for block in range(BLOCKS):
        name, odd = route[block & 1]
        place = (block // STEP[name]) % SIZE[name]
        sign = 1 - 2 * ((place + odd) & 1)
        if 0 <= place + sign < SIZE[name]:
            found.append((block, block + sign * STEP[name]))
    return found


def swapped(message, index):
    return lax.ppermute(message, AXES, route_pairs(ROUTES[index]))


def partner_of(me, index):
    targets = []
    for name, odd in ROUTES[index]:
        place = lax.div(me, jnp.int32(STEP[name])) & (SIZE[name] - 1)
        sign = 1 - 2 * ((place + odd) & 1)
        targets.append(me + sign * STEP[name])
    return jnp.where((me & 1) == 0, targets[0], targets[1])


def bias_of(partners, me, index):
    target = partner_of(me, index)
    listed = jnp.int32(0)
    for slot in range(1, 7):
        listed = listed | (partners[0, slot] == target).astype(jnp.int32)
    return jnp.where(listed > 0, jnp.float32(0.0), jnp.float32(NEG))


def dot(a, b, da, db):
    return lax.dot_general(a, b, (((da,), (db,)), ((), ())), preferred_element_type=jnp.float32)


KEYS = pl.ds(0, BLOCK)
VALUES = pl.ds(BLOCK, BLOCK)


def lanes_of(head):
    return pl.ds(head * HD, HD)


def score(blocks, q, lanes):
    return [dot(block[KEYS, lanes], q, 1, 1) for block in blocks]


def weigh(scores, blocks, biases, do, lanes, before=None):
    tops = [
        jnp.max(s, axis=0, keepdims=True) * SCALE2 + bias for s, bias in zip(scores, biases)
    ]
    top = functools.reduce(jnp.maximum, tops + ([before] if before is not None else []))
    weights = [jnp.exp2(s * SCALE2 + (bias - top)) for s, bias in zip(scores, biases)]
    grads = [dot(block[VALUES, lanes], do, 1, 1) for block in blocks]
    total = functools.reduce(jnp.add, [jnp.sum(w, axis=0, keepdims=True) for w in weights])
    delta = functools.reduce(
        jnp.add, [jnp.sum(w * g, axis=0, keepdims=True) for w, g in zip(weights, grads)]
    )
    return weights, grads, top, total, delta


def pack_kernel(query, keys, values, dout, own, asks, sems):
    copies = [
        pltpu.make_async_copy(source, target, sems.at[i])
        for i, (source, target) in enumerate(
            (
                (keys, own.at[KEYS, :]),
                (values, own.at[VALUES, :]),
                (query, asks.at[KEYS, :]),
                (dout, asks.at[VALUES, :]),
            )
        )
    ]
    for copy in copies:
        copy.start()
    for copy in copies:
        copy.wait()


def early_kernel(partners, asks, own, *refs):
    blocks, refs = (own,) + refs[:EARLY][::-1], refs[EARLY:]
    weights_out, grads_out, stats_out, partner_list, sem = refs
    fetch = pltpu.make_async_copy(partners, partner_list, sem)
    fetch.start()

    def read_lists():
        fetch.wait()
        me = partner_list[0, 0]
        return [
            jnp.full((1, HD), bias_of(partner_list, me, index), jnp.float32)
            for index in range(6)
        ]

    rows = None
    for head in range(HEADS):
        lanes = lanes_of(head)
        q, do = asks[KEYS, lanes], asks[VALUES, lanes]
        scores = score(blocks, q, lanes)
        if rows is None:
            rows = [jnp.zeros((1, HD), jnp.float32)] + read_lists()
        weights, grads, top, total, delta = weigh(scores, blocks, rows[: EARLY + 1], do, lanes)
        for index in range(EARLY + 1):
            weights_out[index, :, lanes] = weights[index]
            grads_out[index, :, lanes] = grads[index]
        stats_out[0:1, lanes] = top
        stats_out[1:2, lanes] = total
        stats_out[2:3, lanes] = delta
        for index in range(EARLY, 6):
            stats_out[3 + index - EARLY : 4 + index - EARLY, lanes] = rows[1 + index]


def late_kernel(asks, early_weights, early_grads, stats, *refs):
    late = 6 - EARLY
    blocks, refs = refs[:late][::-1], refs[late:]
    terms, dscores_out, final_out = refs[:6], refs[6], refs[7]
    for head in range(HEADS):
        lanes = lanes_of(head)
        q, do = asks[KEYS, lanes], asks[VALUES, lanes]
        before = stats[0:1, lanes]
        rows = [stats[3 + i : 4 + i, lanes] for i in range(late)]
        scores = score(blocks, q, lanes)
        weights, grads, top, total, delta = weigh(scores, blocks, rows, do, lanes, before)
        old = jnp.exp2(before - top)
        total = total + stats[1:2, lanes] * old
        delta = delta + stats[2:3, lanes] * old
        new = 1.0 / total
        delta = delta * new
        old = old * new
        final_out[0:1, lanes] = old
        final_out[1:2, lanes] = delta
        for index in range(6):
            if index < EARLY:
                probs = early_weights[index + 1, :, lanes] * old
                grad = early_grads[index + 1, :, lanes]
            else:
                probs = weights[index - EARLY] * new
                grad = grads[index - EARLY]
            dscores = (probs * (grad - delta)).astype(jnp.bfloat16)
            probs = probs.astype(jnp.bfloat16)
            dscores_out[index, :, lanes] = dscores
            out = terms[index]
            out[KEYS, lanes] = dot(dscores, q, 1, 0).astype(out.dtype)
            out[VALUES, lanes] = dot(probs, do, 1, 0).astype(out.dtype)


def own_kernel(asks, early_weights, early_grads, final, dscores, own, *refs):
    blocks, parts, (query_out, own_out) = refs[:6], refs[6 : 6 + SUMMED], refs[6 + SUMMED :]
    for head in range(HEADS):
        lanes = lanes_of(head)
        probs = early_weights[0, :, lanes] * final[0:1, lanes]
        mine = (probs * (early_grads[0, :, lanes] - final[1:2, lanes])).astype(jnp.bfloat16)
        probs = probs.astype(jnp.bfloat16)
        grad = dot(mine, own[KEYS, lanes], 0, 0)
        for index in range(6):
            grad = grad + dot(dscores[index, :, lanes], blocks[index][KEYS, lanes], 0, 0)
        query_out[:, lanes] = (grad * SCALE).astype(query_out.dtype)
        for rows, low in ((KEYS, mine), (VALUES, probs)):
            total = dot(low, asks[rows, lanes], 1, 0)
            for part in parts:
                total = total + part[rows, lanes].astype(jnp.float32)
            own_out[rows, lanes] = total


def sum_kernel(own, *refs):
    parts, (key_out, value_out) = refs[:-2], refs[-2:]
    for rows, out, scale in ((KEYS, key_out, SCALE), (VALUES, value_out, 1.0)):
        total = own[rows, :]
        for part in parts:
            total = total + part[rows, :].astype(jnp.float32)
        out[...] = (total * scale).astype(out.dtype)


FAR = pl.BlockSpec(memory_space=pltpu.HBM)
VM = pl.BlockSpec(memory_space=pltpu.VMEM)
SM = pl.BlockSpec(memory_space=pltpu.SMEM)
WIDE = (2 * BLOCK, HEADS * HD)
NARROW = (BLOCK, HEADS * HD)


NEAR = pltpu.VMEM
PLAIN = jax.ShapeDtypeStruct


def far(array):
    return pltpu.with_memory_space_constraint(array, pltpu.HBM)


def call(kernel, ins, outs, name, scratch=()):
    return pl.pallas_call(
        kernel,
        out_shape=[
            place(shape, dtype) for place, shape, dtype in outs
        ],
        in_specs=ins,
        out_specs=[VM] * len(outs),
        scratch_shapes=list(scratch),
        compiler_params=pltpu.CompilerParams(vmem_limit_bytes=40 * 1024 * 1024),
        name=name,
    )


def on_device(query, keys, values, dout, partners, counts):
    low, full = jnp.bfloat16, jnp.float32
    own, asks = call(
        pack_kernel,
        [FAR] * 4,
        [(NEAR, WIDE, low)] * 2,
        "pack",
        [pltpu.SemaphoreType.DMA((4,))],
    )(far(query), far(keys), far(values), far(dout))
    blocks = [swapped(own, index) for index in range(6)]
    weights, grads, stats = call(
        early_kernel,
        [FAR] + [VM] * (2 + EARLY),
        [(NEAR, (EARLY + 1,) + NARROW, full)] * 2 + [(NEAR, (8, HEADS * HD), full)],
        "early",
        [
            pltpu.SMEM((1, 7), jnp.int32),
            pltpu.SemaphoreType.DMA,
        ],
    )(far(partners), asks, own, *blocks[:EARLY][::-1])
    outs = call(
        late_kernel,
        [VM] * (4 + 6 - EARLY),
        [(NEAR, WIDE, low)] * 6 + [(NEAR, (6,) + NARROW, low), (NEAR, (8, HEADS * HD), full)],
        "late",
    )(asks, weights, grads, stats, *blocks[EARLY:][::-1])
    terms, dscores, final = outs[:6], outs[6], outs[7]
    arrived = [swapped(terms[index], index) for index in BACK]
    query_out, own_out = call(
        own_kernel, [VM] * (12 + SUMMED), [(PLAIN, NARROW, low), (NEAR, WIDE, full)], "own"
    )(asks, weights, grads, final, dscores, own, *blocks, *arrived[:SUMMED])
    key_out, value_out = call(sum_kernel, [VM] * (7 - SUMMED), [(PLAIN, NARROW, low)] * 2, "sums")(
        own_out, *arrived[SUMMED:]
    )
    return query_out, key_out, value_out


def solution(mesh):
    tokens = P(AXES, None)
    return jax.shard_map(
        on_device,
        mesh=mesh,
        in_specs=(tokens, tokens, tokens, tokens, tokens, P(AXES)),
        out_specs=(tokens, tokens, tokens),
        check_vma=False,
    )
```

time: 61 us -> 50.2 us (0.82)
  the two profiles are of different devices: /device:TPU:217 before, /device:TPU:211 now
where the time goes in v2:
time: 50.2 us; the launch traced here: 49.7 us
  starting transfers between devices  35.1 us (70%)
  Pallas kernels  8.07 us (16%)
  waiting for transfers between devices  5.73 us (11%)
  between operations  0.8 us (2%)
    ppermute x12, starting transfers between devices, swapped(): return lax.ppermute(message, AXES, route_pairs(ROUTES[index]))  35.1 us
    ppermute x12, waiting for transfers between devices, swapped(): return lax.ppermute(message, AXES, route_pairs(ROUTES[index]))  5.73 us
    pallas_call x1, Pallas kernels, on_device(): call(late_kernel, [VM] * (4 + 6 - EARLY), [(NEAR, WIDE, low)] * 6 + [(NEA...  2.46 us
    pallas_call x1, Pallas kernels, on_device(): call(early_kernel, [FAR] + [VM] * (2 + EARLY), [(NEAR, (EARLY + 1,) + NAR...  2.16 us
    pallas_call x1, Pallas kernels, on_device(): call(own_kernel, [VM] * (12 + SUMMED), [(PLAIN, NARROW, low), (NEAR, WIDE...  1.38 us
    pallas_call x1, Pallas kernels, on_device(): call(pack_kernel, [FAR] * 4, [(NEAR, WIDE, low)] * 2, 'pack', [pltpu.Sema...  1.25 us
  transfers between devices with their start and end apart: 12, of which 4 were waited for; matrix products, arithmetic and copies ran while one was open for 0% of the time, Pallas kernels for 7%

profile of v2, /device:TPU:211, one launch (start us, length us, event | category | flops | bytes accessed | tf_op | source)
XLA Modules:
  0.0 49.7 jit_solution(8125770495393749822)
XLA Ops:
  0.6 1.3 %pack.1 = (bf16[256,768]{1,0:T(8,128)(2,1)S(1)}, bf16[256,768]{1,0:T(8,128)(2,1)S(1)}) custom-call(bf16[128,768]{1,0:T(8,128)(2,1)} %query.1, bf16[128,768]{1,0:T(8,128)(2,1)} %keys.1, bf16[128,768]{1,0:T(8,128)(2,1)} %values.1, bf16[128,768]{1,0:T(8,128)(2,1)} %dout.1), custom_call_target="tpu_custom_call" | custom-call | tf_op jit(solution)/shard_map/pack/pallas_call | solution.py:237
  1.9 5.8 %collective-permute-start.3 = (bf16[256,768]{1,0:T(8,128)(2,1)S(1)}, bf16[256,768]{1,0:T(8,128)(2,1)S(1)}, u32[]{:S(2)}, u32[]{:S(2)}) collective-permute-start(bf16[256,768]{1,0:T(8,128)(2,1)S(1)} %get-tuple-element.21.own), channel_id=1, source_target_pairs={{1,2},{2,1},{3,4},{4,3},{5,6},{6,5},{7,8},{8,7},{9,10},{10,9},{11,... | collective-permute-start | bytes 1179656 | tf_op jit(solution)/shard_map/ppermute | solution.py:45
  7.7 2.2 %collective-permute-start.2 = (bf16[256,768]{1,0:T(8,128)(2,1)S(1)}, bf16[256,768]{1,0:T(8,128)(2,1)S(1)}, u32[]{:S(2)}, u32[]{:S(2)}) collective-permute-start(bf16[256,768]{1,0:T(8,128)(2,1)S(1)} %get-tuple-element.21.own), channel_id=1, source_target_pairs={{0,64},{1,17},{2,66},{3,19},{4,68},{5,21},{6,70},{7,23},{8,72},{9,... | collective-permute-start | bytes 1179656 | tf_op jit(solution)/shard_map/ppermute | solution.py:45
  9.8 3.8 %collective-permute-start.1 = (bf16[256,768]{1,0:T(8,128)(2,1)S(1)}, bf16[256,768]{1,0:T(8,128)(2,1)S(1)}, u32[]{:S(2)}, u32[]{:S(2)}) collective-permute-start(bf16[256,768]{1,0:T(8,128)(2,1)S(1)} %get-tuple-element.21.own), channel_id=1, source_target_pairs={{17,33},{19,35},{21,37},{23,39},{25,41},{27,43},{29,45},{31,47},{3... | collective-permute-start | bytes 1179656 | tf_op jit(solution)/shard_map/ppermute | solution.py:45
  13.6 3.2 %collective-permute-start = (bf16[256,768]{1,0:T(8,128)(2,1)S(1)}, bf16[256,768]{1,0:T(8,128)(2,1)S(1)}, u32[]{:S(2)}, u32[]{:S(2)}) collective-permute-start(bf16[256,768]{1,0:T(8,128)(2,1)S(1)} %get-tuple-element.21.own), channel_id=1, source_target_pairs={{0,16},{1,65},{2,18},{3,67},{4,20},{5,69},{6,22},{7,71},{8,24},{9,... | collective-permute-start | bytes 1179656 | tf_op jit(solution)/shard_map/ppermute | solution.py:45
  16.8 1.9 %collective-permute-start.5 = (bf16[256,768]{1,0:T(8,128)(2,1)S(1)}, bf16[256,768]{1,0:T(8,128)(2,1)S(1)}, u32[]{:S(2)}, u32[]{:S(2)}) collective-permute-start(bf16[256,768]{1,0:T(8,128)(2,1)S(1)} %get-tuple-element.21.own), channel_id=1, source_target_pairs={{16,32},{18,34},{20,36},{22,38},{24,40},{26,42},{28,44},{30,46},{3... | collective-permute-start | bytes 1179656 | tf_op jit(solution)/shard_map/ppermute | solution.py:45
  18.8 0.0 collective-permute-done.3.refs_3_.refs_0_
  18.8 1.9 %collective-permute-start.4 = (bf16[256,768]{1,0:T(8,128)(2,1)S(1)}, bf16[256,768]{1,0:T(8,128)(2,1)S(1)}, u32[]{:S(2)}, u32[]{:S(2)}) collective-permute-start(bf16[256,768]{1,0:T(8,128)(2,1)S(1)} %get-tuple-element.21.own), channel_id=1, source_target_pairs={{0,1},{1,0},{2,3},{3,2},{4,5},{5,4},{6,7},{7,6},{8,9},{9,8},{10,11... | collective-permute-start | bytes 1179656 | tf_op jit(solution)/shard_map/ppermute | solution.py:45
  20.7 0.0 collective-permute-done.2.refs_2_.refs_1_
  20.7 0.0 collective-permute-done.1.refs_1_.refs_2_
  20.7 1.7 %collective-permute-done.refs_0_.refs_3_ = bf16[256,768]{1,0:T(8,128)(2,1)S(1)} collective-permute-done((bf16[256,768]{1,0:T(8,128)(2,1)S(1)}, bf16[256,768]{1,0:T(8,128)(2,1)S(1)}, u32[]{:S(2)}, u32[]{:S(2)}) %collective-permute-start) | collective-permute-done | bytes 393248 | tf_op jit(solution)/shard_map/ppermute | solution.py:45
  22.4 2.2 %early.1 = (f32[5,128,768]{2,1,0:T(8,128)S(1)}, f32[5,128,768]{2,1,0:T(8,128)S(1)}, f32[8,768]{1,0:T(8,128)S(1)}) custom-call(s32[1,7]{1,0:T(1,128)} %partners.1, bf16[256,768]{1,0:T(8,128)(2,1)S(1)} %get-tuple-element.20.asks, bf16[256,768]{1,0:T(8,128)(2,1)S(1)} %get-tuple-element.21.own, bf16[256,768]{1,0:T(8,128)(2,1)S(1)} %collective-permute-done.refs_0_.refs_3_, ...), custom_call_target="tpu_custom_call" | custom-call | tf_op jit(solution)/shard_map/early/pallas_call | solution.py:245
  24.6 0.7 %collective-permute-done.5.refs_1_.refs_4_ = bf16[256,768]{1,0:T(8,128)(2,1)S(1)} collective-permute-done((bf16[256,768]{1,0:T(8,128)(2,1)S(1)}, bf16[256,768]{1,0:T(8,128)(2,1)S(1)}, u32[]{:S(2)}, u32[]{:S(2)}) %collective-permute-start.5) | collective-permute-done | bytes 393248 | tf_op jit(solution)/shard_map/ppermute | solution.py:45
  25.4 0.0 collective-permute-done.4.refs_0_.refs_5_
  25.4 2.5 %late.1 = (bf16[256,768]{1,0:T(8,128)(2,1)S(1)}, bf16[256,768]{1,0:T(8,128)(2,1)S(1)}, bf16[256,768]{1,0:T(8,128)(2,1)S(1)}, bf16[256,768]{1,0:T(8,128)(2,1)S(1)...) custom-call(bf16[256,768]{1,0:T(8,128)(2,1)S(1)} %get-tuple-element., ...), custom_call_target="tpu_custom_call" | custom-call | tf_op jit(solution)/shard_map/late/pallas_call | solution.py:255
  27.8 1.9 %collective-permute-start.6 = (bf16[256,768]{1,0:T(8,128)(2,1)S(1)}, bf16[256,768]{1,0:T(8,128)(2,1)S(1)}, u32[]{:S(2)}, u32[]{:S(2)}) collective-permute-start(bf16[256,768]{1,0:T(8,128)(2,1)S(1)} %get-tuple-element.27), channel_id=1, source_target_pairs={{1,2},{2,1},{3,4},{4,3},{5,6},{6,5},{7,8},{8,7},{9,10},{10,9},{11,... | collective-permute-start | bytes 1179656 | tf_op jit(solution)/shard_map/ppermute | solution.py:45
  29.8 1.9 %collective-permute-start.7 = (bf16[256,768]{1,0:T(8,128)(2,1)S(1)}, bf16[256,768]{1,0:T(8,128)(2,1)S(1)}, u32[]{:S(2)}, u32[]{:S(2)}) collective-permute-start(bf16[256,768]{1,0:T(8,128)(2,1)S(1)} %get-tuple-element.28), channel_id=1, source_target_pairs={{0,64},{1,17},{2,66},{3,19},{4,68},{5,21},{6,70},{7,23},{8,72},{9,... | collective-permute-start | bytes 1179656 | tf_op jit(solution)/shard_map/ppermute | solution.py:45
  31.7 3.6 %collective-permute-start.8 = (bf16[256,768]{1,0:T(8,128)(2,1)S(1)}, bf16[256,768]{1,0:T(8,128)(2,1)S(1)}, u32[]{:S(2)}, u32[]{:S(2)}) collective-permute-start(bf16[256,768]{1,0:T(8,128)(2,1)S(1)} %get-tuple-element.29), channel_id=1, source_target_pairs={{17,33},{19,35},{21,37},{23,39},{25,41},{27,43},{29,45},{31,47},{3... | collective-permute-start | bytes 1179656 | tf_op jit(solution)/shard_map/ppermute | solution.py:45
  35.3 5.1 %collective-permute-start.9 = (bf16[256,768]{1,0:T(8,128)(2,1)S(1)}, bf16[256,768]{1,0:T(8,128)(2,1)S(1)}, u32[]{:S(2)}, u32[]{:S(2)}) collective-permute-start(bf16[256,768]{1,0:T(8,128)(2,1)S(1)} %get-tuple-element.30), channel_id=1, source_target_pairs={{0,16},{1,65},{2,18},{3,67},{4,20},{5,69},{6,22},{7,71},{8,24},{9,... | collective-permute-start | bytes 1179656 | tf_op jit(solution)/shard_map/ppermute | solution.py:45
  40.4 1.9 %collective-permute-start.10 = (bf16[256,768]{1,0:T(8,128)(2,1)S(1)}, bf16[256,768]{1,0:T(8,128)(2,1)S(1)}, u32[]{:S(2)}, u32[]{:S(2)}) collective-permute-start(bf16[256,768]{1,0:T(8,128)(2,1)S(1)} %get-tuple-element.33), channel_id=1, source_target_pairs={{16,32},{18,34},{20,36},{22,38},{24,40},{26,42},{28,44},{30,46},{3... | collective-permute-start | bytes 1179656 | tf_op jit(solution)/shard_map/ppermute | solution.py:45
  42.3 0.0 collective-permute-done.6.refs_6_
  42.3 1.9 %collective-permute-start.11 = (bf16[256,768]{1,0:T(8,128)(2,1)S(1)}, bf16[256,768]{1,0:T(8,128)(2,1)S(1)}, u32[]{:S(2)}, u32[]{:S(2)}) collective-permute-start(bf16[256,768]{1,0:T(8,128)(2,1)S(1)} %get-tuple-element.34), channel_id=1, source_target_pairs={{0,1},{1,0},{2,3},{3,2},{4,5},{5,4},{6,7},{7,6},{8,9},{9,8},{10,11... | collective-permute-start | bytes 1179656 | tf_op jit(solution)/shard_map/ppermute | solution.py:45
  44.3 0.0 collective-permute-done.7.refs_7_
  44.3 0.0 collective-permute-done.8.refs_8_
  44.3 1.6 %collective-permute-done.9.refs_9_ = bf16[256,768]{1,0:T(8,128)(2,1)S(1)} collective-permute-done((bf16[256,768]{1,0:T(8,128)(2,1)S(1)}, bf16[256,768]{1,0:T(8,128)(2,1)S(1)}, u32[]{:S(2)}, u32[]{:S(2)}) %collective-permute-start.9) | collective-permute-done | bytes 393248 | tf_op jit(solution)/shard_map/ppermute | solution.py:45
  45.8 1.4 %own.1 = (bf16[128,768]{1,0:T(8,128)(2,1)}, f32[256,768]{1,0:T(8,128)S(1)}) custom-call(bf16[256,768]{1,0:T(8,128)(2,1)S(1)} %get-tuple-element.20.asks, f32[5,128,768]{2,1,0:T(8,128)S(1)} %get-tuple-element.22.early_weights, f32[5,128,768]{2,1,0:T(8,128)S(1)} %get-tuple-element.23.early_grads, f32[8,768]{1,0:T(8,128)S(1)} %get-tuple-element.25.final, ...), custom_call_target="tpu_custom_call" | custom-call | tf_op jit(solution)/shard_map/own/pallas_call | solution.py:263
  47.2 1.7 %collective-permute-done.10.refs_0_ = bf16[256,768]{1,0:T(8,128)(2,1)S(1)} collective-permute-done((bf16[256,768]{1,0:T(8,128)(2,1)S(1)}, bf16[256,768]{1,0:T(8,128)(2,1)S(1)}, u32[]{:S(2)}, u32[]{:S(2)}) %collective-permute-start.10) | collective-permute-done | bytes 393248 | tf_op jit(solution)/shard_map/ppermute | solution.py:45
  48.9 0.0 collective-permute-done.11.refs_1_
  48.9 0.8 %sums.1 = (bf16[128,768]{1,0:T(8,128)(2,1)}, bf16[128,768]{1,0:T(8,128)(2,1)}) custom-call(f32[256,768]{1,0:T(8,128)S(1)} %get-tuple-element.32.own, bf16[256,768]{1,0:T(8,128)(2,1)S(1)} %collective-permute-done.10.refs_0_, bf16[256,768]{1,0:T(8,128)(2,1)S(1)} %collective-permute-done.11.refs_1_), custom_call_target="tpu_custom_call" | custom-call | tf_op jit(solution)/shard_map/sums/pallas_call | solution.py:266
Async XLA Ops:
  1.9 16.9 %collective-permute-start.3 = (bf16[256,768]{1,0:T(8,128)(2,1)S(1)}, bf16[256,768]{1,0:T(8,128)(2,1)S(1)}, u32[]{:S(2)}, u32[]{:S(2)}) collective-permute-start(bf16[256,768]{1,0:T(8,128)(2,1)S(1)} %get-tuple-element.21.own), channel_id=1, source_target_pairs={{1,2},{2,1},{3,4},{4,3},{5,6},{6,5},{7,8},{8,7},{9,10},{10,9},{11,... | collective-permute-start | bytes 1179656 | tf_op jit(solution)/shard_map/ppermute | solution.py:45
  7.7 13.0 %collective-permute-start.2 = (bf16[256,768]{1,0:T(8,128)(2,1)S(1)}, bf16[256,768]{1,0:T(8,128)(2,1)S(1)}, u32[]{:S(2)}, u32[]{:S(2)}) collective-permute-start(bf16[256,768]{1,0:T(8,128)(2,1)S(1)} %get-tuple-element.21.own), channel_id=1, source_target_pairs={{0,64},{1,17},{2,66},{3,19},{4,68},{5,21},{6,70},{7,23},{8,72},{9,... | collective-permute-start | bytes 1179656 | tf_op jit(solution)/shard_map/ppermute | solution.py:45
  9.8 10.9 %collective-permute-start.1 = (bf16[256,768]{1,0:T(8,128)(2,1)S(1)}, bf16[256,768]{1,0:T(8,128)(2,1)S(1)}, u32[]{:S(2)}, u32[]{:S(2)}) collective-permute-start(bf16[256,768]{1,0:T(8,128)(2,1)S(1)} %get-tuple-element.21.own), channel_id=1, source_target_pairs={{17,33},{19,35},{21,37},{23,39},{25,41},{27,43},{29,45},{31,47},{3... | collective-permute-start | bytes 1179656 | tf_op jit(solution)/shard_map/ppermute | solution.py:45
  13.6 8.8 %collective-permute-start = (bf16[256,768]{1,0:T(8,128)(2,1)S(1)}, bf16[256,768]{1,0:T(8,128)(2,1)S(1)}, u32[]{:S(2)}, u32[]{:S(2)}) collective-permute-start(bf16[256,768]{1,0:T(8,128)(2,1)S(1)} %get-tuple-element.21.own), channel_id=1, source_target_pairs={{0,16},{1,65},{2,18},{3,67},{4,20},{5,69},{6,22},{7,71},{8,24},{9,... | collective-permute-start | bytes 1179656 | tf_op jit(solution)/shard_map/ppermute | solution.py:45
  16.8 8.5 %collective-permute-start.5 = (bf16[256,768]{1,0:T(8,128)(2,1)S(1)}, bf16[256,768]{1,0:T(8,128)(2,1)S(1)}, u32[]{:S(2)}, u32[]{:S(2)}) collective-permute-start(bf16[256,768]{1,0:T(8,128)(2,1)S(1)} %get-tuple-element.21.own), channel_id=1, source_target_pairs={{16,32},{18,34},{20,36},{22,38},{24,40},{26,42},{28,44},{30,46},{3... | collective-permute-start | bytes 1179656 | tf_op jit(solution)/shard_map/ppermute | solution.py:45
  18.8 6.6 %collective-permute-start.4 = (bf16[256,768]{1,0:T(8,128)(2,1)S(1)}, bf16[256,768]{1,0:T(8,128)(2,1)S(1)}, u32[]{:S(2)}, u32[]{:S(2)}) collective-permute-start(bf16[256,768]{1,0:T(8,128)(2,1)S(1)} %get-tuple-element.21.own), channel_id=1, source_target_pairs={{0,1},{1,0},{2,3},{3,2},{4,5},{5,4},{6,7},{7,6},{8,9},{9,8},{10,11... | collective-permute-start | bytes 1179656 | tf_op jit(solution)/shard_map/ppermute | solution.py:45
  27.8 14.5 %collective-permute-start.6 = (bf16[256,768]{1,0:T(8,128)(2,1)S(1)}, bf16[256,768]{1,0:T(8,128)(2,1)S(1)}, u32[]{:S(2)}, u32[]{:S(2)}) collective-permute-start(bf16[256,768]{1,0:T(8,128)(2,1)S(1)} %get-tuple-element.27), channel_id=1, source_target_pairs={{1,2},{2,1},{3,4},{4,3},{5,6},{6,5},{7,8},{8,7},{9,10},{10,9},{11,... | collective-permute-start | bytes 1179656 | tf_op jit(solution)/shard_map/ppermute | solution.py:45
  29.8 14.5 %collective-permute-start.7 = (bf16[256,768]{1,0:T(8,128)(2,1)S(1)}, bf16[256,768]{1,0:T(8,128)(2,1)S(1)}, u32[]{:S(2)}, u32[]{:S(2)}) collective-permute-start(bf16[256,768]{1,0:T(8,128)(2,1)S(1)} %get-tuple-element.28), channel_id=1, source_target_pairs={{0,64},{1,17},{2,66},{3,19},{4,68},{5,21},{6,70},{7,23},{8,72},{9,... | collective-permute-start | bytes 1179656 | tf_op jit(solution)/shard_map/ppermute | solution.py:45
  31.7 12.6 %collective-permute-start.8 = (bf16[256,768]{1,0:T(8,128)(2,1)S(1)}, bf16[256,768]{1,0:T(8,128)(2,1)S(1)}, u32[]{:S(2)}, u32[]{:S(2)}) collective-permute-start(bf16[256,768]{1,0:T(8,128)(2,1)S(1)} %get-tuple-element.29), channel_id=1, source_target_pairs={{17,33},{19,35},{21,37},{23,39},{25,41},{27,43},{29,45},{31,47},{3... | collective-permute-start | bytes 1179656 | tf_op jit(solution)/shard_map/ppermute | solution.py:45
  35.3 10.5 %collective-permute-start.9 = (bf16[256,768]{1,0:T(8,128)(2,1)S(1)}, bf16[256,768]{1,0:T(8,128)(2,1)S(1)}, u32[]{:S(2)}, u32[]{:S(2)}) collective-permute-start(bf16[256,768]{1,0:T(8,128)(2,1)S(1)} %get-tuple-element.30), channel_id=1, source_target_pairs={{0,16},{1,65},{2,18},{3,67},{4,20},{5,69},{6,22},{7,71},{8,24},{9,... | collective-permute-start | bytes 1179656 | tf_op jit(solution)/shard_map/ppermute | solution.py:45
  40.4 8.5 %collective-permute-start.10 = (bf16[256,768]{1,0:T(8,128)(2,1)S(1)}, bf16[256,768]{1,0:T(8,128)(2,1)S(1)}, u32[]{:S(2)}, u32[]{:S(2)}) collective-permute-start(bf16[256,768]{1,0:T(8,128)(2,1)S(1)} %get-tuple-element.33), channel_id=1, source_target_pairs={{16,32},{18,34},{20,36},{22,38},{24,40},{26,42},{28,44},{30,46},{3... | collective-permute-start | bytes 1179656 | tf_op jit(solution)/shard_map/ppermute | solution.py:45
  42.3 6.6 %collective-permute-start.11 = (bf16[256,768]{1,0:T(8,128)(2,1)S(1)}, bf16[256,768]{1,0:T(8,128)(2,1)S(1)}, u32[]{:S(2)}, u32[]{:S(2)}) collective-permute-start(bf16[256,768]{1,0:T(8,128)(2,1)S(1)} %get-tuple-element.34), channel_id=1, source_target_pairs={{0,1},{1,0},{2,3},{3,2},{4,5},{5,4},{6,7},{7,6},{8,9},{9,8},{10,11... | collective-permute-start | bytes 1179656 | tf_op jit(solution)/shard_map/ppermute | solution.py:45

commit v3 on v2

v3 whole, which is shorter than its diff:
```python
import functools

import jax
import jax.numpy as jnp
from jax import lax
from jax.experimental import pallas as pl
from jax.experimental.pallas import tpu as pltpu
from jax.sharding import PartitionSpec as P

HEADS = 6
HD = 128
BLOCK = 128
AXES = ("inner", "outer")
SCALE = HD ** -0.5
SCALE2 = SCALE * 1.4426950408889634
NEG = -1e30
STEP = {"x": 16, "y": 64, "z": 1}
SIZE = {"x": 4, "y": 8, "z": 16}
BLOCKS = 512
ROUTES = (
    (("z", 1), ("z", 1)),
    (("y", 0), ("x", 0)),
    (("y", 1), ("x", 1)),
    (("x", 0), ("y", 0)),
    (("x", 1), ("y", 1)),
    (("z", 0), ("z", 0)),
)
GROUPS = ((0, 1, 2, 3, 4, 5),)
EARLY = 4
BACK = (0, 1, 2, 3, 4, 5)
SUMMED = 4


def route_pairs(route):
    found = []
    for block in range(BLOCKS):
        name, odd = route[block & 1]
        place = (block // STEP[name]) % SIZE[name]
        sign = 1 - 2 * ((place + odd) & 1)
        if 0 <= place + sign < SIZE[name]:
            found.append((block, block + sign * STEP[name]))
    return found


def swapped(message, index):
    return lax.ppermute(message, AXES, route_pairs(ROUTES[index]))


def partner_of(me, index):
    targets = []
    for name, odd in ROUTES[index]:
        place = lax.div(me, jnp.int32(STEP[name])) & (SIZE[name] - 1)
        sign = 1 - 2 * ((place + odd) & 1)
        targets.append(me + sign * STEP[name])
    return jnp.where((me & 1) == 0, targets[0], targets[1])


def bias_of(partners, me, index):
    target = partner_of(me, index)
    listed = jnp.int32(0)
    for slot in range(1, 7):
        listed = listed | (partners[0, slot] == target).astype(jnp.int32)
    return jnp.where(listed > 0, jnp.float32(0.0), jnp.float32(NEG))


def dot(a, b, da, db):
    return lax.dot_general(a, b, (((da,), (db,)), ((), ())), preferred_element_type=jnp.float32)


KEYS = pl.ds(0, BLOCK)
VALUES = pl.ds(BLOCK, BLOCK)


def lanes_of(head):
    return pl.ds(head * HD, HD)


def summed(items):
    return functools.reduce(jnp.add, items)


def weigh(blocks, biases, asks, heads, before=None):
    span = [lanes_of(head) for head in heads]
    scores = [[dot(block[KEYS, l], asks[KEYS, l], 1, 1) for block in blocks] for l in span]
    grads = [[dot(block[VALUES, l], asks[VALUES, l], 1, 1) for block in blocks] for l in span]
    tops = [
        functools.reduce(
            jnp.maximum,
            [
                jnp.max(s, axis=0, keepdims=True) * SCALE2 + bias[:, l]
                for s, bias in zip(row, biases)
            ]
            + ([before[:, l]] if before is not None else []),
        )
        for row, l in zip(scores, span)
    ]
    weights = [
        [jnp.exp2(s * SCALE2 + (bias[:, l] - top)) for s, bias in zip(row, biases)]
        for row, top, l in zip(scores, tops, span)
    ]
    totals = [summed([jnp.sum(w, axis=0, keepdims=True) for w in row]) for row in weights]
    deltas = [
        summed([jnp.sum(w * g, axis=0, keepdims=True) for w, g in zip(row, more)])
        for row, more in zip(weights, grads)
    ]
    return weights, grads, tops, totals, deltas


def pack_kernel(partners, query, keys, values, dout, own, asks, bias_out, partner_list, sems):
    copies = [
        pltpu.make_async_copy(source, target, sems.at[i])
        for i, (source, target) in enumerate(
            (
                (partners, partner_list),
                (keys, own.at[KEYS, :]),
                (values, own.at[VALUES, :]),
                (query, asks.at[KEYS, :]),
                (dout, asks.at[VALUES, :]),
            )
        )
    ]
    for copy in copies:
        copy.start()
    copies[0].wait()
    me = partner_list[0, 0]
    for index in range(6):
        bias = bias_of(partner_list, me, index)
        bias_out[index : index + 1, :] = jnp.full((1, HEADS * HD), bias, jnp.float32)
    for copy in copies[1:]:
        copy.wait()


def early_kernel(asks, biases, own, *refs):
    blocks, refs = (own,) + refs[:EARLY][::-1], refs[EARLY:]
    weights_out, grads_out, stats_out = refs
    rows = [jnp.zeros((1, HEADS * HD), jnp.float32)]
    rows += [biases[index : index + 1, :] for index in range(EARLY)]
    for heads in GROUPS:
        weights, grads, tops, totals, deltas = weigh(blocks, rows, asks, heads)
        for place, head in enumerate(heads):
            lanes = lanes_of(head)
            for index in range(EARLY + 1):
                weights_out[index, :, lanes] = weights[place][index]
                grads_out[index, :, lanes] = grads[place][index]
            stats_out[0:1, lanes] = tops[place]
            stats_out[1:2, lanes] = totals[place]
            stats_out[2:3, lanes] = deltas[place]


def late_kernel(asks, biases, early_weights, early_grads, stats, *refs):
    late = 6 - EARLY
    blocks, refs = refs[:late][::-1], refs[late:]
    terms, dscores_out, final_out = refs[:6], refs[6], refs[7]
    rows = [biases[index : index + 1, :] for index in range(EARLY, 6)]
    before = stats[0:1, :]
    for heads in GROUPS:
        weights, grads, tops, totals, deltas = weigh(blocks, rows, asks, heads, before)
        spread = []
        for place, head in enumerate(heads):
            lanes = lanes_of(head)
            old = jnp.exp2(before[:, lanes] - tops[place])
            new = 1.0 / (totals[place] + stats[1:2, lanes] * old)
            delta = (deltas[place] + stats[2:3, lanes] * old) * new
            final_out[0:1, lanes] = old * new
            final_out[1:2, lanes] = delta
            spread.append((old * new, new, delta))
        for index in range(6):
            for place, head in enumerate(heads):
                lanes = lanes_of(head)
                old, new, delta = spread[place]
                if index < EARLY:
                    probs = early_weights[index + 1, :, lanes] * old
                    grad = early_grads[index + 1, :, lanes]
                else:
                    probs = weights[place][index - EARLY] * new
                    grad = grads[place][index - EARLY]
                dscores = (probs * (grad - delta)).astype(jnp.bfloat16)
                probs = probs.astype(jnp.bfloat16)
                dscores_out[index, :, lanes] = dscores
                out = terms[index]
                out[KEYS, lanes] = dot(dscores, asks[KEYS, lanes], 1, 0).astype(out.dtype)
                out[VALUES, lanes] = dot(probs, asks[VALUES, lanes], 1, 0).astype(out.dtype)


def own_kernel(asks, early_weights, early_grads, final, dscores, own, *refs):
    blocks, parts, (query_out, own_out) = refs[:6], refs[6 : 6 + SUMMED], refs[6 + SUMMED :]
    for heads in GROUPS:
        span = [lanes_of(head) for head in heads]
        probs = [early_weights[0, :, l] * final[0:1, l] for l in span]
        mine = [
            (p * (early_grads[0, :, l] - final[1:2, l])).astype(jnp.bfloat16)
            for p, l in zip(probs, span)
        ]
        probs = [p.astype(jnp.bfloat16) for p in probs]
        grads = [dot(m, own[KEYS, l], 0, 0) for m, l in zip(mine, span)]
        for index in range(6):
            grads = [
                grad + dot(dscores[index, :, l], blocks[index][KEYS, l], 0, 0)
                for grad, l in zip(grads, span)
            ]
        for low, rows in ((mine, KEYS), (probs, VALUES)):
            totals = [dot(m, asks[rows, l], 1, 0) for m, l in zip(low, span)]
            for total, l in zip(totals, span):
                own_out[rows, l] = total + summed(
                    [part[rows, l].astype(jnp.float32) for part in parts]
                )
        for grad, l in zip(grads, span):
            query_out[:, l] = (grad * SCALE).astype(query_out.dtype)


def sum_kernel(own, *refs):
    parts, (key_out, value_out) = refs[:-2], refs[-2:]
    for rows, out, scale in ((KEYS, key_out, SCALE), (VALUES, value_out, 1.0)):
        total = own[rows, :]
        for part in parts:
            total = total + part[rows, :].astype(jnp.float32)
        out[...] = (total * scale).astype(out.dtype)


FAR = pl.BlockSpec(memory_space=pltpu.HBM)
VM = pl.BlockSpec(memory_space=pltpu.VMEM)
SM = pl.BlockSpec(memory_space=pltpu.SMEM)
WIDE = (2 * BLOCK, HEADS * HD)
NARROW = (BLOCK, HEADS * HD)


NEAR = pltpu.VMEM
PLAIN = jax.ShapeDtypeStruct


def far(array):
    return pltpu.with_memory_space_constraint(array, pltpu.HBM)


def call(kernel, ins, outs, name, scratch=()):
    return pl.pallas_call(
        kernel,
        out_shape=[
            place(shape, dtype) for place, shape, dtype in outs
        ],
        in_specs=ins,
        out_specs=[VM] * len(outs),
        scratch_shapes=list(scratch),
        compiler_params=pltpu.CompilerParams(vmem_limit_bytes=40 * 1024 * 1024),
        name=name,
    )


def on_device(query, keys, values, dout, partners, counts):
    low, full = jnp.bfloat16, jnp.float32
    stats_row = (NEAR, (8, HEADS * HD), full)
    own, asks, biases = call(
        pack_kernel,
        [FAR] * 5,
        [(NEAR, WIDE, low)] * 2 + [stats_row],
        "pack",
        [pltpu.SMEM((1, 7), jnp.int32), pltpu.SemaphoreType.DMA((5,))],
    )(far(partners), far(query), far(keys), far(values), far(dout))
    blocks = [swapped(own, index) for index in range(6)]
    weights, grads, stats = call(
        early_kernel,
        [VM] * (3 + EARLY),
        [(NEAR, (EARLY + 1,) + NARROW, full)] * 2 + [stats_row],
        "early",
    )(asks, biases, own, *blocks[:EARLY][::-1])
    outs = call(
        late_kernel,
        [VM] * (5 + 6 - EARLY),
        [(NEAR, WIDE, low)] * 6 + [(NEAR, (6,) + NARROW, low), stats_row],
        "late",
    )(asks, biases, weights, grads, stats, *blocks[EARLY:][::-1])
    terms, dscores, final = outs[:6], outs[6], outs[7]
    arrived = [swapped(terms[index], index) for index in BACK]
    query_out, own_out = call(
        own_kernel, [VM] * (12 + SUMMED), [(PLAIN, NARROW, low), (NEAR, WIDE, full)], "own"
    )(asks, weights, grads, final, dscores, own, *blocks, *arrived[:SUMMED])
    key_out, value_out = call(sum_kernel, [VM] * (7 - SUMMED), [(PLAIN, NARROW, low)] * 2, "sums")(
        own_out, *arrived[SUMMED:]
    )
    return query_out, key_out, value_out


def solution(mesh):
    tokens = P(AXES, None)
    return jax.shard_map(
        on_device,
        mesh=mesh,
        in_specs=(tokens, tokens, tokens, tokens, tokens, P(AXES)),
        out_specs=(tokens, tokens, tokens),
        check_vma=False,
    )
```

time: 50.2 us -> 49.4 us (0.984)
  Pallas kernels: 8.07 us -> 6.58 us
  waiting for transfers between devices: 5.73 us -> 6.45 us
    pallas_call x3, Pallas kernels: 5.87 us -> 4.5 us  [the longest x1 1.67 us: on_device(): call(late_kernel, [VM] * (5 + 6 - EARLY), [(NEAR, WIDE, low)] * 6 + [(NEA...]
    ppermute x12, waiting for transfers between devices: 5.73 us -> 6.45 us  [swapped(): return lax.ppermute(message, AXES, route_pairs(ROUTES[index]))]
  transfers between devices with their start and end apart: 12 -> 12, of which waited for: 4 -> 4; matrix products, arithmetic and copies ran while one was open for 0% -> 0% of each run, Pallas kernels for 7% -> 6%
where the time goes in v3:
time: 49.4 us; the launch traced here: 49 us
  starting transfers between devices  35.2 us (71%)
  Pallas kernels  6.58 us (13%)
  waiting for transfers between devices  6.45 us (13%)
  between operations  0.8 us (2%)
    ppermute x12, starting transfers between devices, swapped(): return lax.ppermute(message, AXES, route_pairs(ROUTES[index]))  35.2 us
    ppermute x12, waiting for transfers between devices, swapped(): return lax.ppermute(message, AXES, route_pairs(ROUTES[index]))  6.45 us
    pallas_call x1, Pallas kernels, on_device(): call(late_kernel, [VM] * (5 + 6 - EARLY), [(NEAR, WIDE, low)] * 6 + [(NEA...  1.67 us
    pallas_call x1, Pallas kernels, on_device(): call(early_kernel, [VM] * (3 + EARLY), [(NEAR, (EARLY + 1,) + NARROW, ful...  1.57 us
    pallas_call x1, Pallas kernels, on_device(): call(pack_kernel, [FAR] * 5, [(NEAR, WIDE, low)] * 2 + [stats_row], 'pack...  1.26 us
    pallas_call x1, Pallas kernels, on_device(): call(own_kernel, [VM] * (12 + SUMMED), [(PLAIN, NARROW, low), (NEAR, WIDE...  1.26 us
  transfers between devices with their start and end apart: 12, of which 4 were waited for; matrix products, arithmetic and copies ran while one was open for 0% of the time, Pallas kernels for 6%

profile of v3, /device:TPU:211, one launch (start us, length us, event | category | flops | bytes accessed | tf_op | source)
XLA Modules:
  0.0 49.0 jit_solution(12291983192969211436)
XLA Ops:
  0.6 1.3 %pack.1 = (bf16[256,768]{1,0:T(8,128)(2,1)S(1)}, bf16[256,768]{1,0:T(8,128)(2,1)S(1)}, f32[8,768]{1,0:T(8,128)S(1)}) custom-call(s32[1,7]{1,0:T(1,128)} %partners.1, bf16[128,768]{1,0:T(8,128)(2,1)} %query.1, bf16[128,768]{1,0:T(8,128)(2,1)} %keys.1, bf16[128,768]{1,0:T(8,128)(2,1)} %values.1, bf16[128,768]{1,0:T(8,128)(2,1)} %dout.1), custom_call_target="tpu_custom_call" | custom-call | tf_op jit(solution)/shard_map/pack/pallas_call | solution.py:252
  1.9 5.8 %collective-permute-start.3 = (bf16[256,768]{1,0:T(8,128)(2,1)S(1)}, bf16[256,768]{1,0:T(8,128)(2,1)S(1)}, u32[]{:S(2)}, u32[]{:S(2)}) collective-permute-start(bf16[256,768]{1,0:T(8,128)(2,1)S(1)} %get-tuple-element.23.own), channel_id=1, source_target_pairs={{1,2},{2,1},{3,4},{4,3},{5,6},{6,5},{7,8},{8,7},{9,10},{10,9},{11,... | collective-permute-start | bytes 1179656 | tf_op jit(solution)/shard_map/ppermute | solution.py:46
  7.7 2.2 %collective-permute-start.2 = (bf16[256,768]{1,0:T(8,128)(2,1)S(1)}, bf16[256,768]{1,0:T(8,128)(2,1)S(1)}, u32[]{:S(2)}, u32[]{:S(2)}) collective-permute-start(bf16[256,768]{1,0:T(8,128)(2,1)S(1)} %get-tuple-element.23.own), channel_id=1, source_target_pairs={{0,64},{1,17},{2,66},{3,19},{4,68},{5,21},{6,70},{7,23},{8,72},{9,... | collective-permute-start | bytes 1179656 | tf_op jit(solution)/shard_map/ppermute | solution.py:46
  9.9 3.8 %collective-permute-start.1 = (bf16[256,768]{1,0:T(8,128)(2,1)S(1)}, bf16[256,768]{1,0:T(8,128)(2,1)S(1)}, u32[]{:S(2)}, u32[]{:S(2)}) collective-permute-start(bf16[256,768]{1,0:T(8,128)(2,1)S(1)} %get-tuple-element.23.own), channel_id=1, source_target_pairs={{17,33},{19,35},{21,37},{23,39},{25,41},{27,43},{29,45},{31,47},{3... | collective-permute-start | bytes 1179656 | tf_op jit(solution)/shard_map/ppermute | solution.py:46
  13.6 3.2 %collective-permute-start = (bf16[256,768]{1,0:T(8,128)(2,1)S(1)}, bf16[256,768]{1,0:T(8,128)(2,1)S(1)}, u32[]{:S(2)}, u32[]{:S(2)}) collective-permute-start(bf16[256,768]{1,0:T(8,128)(2,1)S(1)} %get-tuple-element.23.own), channel_id=1, source_target_pairs={{0,16},{1,65},{2,18},{3,67},{4,20},{5,69},{6,22},{7,71},{8,24},{9,... | collective-permute-start | bytes 1179656 | tf_op jit(solution)/shard_map/ppermute | solution.py:46
  16.9 1.9 %collective-permute-start.5 = (bf16[256,768]{1,0:T(8,128)(2,1)S(1)}, bf16[256,768]{1,0:T(8,128)(2,1)S(1)}, u32[]{:S(2)}, u32[]{:S(2)}) collective-permute-start(bf16[256,768]{1,0:T(8,128)(2,1)S(1)} %get-tuple-element.23.own), channel_id=1, source_target_pairs={{16,32},{18,34},{20,36},{22,38},{24,40},{26,42},{28,44},{30,46},{3... | collective-permute-start | bytes 1179656 | tf_op jit(solution)/shard_map/ppermute | solution.py:46
  18.8 0.0 collective-permute-done.3.refs_3_.refs_0_
  18.8 1.9 %collective-permute-start.4 = (bf16[256,768]{1,0:T(8,128)(2,1)S(1)}, bf16[256,768]{1,0:T(8,128)(2,1)S(1)}, u32[]{:S(2)}, u32[]{:S(2)}) collective-permute-start(bf16[256,768]{1,0:T(8,128)(2,1)S(1)} %get-tuple-element.23.own), channel_id=1, source_target_pairs={{0,1},{1,0},{2,3},{3,2},{4,5},{5,4},{6,7},{7,6},{8,9},{9,8},{10,11... | collective-permute-start | bytes 1179656 | tf_op jit(solution)/shard_map/ppermute | solution.py:46
  20.7 0.0 collective-permute-done.2.refs_2_.refs_1_
  20.7 0.0 collective-permute-done.1.refs_1_.refs_2_
  20.7 1.7 %collective-permute-done.refs_0_.refs_3_ = bf16[256,768]{1,0:T(8,128)(2,1)S(1)} collective-permute-done((bf16[256,768]{1,0:T(8,128)(2,1)S(1)}, bf16[256,768]{1,0:T(8,128)(2,1)S(1)}, u32[]{:S(2)}, u32[]{:S(2)}) %collective-permute-start) | collective-permute-done | bytes 393248 | tf_op jit(solution)/shard_map/ppermute | solution.py:46
  22.5 1.6 %early.1 = (f32[5,128,768]{2,1,0:T(8,128)S(1)}, f32[5,128,768]{2,1,0:T(8,128)S(1)}, f32[8,768]{1,0:T(8,128)S(1)}) custom-call(bf16[256,768]{1,0:T(8,128)(2,1)S(1)} %get-tuple-element.21.asks, f32[8,768]{1,0:T(8,128)S(1)} %get-tuple-element.22.biases, bf16[256,768]{1,0:T(8,128)(2,1)S(1)} %get-tuple-element.23.own, ...), custom_call_target="tpu_custom_call" | custom-call | tf_op jit(solution)/shard_map/early/pallas_call | solution.py:260
  24.0 1.3 %collective-permute-done.5.refs_1_.refs_4_ = bf16[256,768]{1,0:T(8,128)(2,1)S(1)} collective-permute-done((bf16[256,768]{1,0:T(8,128)(2,1)S(1)}, bf16[256,768]{1,0:T(8,128)(2,1)S(1)}, u32[]{:S(2)}, u32[]{:S(2)}) %collective-permute-start.5) | collective-permute-done | bytes 393248 | tf_op jit(solution)/shard_map/ppermute | solution.py:46
  25.4 0.0 collective-permute-done.4.refs_0_.refs_5_
  25.4 1.7 %late.1 = (bf16[256,768]{1,0:T(8,128)(2,1)S(1)}, bf16[256,768]{1,0:T(8,128)(2,1)S(1)}, bf16[256,768]{1,0:T(8,128)(2,1)S(1)}, bf16[256,768]{1,0:T(8,128)(2,1)S(1)...) custom-call(bf16[256,768]{1,0:T(8,128)(2,1)S(1)} %get-tuple-element., ...), custom_call_target="tpu_custom_call" | custom-call | tf_op jit(solution)/shard_map/late/pallas_call | solution.py:266
  27.1 1.9 %collective-permute-start.6 = (bf16[256,768]{1,0:T(8,128)(2,1)S(1)}, bf16[256,768]{1,0:T(8,128)(2,1)S(1)}, u32[]{:S(2)}, u32[]{:S(2)}) collective-permute-start(bf16[256,768]{1,0:T(8,128)(2,1)S(1)} %get-tuple-element.29), channel_id=1, source_target_pairs={{1,2},{2,1},{3,4},{4,3},{5,6},{6,5},{7,8},{8,7},{9,10},{10,9},{11,... | collective-permute-start | bytes 1179656 | tf_op jit(solution)/shard_map/ppermute | solution.py:46
  29.0 1.9 %collective-permute-start.7 = (bf16[256,768]{1,0:T(8,128)(2,1)S(1)}, bf16[256,768]{1,0:T(8,128)(2,1)S(1)}, u32[]{:S(2)}, u32[]{:S(2)}) collective-permute-start(bf16[256,768]{1,0:T(8,128)(2,1)S(1)} %get-tuple-element.30), channel_id=1, source_target_pairs={{0,64},{1,17},{2,66},{3,19},{4,68},{5,21},{6,70},{7,23},{8,72},{9,... | collective-permute-start | bytes 1179656 | tf_op jit(solution)/shard_map/ppermute | solution.py:46
  30.9 3.6 %collective-permute-start.8 = (bf16[256,768]{1,0:T(8,128)(2,1)S(1)}, bf16[256,768]{1,0:T(8,128)(2,1)S(1)}, u32[]{:S(2)}, u32[]{:S(2)}) collective-permute-start(bf16[256,768]{1,0:T(8,128)(2,1)S(1)} %get-tuple-element.31), channel_id=1, source_target_pairs={{17,33},{19,35},{21,37},{23,39},{25,41},{27,43},{29,45},{31,47},{3... | collective-permute-start | bytes 1179656 | tf_op jit(solution)/shard_map/ppermute | solution.py:46
  34.5 5.1 %collective-permute-start.9 = (bf16[256,768]{1,0:T(8,128)(2,1)S(1)}, bf16[256,768]{1,0:T(8,128)(2,1)S(1)}, u32[]{:S(2)}, u32[]{:S(2)}) collective-permute-start(bf16[256,768]{1,0:T(8,128)(2,1)S(1)} %get-tuple-element.32), channel_id=1, source_target_pairs={{0,16},{1,65},{2,18},{3,67},{4,20},{5,69},{6,22},{7,71},{8,24},{9,... | collective-permute-start | bytes 1179656 | tf_op jit(solution)/shard_map/ppermute | solution.py:46
  39.6 1.9 %collective-permute-start.10 = (bf16[256,768]{1,0:T(8,128)(2,1)S(1)}, bf16[256,768]{1,0:T(8,128)(2,1)S(1)}, u32[]{:S(2)}, u32[]{:S(2)}) collective-permute-start(bf16[256,768]{1,0:T(8,128)(2,1)S(1)} %get-tuple-element.35), channel_id=1, source_target_pairs={{16,32},{18,34},{20,36},{22,38},{24,40},{26,42},{28,44},{30,46},{3... | collective-permute-start | bytes 1179656 | tf_op jit(solution)/shard_map/ppermute | solution.py:46
  41.6 0.0 collective-permute-done.6.refs_6_
  41.6 1.9 %collective-permute-start.11 = (bf16[256,768]{1,0:T(8,128)(2,1)S(1)}, bf16[256,768]{1,0:T(8,128)(2,1)S(1)}, u32[]{:S(2)}, u32[]{:S(2)}) collective-permute-start(bf16[256,768]{1,0:T(8,128)(2,1)S(1)} %get-tuple-element.36), channel_id=1, source_target_pairs={{0,1},{1,0},{2,3},{3,2},{4,5},{5,4},{6,7},{7,6},{8,9},{9,8},{10,11... | collective-permute-start | bytes 1179656 | tf_op jit(solution)/shard_map/ppermute | solution.py:46
  43.5 0.0 collective-permute-done.7.refs_7_
  43.5 0.0 collective-permute-done.8.refs_8_
  43.5 1.3 %collective-permute-done.9.refs_9_ = bf16[256,768]{1,0:T(8,128)(2,1)S(1)} collective-permute-done((bf16[256,768]{1,0:T(8,128)(2,1)S(1)}, bf16[256,768]{1,0:T(8,128)(2,1)S(1)}, u32[]{:S(2)}, u32[]{:S(2)}) %collective-permute-start.9) | collective-permute-done | bytes 393248 | tf_op jit(solution)/shard_map/ppermute | solution.py:46
  44.8 1.3 %own.1 = (bf16[128,768]{1,0:T(8,128)(2,1)}, f32[256,768]{1,0:T(8,128)S(1)}) custom-call(bf16[256,768]{1,0:T(8,128)(2,1)S(1)} %get-tuple-element.21.asks, f32[5,128,768]{2,1,0:T(8,128)S(1)} %get-tuple-element.24.early_weights, f32[5,128,768]{2,1,0:T(8,128)S(1)} %get-tuple-element.25.early_grads, f32[8,768]{1,0:T(8,128)S(1)} %get-tuple-element.27.final, ...), custom_call_target="tpu_custom_call" | custom-call | tf_op jit(solution)/shard_map/own/pallas_call | solution.py:274
  46.0 2.1 %collective-permute-done.10.refs_0_ = bf16[256,768]{1,0:T(8,128)(2,1)S(1)} collective-permute-done((bf16[256,768]{1,0:T(8,128)(2,1)S(1)}, bf16[256,768]{1,0:T(8,128)(2,1)S(1)}, u32[]{:S(2)}, u32[]{:S(2)}) %collective-permute-start.10) | collective-permute-done | bytes 393248 | tf_op jit(solution)/shard_map/ppermute | solution.py:46
  48.2 0.0 collective-permute-done.11.refs_1_
  48.2 0.8 %sums.1 = (bf16[128,768]{1,0:T(8,128)(2,1)}, bf16[128,768]{1,0:T(8,128)(2,1)}) custom-call(f32[256,768]{1,0:T(8,128)S(1)} %get-tuple-element.34.own, bf16[256,768]{1,0:T(8,128)(2,1)S(1)} %collective-permute-done.10.refs_0_, bf16[256,768]{1,0:T(8,128)(2,1)S(1)} %collective-permute-done.11.refs_1_), custom_call_target="tpu_custom_call" | custom-call | tf_op jit(solution)/shard_map/sums/pallas_call | solution.py:277
Async XLA Ops:
  1.9 16.9 %collective-permute-start.3 = (bf16[256,768]{1,0:T(8,128)(2,1)S(1)}, bf16[256,768]{1,0:T(8,128)(2,1)S(1)}, u32[]{:S(2)}, u32[]{:S(2)}) collective-permute-start(bf16[256,768]{1,0:T(8,128)(2,1)S(1)} %get-tuple-element.23.own), channel_id=1, source_target_pairs={{1,2},{2,1},{3,4},{4,3},{5,6},{6,5},{7,8},{8,7},{9,10},{10,9},{11,... | collective-permute-start | bytes 1179656 | tf_op jit(solution)/shard_map/ppermute | solution.py:46
  7.7 13.0 %collective-permute-start.2 = (bf16[256,768]{1,0:T(8,128)(2,1)S(1)}, bf16[256,768]{1,0:T(8,128)(2,1)S(1)}, u32[]{:S(2)}, u32[]{:S(2)}) collective-permute-start(bf16[256,768]{1,0:T(8,128)(2,1)S(1)} %get-tuple-element.23.own), channel_id=1, source_target_pairs={{0,64},{1,17},{2,66},{3,19},{4,68},{5,21},{6,70},{7,23},{8,72},{9,... | collective-permute-start | bytes 1179656 | tf_op jit(solution)/shard_map/ppermute | solution.py:46
  9.9 10.9 %collective-permute-start.1 = (bf16[256,768]{1,0:T(8,128)(2,1)S(1)}, bf16[256,768]{1,0:T(8,128)(2,1)S(1)}, u32[]{:S(2)}, u32[]{:S(2)}) collective-permute-start(bf16[256,768]{1,0:T(8,128)(2,1)S(1)} %get-tuple-element.23.own), channel_id=1, source_target_pairs={{17,33},{19,35},{21,37},{23,39},{25,41},{27,43},{29,45},{31,47},{3... | collective-permute-start | bytes 1179656 | tf_op jit(solution)/shard_map/ppermute | solution.py:46
  13.6 8.8 %collective-permute-start = (bf16[256,768]{1,0:T(8,128)(2,1)S(1)}, bf16[256,768]{1,0:T(8,128)(2,1)S(1)}, u32[]{:S(2)}, u32[]{:S(2)}) collective-permute-start(bf16[256,768]{1,0:T(8,128)(2,1)S(1)} %get-tuple-element.23.own), channel_id=1, source_target_pairs={{0,16},{1,65},{2,18},{3,67},{4,20},{5,69},{6,22},{7,71},{8,24},{9,... | collective-permute-start | bytes 1179656 | tf_op jit(solution)/shard_map/ppermute | solution.py:46
  16.9 8.5 %collective-permute-start.5 = (bf16[256,768]{1,0:T(8,128)(2,1)S(1)}, bf16[256,768]{1,0:T(8,128)(2,1)S(1)}, u32[]{:S(2)}, u32[]{:S(2)}) collective-permute-start(bf16[256,768]{1,0:T(8,128)(2,1)S(1)} %get-tuple-element.23.own), channel_id=1, source_target_pairs={{16,32},{18,34},{20,36},{22,38},{24,40},{26,42},{28,44},{30,46},{3... | collective-permute-start | bytes 1179656 | tf_op jit(solution)/shard_map/ppermute | solution.py:46
  18.8 6.6 %collective-permute-start.4 = (bf16[256,768]{1,0:T(8,128)(2,1)S(1)}, bf16[256,768]{1,0:T(8,128)(2,1)S(1)}, u32[]{:S(2)}, u32[]{:S(2)}) collective-permute-start(bf16[256,768]{1,0:T(8,128)(2,1)S(1)} %get-tuple-element.23.own), channel_id=1, source_target_pairs={{0,1},{1,0},{2,3},{3,2},{4,5},{5,4},{6,7},{7,6},{8,9},{9,8},{10,11... | collective-permute-start | bytes 1179656 | tf_op jit(solution)/shard_map/ppermute | solution.py:46
  27.1 14.5 %collective-permute-start.6 = (bf16[256,768]{1,0:T(8,128)(2,1)S(1)}, bf16[256,768]{1,0:T(8,128)(2,1)S(1)}, u32[]{:S(2)}, u32[]{:S(2)}) collective-permute-start(bf16[256,768]{1,0:T(8,128)(2,1)S(1)} %get-tuple-element.29), channel_id=1, source_target_pairs={{1,2},{2,1},{3,4},{4,3},{5,6},{6,5},{7,8},{8,7},{9,10},{10,9},{11,... | collective-permute-start | bytes 1179656 | tf_op jit(solution)/shard_map/ppermute | solution.py:46
  29.0 14.5 %collective-permute-start.7 = (bf16[256,768]{1,0:T(8,128)(2,1)S(1)}, bf16[256,768]{1,0:T(8,128)(2,1)S(1)}, u32[]{:S(2)}, u32[]{:S(2)}) collective-permute-start(bf16[256,768]{1,0:T(8,128)(2,1)S(1)} %get-tuple-element.30), channel_id=1, source_target_pairs={{0,64},{1,17},{2,66},{3,19},{4,68},{5,21},{6,70},{7,23},{8,72},{9,... | collective-permute-start | bytes 1179656 | tf_op jit(solution)/shard_map/ppermute | solution.py:46
  30.9 12.6 %collective-permute-start.8 = (bf16[256,768]{1,0:T(8,128)(2,1)S(1)}, bf16[256,768]{1,0:T(8,128)(2,1)S(1)}, u32[]{:S(2)}, u32[]{:S(2)}) collective-permute-start(bf16[256,768]{1,0:T(8,128)(2,1)S(1)} %get-tuple-element.31), channel_id=1, source_target_pairs={{17,33},{19,35},{21,37},{23,39},{25,41},{27,43},{29,45},{31,47},{3... | collective-permute-start | bytes 1179656 | tf_op jit(solution)/shard_map/ppermute | solution.py:46
  34.5 10.2 %collective-permute-start.9 = (bf16[256,768]{1,0:T(8,128)(2,1)S(1)}, bf16[256,768]{1,0:T(8,128)(2,1)S(1)}, u32[]{:S(2)}, u32[]{:S(2)}) collective-permute-start(bf16[256,768]{1,0:T(8,128)(2,1)S(1)} %get-tuple-element.32), channel_id=1, source_target_pairs={{0,16},{1,65},{2,18},{3,67},{4,20},{5,69},{6,22},{7,71},{8,24},{9,... | collective-permute-start | bytes 1179656 | tf_op jit(solution)/shard_map/ppermute | solution.py:46
  39.6 8.5 %collective-permute-start.10 = (bf16[256,768]{1,0:T(8,128)(2,1)S(1)}, bf16[256,768]{1,0:T(8,128)(2,1)S(1)}, u32[]{:S(2)}, u32[]{:S(2)}) collective-permute-start(bf16[256,768]{1,0:T(8,128)(2,1)S(1)} %get-tuple-element.35), channel_id=1, source_target_pairs={{16,32},{18,34},{20,36},{22,38},{24,40},{26,42},{28,44},{30,46},{3... | collective-permute-start | bytes 1179656 | tf_op jit(solution)/shard_map/ppermute | solution.py:46
  41.6 6.6 %collective-permute-start.11 = (bf16[256,768]{1,0:T(8,128)(2,1)S(1)}, bf16[256,768]{1,0:T(8,128)(2,1)S(1)}, u32[]{:S(2)}, u32[]{:S(2)}) collective-permute-start(bf16[256,768]{1,0:T(8,128)(2,1)S(1)} %get-tuple-element.36), channel_id=1, source_target_pairs={{0,1},{1,0},{2,3},{3,2},{4,5},{5,4},{6,7},{7,6},{8,9},{9,8},{10,11... | collective-permute-start | bytes 1179656 | tf_op jit(solution)/shard_map/ppermute | solution.py:46

commit v4 on v3

--- a/solution.py
+++ b/solution.py
@@ -28,7 +28,7 @@
 GROUPS = ((0, 1, 2, 3, 4, 5),)
 EARLY = 4
 BACK = (0, 1, 2, 3, 4, 5)
-SUMMED = 4
+SUMMED = 3
 
 
 def route_pairs(route):
@@ -106,21 +106,25 @@
     return weights, grads, tops, totals, deltas
 
 
-def pack_kernel(partners, query, keys, values, dout, own, asks, bias_out, partner_list, sems):
+def copied(pairs, sems):
     copies = [
         pltpu.make_async_copy(source, target, sems.at[i])
-        for i, (source, target) in enumerate(
-            (
-                (partners, partner_list),
-                (keys, own.at[KEYS, :]),
-                (values, own.at[VALUES, :]),
-                (query, asks.at[KEYS, :]),
-                (dout, asks.at[VALUES, :]),
-            )
-        )
+        for i, (source, target) in enumerate(pairs)
     ]
     for copy in copies:
         copy.start()
+    return copies
+
+
+def pack_kernel(keys, values, own, sems):
+    for copy in copied(((keys, own.at[KEYS, :]), (values, own.at[VALUES, :])), sems):
+        copy.wait()
+
+
+def load_kernel(partners, query, dout, asks, bias_out, partner_list, sems):
+    copies = copied(
+        ((partners, partner_list), (query, asks.at[KEYS, :]), (dout, asks.at[VALUES, :])), sems
+    )
     copies[0].wait()
     me = partner_list[0, 0]
     for index in range(6):
@@ -249,13 +253,16 @@
 def on_device(query, keys, values, dout, partners, counts):
     low, full = jnp.bfloat16, jnp.float32
     stats_row = (NEAR, (8, HEADS * HD), full)
-    own, asks, biases = call(
-        pack_kernel,
-        [FAR] * 5,
-        [(NEAR, WIDE, low)] * 2 + [stats_row],
-        "pack",
-        [pltpu.SMEM((1, 7), jnp.int32), pltpu.SemaphoreType.DMA((5,))],
-    )(far(partners), far(query), far(keys), far(values), far(dout))
+    (own,) = call(
+        pack_kernel, [FAR] * 2, [(NEAR, WIDE, low)], "pack", [pltpu.SemaphoreType.DMA((2,))]
+    )(far(keys), far(values))
+    asks, biases = call(
+        load_kernel,
+        [FAR] * 3,
+        [(NEAR, WIDE, low), stats_row],
+        "load",
+        [pltpu.SMEM((1, 7), jnp.int32), pltpu.SemaphoreType.DMA((3,))],
+    )(far(partners), far(query), far(dout))
     blocks = [swapped(own, index) for index in range(6)]
     weights, grads, stats = call(
         early_kernel,

time: 49.4 us -> 49.2 us (level)
  waiting for transfers between devices: 6.45 us -> 5.37 us
  Pallas kernels: 6.58 us -> 7.47 us
    ppermute x12, waiting for transfers between devices: 6.45 us -> 5.37 us  [swapped(): return lax.ppermute(message, AXES, route_pairs(ROUTES[index]))]
    pallas_call x1 -> x2, Pallas kernels: 1.26 us -> 2.09 us  [the longest x1 1.05 us: on_device(): call(load_kernel, [FAR] * 3, [(NEAR, WIDE, low), stats_row], 'load', [plt...]
  transfers between devices with their start and end apart: 12 -> 12, of which waited for: 4 -> 4; matrix products, arithmetic and copies ran while one was open for 0% -> 0% of each run, Pallas kernels for 6% -> 8%
where the time goes in v4:
time: 49.2 us; the launch traced here: 48.8 us
  starting transfers between devices  35.2 us (72%)
  Pallas kernels  7.47 us (15%)
  waiting for transfers between devices  5.37 us (11%)
  between operations  0.81 us (2%)
    ppermute x12, starting transfers between devices, swapped(): return lax.ppermute(message, AXES, route_pairs(ROUTES[index]))  35.2 us
    ppermute x12, waiting for transfers between devices, swapped(): return lax.ppermute(message, AXES, route_pairs(ROUTES[index]))  5.37 us
    pallas_call x1, Pallas kernels, on_device(): call(late_kernel, [VM] * (5 + 6 - EARLY), [(NEAR, WIDE, low)] * 6 + [(NEA...  1.66 us
    pallas_call x1, Pallas kernels, on_device(): call(early_kernel, [VM] * (3 + EARLY), [(NEAR, (EARLY + 1,) + NARROW, ful...  1.58 us
    pallas_call x1, Pallas kernels, on_device(): call(own_kernel, [VM] * (12 + SUMMED), [(PLAIN, NARROW, low), (NEAR, WIDE...  1.27 us
    pallas_call x1, Pallas kernels, on_device(): call(load_kernel, [FAR] * 3, [(NEAR, WIDE, low), stats_row], 'load', [plt...  1.05 us
    pallas_call x1, Pallas kernels, on_device(): call(pack_kernel, [FAR] * 2, [(NEAR, WIDE, low)], 'pack', [pltpu.Semaphor...  1.04 us
  transfers between devices with their start and end apart: 12, of which 4 were waited for; matrix products, arithmetic and copies ran while one was open for 0% of the time, Pallas kernels for 8%

profile of v4, /device:TPU:211, one launch (start us, length us, event | category | flops | bytes accessed | tf_op | source)
XLA Modules:
  0.0 48.8 jit_solution(12487662606830589117)
XLA Ops:
  0.6 1.0 %pack.1.own = bf16[256,768]{1,0:T(8,128)(2,1)S(1)} custom-call(bf16[128,768]{1,0:T(8,128)(2,1)} %keys.1, bf16[128,768]{1,0:T(8,128)(2,1)} %values.1), custom_call_target="tpu_custom_call" | custom-call | tf_op jit(solution)/shard_map/pack/pallas_call | solution.py:256
  1.7 5.8 %collective-permute-start.3 = (bf16[256,768]{1,0:T(8,128)(2,1)S(1)}, bf16[256,768]{1,0:T(8,128)(2,1)S(1)}, u32[]{:S(2)}, u32[]{:S(2)}) collective-permute-start(bf16[256,768]{1,0:T(8,128)(2,1)S(1)} %pack.1.own), channel_id=1, source_target_pairs={{1,2},{2,1},{3,4},{4,3},{5,6},{6,5},{7,8},{8,7},{9,10},{10,9},{11,... | collective-permute-start | bytes 1179656 | tf_op jit(solution)/shard_map/ppermute | solution.py:46
  7.5 2.2 %collective-permute-start.2 = (bf16[256,768]{1,0:T(8,128)(2,1)S(1)}, bf16[256,768]{1,0:T(8,128)(2,1)S(1)}, u32[]{:S(2)}, u32[]{:S(2)}) collective-permute-start(bf16[256,768]{1,0:T(8,128)(2,1)S(1)} %pack.1.own), channel_id=1, source_target_pairs={{0,64},{1,17},{2,66},{3,19},{4,68},{5,21},{6,70},{7,23},{8,72},{9,... | collective-permute-start | bytes 1179656 | tf_op jit(solution)/shard_map/ppermute | solution.py:46
  9.6 3.8 %collective-permute-start.1 = (bf16[256,768]{1,0:T(8,128)(2,1)S(1)}, bf16[256,768]{1,0:T(8,128)(2,1)S(1)}, u32[]{:S(2)}, u32[]{:S(2)}) collective-permute-start(bf16[256,768]{1,0:T(8,128)(2,1)S(1)} %pack.1.own), channel_id=1, source_target_pairs={{17,33},{19,35},{21,37},{23,39},{25,41},{27,43},{29,45},{31,47},{3... | collective-permute-start | bytes 1179656 | tf_op jit(solution)/shard_map/ppermute | solution.py:46
  13.4 3.2 %collective-permute-start = (bf16[256,768]{1,0:T(8,128)(2,1)S(1)}, bf16[256,768]{1,0:T(8,128)(2,1)S(1)}, u32[]{:S(2)}, u32[]{:S(2)}) collective-permute-start(bf16[256,768]{1,0:T(8,128)(2,1)S(1)} %pack.1.own), channel_id=1, source_target_pairs={{0,16},{1,65},{2,18},{3,67},{4,20},{5,69},{6,22},{7,71},{8,24},{9,... | collective-permute-start | bytes 1179656 | tf_op jit(solution)/shard_map/ppermute | solution.py:46
  16.6 1.9 %collective-permute-start.5 = (bf16[256,768]{1,0:T(8,128)(2,1)S(1)}, bf16[256,768]{1,0:T(8,128)(2,1)S(1)}, u32[]{:S(2)}, u32[]{:S(2)}) collective-permute-start(bf16[256,768]{1,0:T(8,128)(2,1)S(1)} %pack.1.own), channel_id=1, source_target_pairs={{16,32},{18,34},{20,36},{22,38},{24,40},{26,42},{28,44},{30,46},{3... | collective-permute-start | bytes 1179656 | tf_op jit(solution)/shard_map/ppermute | solution.py:46
  18.6 0.0 collective-permute-done.3.refs_3_.refs_0_
  18.6 1.9 %collective-permute-start.4 = (bf16[256,768]{1,0:T(8,128)(2,1)S(1)}, bf16[256,768]{1,0:T(8,128)(2,1)S(1)}, u32[]{:S(2)}, u32[]{:S(2)}) collective-permute-start(bf16[256,768]{1,0:T(8,128)(2,1)S(1)} %pack.1.own), channel_id=1, source_target_pairs={{0,1},{1,0},{2,3},{3,2},{4,5},{5,4},{6,7},{7,6},{8,9},{9,8},{10,11... | collective-permute-start | bytes 1179656 | tf_op jit(solution)/shard_map/ppermute | solution.py:46
  20.5 1.1 %load.1 = (bf16[256,768]{1,0:T(8,128)(2,1)S(1)}, f32[8,768]{1,0:T(8,128)S(1)}) custom-call(s32[1,7]{1,0:T(1,128)} %partners.1, bf16[128,768]{1,0:T(8,128)(2,1)} %query.1, bf16[128,768]{1,0:T(8,128)(2,1)} %dout.1), custom_call_target="tpu_custom_call" | custom-call | tf_op jit(solution)/shard_map/load/pallas_call | solution.py:259
  21.6 0.0 collective-permute-done.2.refs_2_.refs_1_
  21.6 0.0 collective-permute-done.1.refs_1_.refs_2_
  21.6 0.7 %collective-permute-done.refs_0_.refs_3_ = bf16[256,768]{1,0:T(8,128)(2,1)S(1)} collective-permute-done((bf16[256,768]{1,0:T(8,128)(2,1)S(1)}, bf16[256,768]{1,0:T(8,128)(2,1)S(1)}, u32[]{:S(2)}, u32[]{:S(2)}) %collective-permute-start) | collective-permute-done | bytes 393248 | tf_op jit(solution)/shard_map/ppermute | solution.py:46
  22.2 1.6 %early.1 = (f32[5,128,768]{2,1,0:T(8,128)S(1)}, f32[5,128,768]{2,1,0:T(8,128)S(1)}, f32[8,768]{1,0:T(8,128)S(1)}) custom-call(bf16[256,768]{1,0:T(8,128)(2,1)S(1)} %get-tuple-element.20.asks, f32[8,768]{1,0:T(8,128)S(1)} %get-tuple-element.21.biases, bf16[256,768]{1,0:T(8,128)(2,1)S(1)} %pack.1.own, ...), custom_call_target="tpu_custom_call" | custom-call | tf_op jit(solution)/shard_map/early/pallas_call | solution.py:267
  23.8 1.3 %collective-permute-done.5.refs_1_.refs_4_ = bf16[256,768]{1,0:T(8,128)(2,1)S(1)} collective-permute-done((bf16[256,768]{1,0:T(8,128)(2,1)S(1)}, bf16[256,768]{1,0:T(8,128)(2,1)S(1)}, u32[]{:S(2)}, u32[]{:S(2)}) %collective-permute-start.5) | collective-permute-done | bytes 393248 | tf_op jit(solution)/shard_map/ppermute | solution.py:46
  25.2 0.0 collective-permute-done.4.refs_0_.refs_5_
  25.2 1.7 %late.1 = (bf16[256,768]{1,0:T(8,128)(2,1)S(1)}, bf16[256,768]{1,0:T(8,128)(2,1)S(1)}, bf16[256,768]{1,0:T(8,128)(2,1)S(1)}, bf16[256,768]{1,0:T(8,128)(2,1)S(1)...) custom-call(bf16[256,768]{1,0:T(8,128)(2,1)S(1)} %get-tuple-element., ...), custom_call_target="tpu_custom_call" | custom-call | tf_op jit(solution)/shard_map/late/pallas_call | solution.py:273
  26.8 1.9 %collective-permute-start.6 = (bf16[256,768]{1,0:T(8,128)(2,1)S(1)}, bf16[256,768]{1,0:T(8,128)(2,1)S(1)}, u32[]{:S(2)}, u32[]{:S(2)}) collective-permute-start(bf16[256,768]{1,0:T(8,128)(2,1)S(1)} %get-tuple-element.27), channel_id=1, source_target_pairs={{1,2},{2,1},{3,4},{4,3},{5,6},{6,5},{7,8},{8,7},{9,10},{10,9},{11,... | collective-permute-start | bytes 1179656 | tf_op jit(solution)/shard_map/ppermute | solution.py:46
  28.8 1.9 %collective-permute-start.7 = (bf16[256,768]{1,0:T(8,128)(2,1)S(1)}, bf16[256,768]{1,0:T(8,128)(2,1)S(1)}, u32[]{:S(2)}, u32[]{:S(2)}) collective-permute-start(bf16[256,768]{1,0:T(8,128)(2,1)S(1)} %get-tuple-element.28), channel_id=1, source_target_pairs={{0,64},{1,17},{2,66},{3,19},{4,68},{5,21},{6,70},{7,23},{8,72},{9,... | collective-permute-start | bytes 1179656 | tf_op jit(solution)/shard_map/ppermute | solution.py:46
  30.7 3.6 %collective-permute-start.8 = (bf16[256,768]{1,0:T(8,128)(2,1)S(1)}, bf16[256,768]{1,0:T(8,128)(2,1)S(1)}, u32[]{:S(2)}, u32[]{:S(2)}) collective-permute-start(bf16[256,768]{1,0:T(8,128)(2,1)S(1)} %get-tuple-element.29), channel_id=1, source_target_pairs={{17,33},{19,35},{21,37},{23,39},{25,41},{27,43},{29,45},{31,47},{3... | collective-permute-start | bytes 1179656 | tf_op jit(solution)/shard_map/ppermute | solution.py:46
  34.3 5.1 %collective-permute-start.9 = (bf16[256,768]{1,0:T(8,128)(2,1)S(1)}, bf16[256,768]{1,0:T(8,128)(2,1)S(1)}, u32[]{:S(2)}, u32[]{:S(2)}) collective-permute-start(bf16[256,768]{1,0:T(8,128)(2,1)S(1)} %get-tuple-element.32), channel_id=1, source_target_pairs={{0,16},{1,65},{2,18},{3,67},{4,20},{5,69},{6,22},{7,71},{8,24},{9,... | collective-permute-start | bytes 1179656 | tf_op jit(solution)/shard_map/ppermute | solution.py:46
  39.4 1.9 %collective-permute-start.10 = (bf16[256,768]{1,0:T(8,128)(2,1)S(1)}, bf16[256,768]{1,0:T(8,128)(2,1)S(1)}, u32[]{:S(2)}, u32[]{:S(2)}) collective-permute-start(bf16[256,768]{1,0:T(8,128)(2,1)S(1)} %get-tuple-element.33), channel_id=1, source_target_pairs={{16,32},{18,34},{20,36},{22,38},{24,40},{26,42},{28,44},{30,46},{3... | collective-permute-start | bytes 1179656 | tf_op jit(solution)/shard_map/ppermute | solution.py:46
  41.3 0.0 collective-permute-done.6.refs_6_
  41.4 1.9 %collective-permute-start.11 = (bf16[256,768]{1,0:T(8,128)(2,1)S(1)}, bf16[256,768]{1,0:T(8,128)(2,1)S(1)}, u32[]{:S(2)}, u32[]{:S(2)}) collective-permute-start(bf16[256,768]{1,0:T(8,128)(2,1)S(1)} %get-tuple-element.34), channel_id=1, source_target_pairs={{0,1},{1,0},{2,3},{3,2},{4,5},{5,4},{6,7},{7,6},{8,9},{9,8},{10,11... | collective-permute-start | bytes 1179656 | tf_op jit(solution)/shard_map/ppermute | solution.py:46
  43.3 0.0 collective-permute-done.7.refs_7_
  43.3 0.0 collective-permute-done.8.refs_8_
  43.3 1.3 %own.1 = (bf16[128,768]{1,0:T(8,128)(2,1)}, f32[256,768]{1,0:T(8,128)S(1)}) custom-call(bf16[256,768]{1,0:T(8,128)(2,1)S(1)} %get-tuple-element.20.asks, f32[5,128,768]{2,1,0:T(8,128)S(1)} %get-tuple-element.22.early_weights, f32[5,128,768]{2,1,0:T(8,128)S(1)} %get-tuple-element.23.early_grads, f32[8,768]{1,0:T(8,128)S(1)} %get-tuple-element.25.final, ...), custom_call_target="tpu_custom_call" | custom-call | tf_op jit(solution)/shard_map/own/pallas_call | solution.py:281
  44.6 0.3 collective-permute-done.9.refs_0_
  44.9 3.1 %collective-permute-done.10.refs_1_ = bf16[256,768]{1,0:T(8,128)(2,1)S(1)} collective-permute-done((bf16[256,768]{1,0:T(8,128)(2,1)S(1)}, bf16[256,768]{1,0:T(8,128)(2,1)S(1)}, u32[]{:S(2)}, u32[]{:S(2)}) %collective-permute-start.10) | collective-permute-done | bytes 393248 | tf_op jit(solution)/shard_map/ppermute | solution.py:46
  47.9 0.0 collective-permute-done.11.refs_2_
  47.9 0.9 %sums.1 = (bf16[128,768]{1,0:T(8,128)(2,1)}, bf16[128,768]{1,0:T(8,128)(2,1)}) custom-call(f32[256,768]{1,0:T(8,128)S(1)} %get-tuple-element.31.own, bf16[256,768]{1,0:T(8,128)(2,1)S(1)} %collective-permute-done.9.refs_0_, bf16[256,768]{1,0:T(8,128)(2,1)S(1)} %collective-permute-done.10.refs_1_, bf16[256,768]{1,0:T(8,128)(2,1)S(1)} %collective-permute-done.11.refs_2_), custom_call_target="tpu_custom_call" | custom-call | tf_op jit(solution)/shard_map/sums/pallas_call | solution.py:284
Async XLA Ops:
  1.7 16.9 %collective-permute-start.3 = (bf16[256,768]{1,0:T(8,128)(2,1)S(1)}, bf16[256,768]{1,0:T(8,128)(2,1)S(1)}, u32[]{:S(2)}, u32[]{:S(2)}) collective-permute-start(bf16[256,768]{1,0:T(8,128)(2,1)S(1)} %pack.1.own), channel_id=1, source_target_pairs={{1,2},{2,1},{3,4},{4,3},{5,6},{6,5},{7,8},{8,7},{9,10},{10,9},{11,... | collective-permute-start | bytes 1179656 | tf_op jit(solution)/shard_map/ppermute | solution.py:46
  7.5 14.1 %collective-permute-start.2 = (bf16[256,768]{1,0:T(8,128)(2,1)S(1)}, bf16[256,768]{1,0:T(8,128)(2,1)S(1)}, u32[]{:S(2)}, u32[]{:S(2)}) collective-permute-start(bf16[256,768]{1,0:T(8,128)(2,1)S(1)} %pack.1.own), channel_id=1, source_target_pairs={{0,64},{1,17},{2,66},{3,19},{4,68},{5,21},{6,70},{7,23},{8,72},{9,... | collective-permute-start | bytes 1179656 | tf_op jit(solution)/shard_map/ppermute | solution.py:46
  9.6 11.9 %collective-permute-start.1 = (bf16[256,768]{1,0:T(8,128)(2,1)S(1)}, bf16[256,768]{1,0:T(8,128)(2,1)S(1)}, u32[]{:S(2)}, u32[]{:S(2)}) collective-permute-start(bf16[256,768]{1,0:T(8,128)(2,1)S(1)} %pack.1.own), channel_id=1, source_target_pairs={{17,33},{19,35},{21,37},{23,39},{25,41},{27,43},{29,45},{31,47},{3... | collective-permute-start | bytes 1179656 | tf_op jit(solution)/shard_map/ppermute | solution.py:46
  13.4 8.8 %collective-permute-start = (bf16[256,768]{1,0:T(8,128)(2,1)S(1)}, bf16[256,768]{1,0:T(8,128)(2,1)S(1)}, u32[]{:S(2)}, u32[]{:S(2)}) collective-permute-start(bf16[256,768]{1,0:T(8,128)(2,1)S(1)} %pack.1.own), channel_id=1, source_target_pairs={{0,16},{1,65},{2,18},{3,67},{4,20},{5,69},{6,22},{7,71},{8,24},{9,... | collective-permute-start | bytes 1179656 | tf_op jit(solution)/shard_map/ppermute | solution.py:46
  16.6 8.5 %collective-permute-start.5 = (bf16[256,768]{1,0:T(8,128)(2,1)S(1)}, bf16[256,768]{1,0:T(8,128)(2,1)S(1)}, u32[]{:S(2)}, u32[]{:S(2)}) collective-permute-start(bf16[256,768]{1,0:T(8,128)(2,1)S(1)} %pack.1.own), channel_id=1, source_target_pairs={{16,32},{18,34},{20,36},{22,38},{24,40},{26,42},{28,44},{30,46},{3... | collective-permute-start | bytes 1179656 | tf_op jit(solution)/shard_map/ppermute | solution.py:46
  18.6 6.6 %collective-permute-start.4 = (bf16[256,768]{1,0:T(8,128)(2,1)S(1)}, bf16[256,768]{1,0:T(8,128)(2,1)S(1)}, u32[]{:S(2)}, u32[]{:S(2)}) collective-permute-start(bf16[256,768]{1,0:T(8,128)(2,1)S(1)} %pack.1.own), channel_id=1, source_target_pairs={{0,1},{1,0},{2,3},{3,2},{4,5},{5,4},{6,7},{7,6},{8,9},{9,8},{10,11... | collective-permute-start | bytes 1179656 | tf_op jit(solution)/shard_map/ppermute | solution.py:46
  26.8 14.5 %collective-permute-start.6 = (bf16[256,768]{1,0:T(8,128)(2,1)S(1)}, bf16[256,768]{1,0:T(8,128)(2,1)S(1)}, u32[]{:S(2)}, u32[]{:S(2)}) collective-permute-start(bf16[256,768]{1,0:T(8,128)(2,1)S(1)} %get-tuple-element.27), channel_id=1, source_target_pairs={{1,2},{2,1},{3,4},{4,3},{5,6},{6,5},{7,8},{8,7},{9,10},{10,9},{11,... | collective-permute-start | bytes 1179656 | tf_op jit(solution)/shard_map/ppermute | solution.py:46
  28.8 14.5 %collective-permute-start.7 = (bf16[256,768]{1,0:T(8,128)(2,1)S(1)}, bf16[256,768]{1,0:T(8,128)(2,1)S(1)}, u32[]{:S(2)}, u32[]{:S(2)}) collective-permute-start(bf16[256,768]{1,0:T(8,128)(2,1)S(1)} %get-tuple-element.28), channel_id=1, source_target_pairs={{0,64},{1,17},{2,66},{3,19},{4,68},{5,21},{6,70},{7,23},{8,72},{9,... | collective-permute-start | bytes 1179656 | tf_op jit(solution)/shard_map/ppermute | solution.py:46
  30.7 12.6 %collective-permute-start.8 = (bf16[256,768]{1,0:T(8,128)(2,1)S(1)}, bf16[256,768]{1,0:T(8,128)(2,1)S(1)}, u32[]{:S(2)}, u32[]{:S(2)}) collective-permute-start(bf16[256,768]{1,0:T(8,128)(2,1)S(1)} %get-tuple-element.29), channel_id=1, source_target_pairs={{17,33},{19,35},{21,37},{23,39},{25,41},{27,43},{29,45},{31,47},{3... | collective-permute-start | bytes 1179656 | tf_op jit(solution)/shard_map/ppermute | solution.py:46
  34.3 10.5 %collective-permute-start.9 = (bf16[256,768]{1,0:T(8,128)(2,1)S(1)}, bf16[256,768]{1,0:T(8,128)(2,1)S(1)}, u32[]{:S(2)}, u32[]{:S(2)}) collective-permute-start(bf16[256,768]{1,0:T(8,128)(2,1)S(1)} %get-tuple-element.32), channel_id=1, source_target_pairs={{0,16},{1,65},{2,18},{3,67},{4,20},{5,69},{6,22},{7,71},{8,24},{9,... | collective-permute-start | bytes 1179656 | tf_op jit(solution)/shard_map/ppermute | solution.py:46
  39.4 8.5 %collective-permute-start.10 = (bf16[256,768]{1,0:T(8,128)(2,1)S(1)}, bf16[256,768]{1,0:T(8,128)(2,1)S(1)}, u32[]{:S(2)}, u32[]{:S(2)}) collective-permute-start(bf16[256,768]{1,0:T(8,128)(2,1)S(1)} %get-tuple-element.33), channel_id=1, source_target_pairs={{16,32},{18,34},{20,36},{22,38},{24,40},{26,42},{28,44},{30,46},{3... | collective-permute-start | bytes 1179656 | tf_op jit(solution)/shard_map/ppermute | solution.py:46
  41.4 6.6 %collective-permute-start.11 = (bf16[256,768]{1,0:T(8,128)(2,1)S(1)}, bf16[256,768]{1,0:T(8,128)(2,1)S(1)}, u32[]{:S(2)}, u32[]{:S(2)}) collective-permute-start(bf16[256,768]{1,0:T(8,128)(2,1)S(1)} %get-tuple-element.34), channel_id=1, source_target_pairs={{0,1},{1,0},{2,3},{3,2},{4,5},{5,4},{6,7},{7,6},{8,9},{9,8},{10,11... | collective-permute-start | bytes 1179656 | tf_op jit(solution)/shard_map/ppermute | solution.py:46

commit v5 on v4

--- a/solution.py
+++ b/solution.py
@@ -26,7 +26,7 @@
     (("z", 0), ("z", 0)),
 )
 GROUPS = ((0, 1, 2, 3, 4, 5),)
-EARLY = 4
+EARLY = 3
 BACK = (0, 1, 2, 3, 4, 5)
 SUMMED = 3
 
@@ -151,11 +151,28 @@
             stats_out[2:3, lanes] = deltas[place]
 
 
-def late_kernel(asks, biases, early_weights, early_grads, stats, *refs):
-    late = 6 - EARLY
+def middle_kernel(asks, biases, stats, block, weights_out, grads_out, stats_out):
+    before = stats[0:1, :]
+    rows = [biases[EARLY : EARLY + 1, :]]
+    for heads in GROUPS:
+        weights, grads, tops, totals, deltas = weigh([block], rows, asks, heads, before)
+        for place, head in enumerate(heads):
+            lanes = lanes_of(head)
+            weights_out[:, lanes] = weights[place][0]
+            grads_out[:, lanes] = grads[place][0]
+            old = jnp.exp2(before[:, lanes] - tops[place])
+            stats_out[0:1, lanes] = tops[place]
+            stats_out[1:2, lanes] = totals[place] + stats[1:2, lanes] * old
+            stats_out[2:3, lanes] = deltas[place] + stats[2:3, lanes] * old
+
+
+def late_kernel(
+    asks, biases, early_weights, early_grads, early_stats, mid_weights, mid_grads, stats, *refs
+):
+    late = 5 - EARLY
     blocks, refs = refs[:late][::-1], refs[late:]
     terms, dscores_out, final_out = refs[:6], refs[6], refs[7]
-    rows = [biases[index : index + 1, :] for index in range(EARLY, 6)]
+    rows = [biases[index : index + 1, :] for index in range(EARLY + 1, 6)]
     before = stats[0:1, :]
     for heads in GROUPS:
         weights, grads, tops, totals, deltas = weigh(blocks, rows, asks, heads, before)
@@ -165,19 +182,22 @@
             old = jnp.exp2(before[:, lanes] - tops[place])
             new = 1.0 / (totals[place] + stats[1:2, lanes] * old)
             delta = (deltas[place] + stats[2:3, lanes] * old) * new
-            final_out[0:1, lanes] = old * new
+            first = jnp.exp2(early_stats[0:1, lanes] - tops[place]) * new
+            final_out[0:1, lanes] = first
             final_out[1:2, lanes] = delta
-            spread.append((old * new, new, delta))
+            spread.append((first, old * new, new, delta))
         for index in range(6):
             for place, head in enumerate(heads):
                 lanes = lanes_of(head)
-                old, new, delta = spread[place]
+                first, old, new, delta = spread[place]
                 if index < EARLY:
-                    probs = early_weights[index + 1, :, lanes] * old
+                    probs = early_weights[index + 1, :, lanes] * first
                     grad = early_grads[index + 1, :, lanes]
+                elif index == EARLY:
+                    probs, grad = mid_weights[:, lanes] * old, mid_grads[:, lanes]
                 else:
-                    probs = weights[place][index - EARLY] * new
-                    grad = grads[place][index - EARLY]
+                    probs = weights[place][index - EARLY - 1] * new
+                    grad = grads[place][index - EARLY - 1]
                 dscores = (probs * (grad - delta)).astype(jnp.bfloat16)
                 probs = probs.astype(jnp.bfloat16)
                 dscores_out[index, :, lanes] = dscores
@@ -213,12 +233,17 @@
 
 
 def sum_kernel(own, *refs):
-    parts, (key_out, value_out) = refs[:-2], refs[-2:]
-    for rows, out, scale in ((KEYS, key_out, SCALE), (VALUES, value_out, 1.0)):
+    parts, (key_out, value_out, held, sems) = refs[:-4], refs[-4:]
+    copies = []
+    for half, rows, out, scale in ((0, VALUES, value_out, 1.0), (1, KEYS, key_out, SCALE)):
         total = own[rows, :]
         for part in parts:
             total = total + part[rows, :].astype(jnp.float32)
-        out[...] = (total * scale).astype(out.dtype)
+        held[half] = (total * scale).astype(held.dtype)
+        copies.append(pltpu.make_async_copy(held.at[half], out, sems.at[half]))
+        copies[-1].start()
+    for copy in copies:
+        copy.wait()
 
 
 FAR = pl.BlockSpec(memory_space=pltpu.HBM)
@@ -230,6 +255,10 @@
 
 NEAR = pltpu.VMEM
 PLAIN = jax.ShapeDtypeStruct
+
+
+def BLOCKED(shape, dtype):
+    return PLAIN(shape, dtype)
 
 
 def far(array):
@@ -243,7 +272,7 @@
             place(shape, dtype) for place, shape, dtype in outs
         ],
         in_specs=ins,
-        out_specs=[VM] * len(outs),
+        out_specs=[FAR if place is PLAIN else VM for place, _, _ in outs],
         scratch_shapes=list(scratch),
         compiler_params=pltpu.CompilerParams(vmem_limit_bytes=40 * 1024 * 1024),
         name=name,
@@ -270,18 +299,26 @@
         [(NEAR, (EARLY + 1,) + NARROW, full)] * 2 + [stats_row],
         "early",
     )(asks, biases, own, *blocks[:EARLY][::-1])
+    mid_weights, mid_grads, mid_stats = call(
+        middle_kernel, [VM] * 4, [(NEAR, NARROW, full)] * 2 + [stats_row], "middle"
+    )(asks, biases, stats, blocks[EARLY])
     outs = call(
         late_kernel,
-        [VM] * (5 + 6 - EARLY),
+        [VM] * (8 + 5 - EARLY),
         [(NEAR, WIDE, low)] * 6 + [(NEAR, (6,) + NARROW, low), stats_row],
         "late",
-    )(asks, biases, weights, grads, stats, *blocks[EARLY:][::-1])
+    )(
+        asks, biases, weights, grads, stats, mid_weights, mid_grads, mid_stats,
+        *blocks[EARLY + 1 :][::-1],
+    )
     terms, dscores, final = outs[:6], outs[6], outs[7]
     arrived = [swapped(terms[index], index) for index in BACK]
     query_out, own_out = call(
-        own_kernel, [VM] * (12 + SUMMED), [(PLAIN, NARROW, low), (NEAR, WIDE, full)], "own"
+        own_kernel, [VM] * (12 + SUMMED), [(BLOCKED, NARROW, low), (NEAR, WIDE, full)], "own"
     )(asks, weights, grads, final, dscores, own, *blocks, *arrived[:SUMMED])
-    key_out, value_out = call(sum_kernel, [VM] * (7 - SUMMED), [(PLAIN, NARROW, low)] * 2, "sums")(
+    key_out, value_out = call(sum_kernel, [VM] * (7 - SUMMED), [(PLAIN, NARROW, low)] * 2, "sums",
+        [pltpu.VMEM((2,) + NARROW, low), pltpu.SemaphoreType.DMA((2,))],
+    )(
         own_out, *arrived[SUMMED:]
     )
     return query_out, key_out, value_out

time: 49.2 us -> 49.2 us (level)
    pallas_call x3 -> x4, Pallas kernels: 3.8 us -> 4.21 us  [the longest x1 1.66 us: on_device(): call(late_kernel, [VM] * (8 + 5 - EARLY), [(NEAR, WIDE, low)] * 6 + [(NEA...]
  transfers between devices with their start and end apart: 12 -> 12, of which waited for: 4 -> 3; matrix products, arithmetic and copies ran while one was open for 0% -> 0% of each run, Pallas kernels for 8% -> 8%
where the time goes in v5:
time: 49.2 us; the launch traced here: 48.8 us
  starting transfers between devices  35.2 us (72%)
  Pallas kernels  7.56 us (15%)
  waiting for transfers between devices  5.27 us (11%)
  between operations  0.82 us (2%)
    ppermute x12, starting transfers between devices, swapped(): return lax.ppermute(message, AXES, route_pairs(ROUTES[index]))  35.2 us
    ppermute x12, waiting for transfers between devices, swapped(): return lax.ppermute(message, AXES, route_pairs(ROUTES[index]))  5.27 us
    pallas_call x1, Pallas kernels, on_device(): call(late_kernel, [VM] * (8 + 5 - EARLY), [(NEAR, WIDE, low)] * 6 + [(NEA...  1.66 us
    pallas_call x1, Pallas kernels, on_device(): call(own_kernel, [VM] * (12 + SUMMED), [(BLOCKED, NARROW, low), (NEAR, WI...  1.27 us
    pallas_call x1, Pallas kernels, on_device(): call(early_kernel, [VM] * (3 + EARLY), [(NEAR, (EARLY + 1,) + NARROW, ful...  1.26 us
    pallas_call x1, Pallas kernels, on_device(): call(load_kernel, [FAR] * 3, [(NEAR, WIDE, low), stats_row], 'load', [plt...  1.05 us
    pallas_call x1, Pallas kernels, on_device(): call(pack_kernel, [FAR] * 2, [(NEAR, WIDE, low)], 'pack', [pltpu.Semaphor...  1.04 us
  transfers between devices with their start and end apart: 12, of which 3 were waited for; matrix products, arithmetic and copies ran while one was open for 0% of the time, Pallas kernels for 8%

profile of v5, /device:TPU:211, one launch (start us, length us, event | category | flops | bytes accessed | tf_op | source)
XLA Modules:
  0.0 48.8 jit_solution(15829034746333770451)
XLA Ops:
  0.6 1.0 %pack.1.own = bf16[256,768]{1,0:T(8,128)(2,1)S(1)} custom-call(bf16[128,768]{1,0:T(8,128)(2,1)} %keys.1, bf16[128,768]{1,0:T(8,128)(2,1)} %values.1), custom_call_target="tpu_custom_call" | custom-call | tf_op jit(solution)/shard_map/pack/pallas_call | solution.py:285
  1.7 5.8 %collective-permute-start.2 = (bf16[256,768]{1,0:T(8,128)(2,1)S(1)}, bf16[256,768]{1,0:T(8,128)(2,1)S(1)}, u32[]{:S(2)}, u32[]{:S(2)}) collective-permute-start(bf16[256,768]{1,0:T(8,128)(2,1)S(1)} %pack.1.own), channel_id=1, source_target_pairs={{1,2},{2,1},{3,4},{4,3},{5,6},{6,5},{7,8},{8,7},{9,10},{10,9},{11,... | collective-permute-start | bytes 1179656 | tf_op jit(solution)/shard_map/ppermute | solution.py:46
  7.5 2.2 %collective-permute-start.1 = (bf16[256,768]{1,0:T(8,128)(2,1)S(1)}, bf16[256,768]{1,0:T(8,128)(2,1)S(1)}, u32[]{:S(2)}, u32[]{:S(2)}) collective-permute-start(bf16[256,768]{1,0:T(8,128)(2,1)S(1)} %pack.1.own), channel_id=1, source_target_pairs={{0,64},{1,17},{2,66},{3,19},{4,68},{5,21},{6,70},{7,23},{8,72},{9,... | collective-permute-start | bytes 1179656 | tf_op jit(solution)/shard_map/ppermute | solution.py:46
  9.6 3.8 %collective-permute-start = (bf16[256,768]{1,0:T(8,128)(2,1)S(1)}, bf16[256,768]{1,0:T(8,128)(2,1)S(1)}, u32[]{:S(2)}, u32[]{:S(2)}) collective-permute-start(bf16[256,768]{1,0:T(8,128)(2,1)S(1)} %pack.1.own), channel_id=1, source_target_pairs={{17,33},{19,35},{21,37},{23,39},{25,41},{27,43},{29,45},{31,47},{3... | collective-permute-start | bytes 1179656 | tf_op jit(solution)/shard_map/ppermute | solution.py:46
  13.4 3.2 %collective-permute-start.3 = (bf16[256,768]{1,0:T(8,128)(2,1)S(1)}, bf16[256,768]{1,0:T(8,128)(2,1)S(1)}, u32[]{:S(2)}, u32[]{:S(2)}) collective-permute-start(bf16[256,768]{1,0:T(8,128)(2,1)S(1)} %pack.1.own), channel_id=1, source_target_pairs={{0,16},{1,65},{2,18},{3,67},{4,20},{5,69},{6,22},{7,71},{8,24},{9,... | collective-permute-start | bytes 1179656 | tf_op jit(solution)/shard_map/ppermute | solution.py:46
  16.6 1.9 %collective-permute-start.5 = (bf16[256,768]{1,0:T(8,128)(2,1)S(1)}, bf16[256,768]{1,0:T(8,128)(2,1)S(1)}, u32[]{:S(2)}, u32[]{:S(2)}) collective-permute-start(bf16[256,768]{1,0:T(8,128)(2,1)S(1)} %pack.1.own), channel_id=1, source_target_pairs={{16,32},{18,34},{20,36},{22,38},{24,40},{26,42},{28,44},{30,46},{3... | collective-permute-start | bytes 1179656 | tf_op jit(solution)/shard_map/ppermute | solution.py:46
  18.6 0.0 collective-permute-done.2.refs_2_.refs_0_
  18.6 1.9 %collective-permute-start.4 = (bf16[256,768]{1,0:T(8,128)(2,1)S(1)}, bf16[256,768]{1,0:T(8,128)(2,1)S(1)}, u32[]{:S(2)}, u32[]{:S(2)}) collective-permute-start(bf16[256,768]{1,0:T(8,128)(2,1)S(1)} %pack.1.own), channel_id=1, source_target_pairs={{0,1},{1,0},{2,3},{3,2},{4,5},{5,4},{6,7},{7,6},{8,9},{9,8},{10,11... | collective-permute-start | bytes 1179656 | tf_op jit(solution)/shard_map/ppermute | solution.py:46
  20.5 1.1 %load.1 = (bf16[256,768]{1,0:T(8,128)(2,1)S(1)}, f32[8,768]{1,0:T(8,128)S(1)}) custom-call(s32[1,7]{1,0:T(1,128)} %partners.1, bf16[128,768]{1,0:T(8,128)(2,1)} %query.1, bf16[128,768]{1,0:T(8,128)(2,1)} %dout.1), custom_call_target="tpu_custom_call" | custom-call | tf_op jit(solution)/shard_map/load/pallas_call | solution.py:288
  21.6 0.0 collective-permute-done.1.refs_1_
  21.6 0.0 collective-permute-done.refs_0_.refs_2_
  21.6 1.3 %early.1 = (f32[4,128,768]{2,1,0:T(8,128)S(1)}, f32[4,128,768]{2,1,0:T(8,128)S(1)}, f32[8,768]{1,0:T(8,128)S(1)}) custom-call(bf16[256,768]{1,0:T(8,128)(2,1)S(1)} %get-tuple-element.23.asks, f32[8,768]{1,0:T(8,128)S(1)} %get-tuple-element.24.biases, bf16[256,768]{1,0:T(8,128)(2,1)S(1)} %pack.1.own, ...), custom_call_target="tpu_custom_call" | custom-call | tf_op jit(solution)/shard_map/early/pallas_call | solution.py:296
  22.8 0.0 collective-permute-done.3.block.refs_3_
  22.9 0.4 middle.1
  23.3 1.9 %collective-permute-done.5.refs_1_.refs_4_ = bf16[256,768]{1,0:T(8,128)(2,1)S(1)} collective-permute-done((bf16[256,768]{1,0:T(8,128)(2,1)S(1)}, bf16[256,768]{1,0:T(8,128)(2,1)S(1)}, u32[]{:S(2)}, u32[]{:S(2)}) %collective-permute-start.5) | collective-permute-done | bytes 393248 | tf_op jit(solution)/shard_map/ppermute | solution.py:46
  25.2 0.0 collective-permute-done.4.refs_0_.refs_5_
  25.2 1.7 %late.1 = (bf16[256,768]{1,0:T(8,128)(2,1)S(1)}, bf16[256,768]{1,0:T(8,128)(2,1)S(1)}, bf16[256,768]{1,0:T(8,128)(2,1)S(1)}, bf16[256,768]{1,0:T(8,128)(2,1)S(1)...) custom-call(bf16[256,768]{1,0:T(8,128)(2,1)S(1)} %get-tuple-element., ...), custom_call_target="tpu_custom_call" | custom-call | tf_op jit(solution)/shard_map/late/pallas_call | solution.py:305
  26.8 1.9 %collective-permute-start.6 = (bf16[256,768]{1,0:T(8,128)(2,1)S(1)}, bf16[256,768]{1,0:T(8,128)(2,1)S(1)}, u32[]{:S(2)}, u32[]{:S(2)}) collective-permute-start(bf16[256,768]{1,0:T(8,128)(2,1)S(1)} %get-tuple-element.33), channel_id=1, source_target_pairs={{1,2},{2,1},{3,4},{4,3},{5,6},{6,5},{7,8},{8,7},{9,10},{10,9},{11,... | collective-permute-start | bytes 1179656 | tf_op jit(solution)/shard_map/ppermute | solution.py:46
  28.7 1.9 %collective-permute-start.7 = (bf16[256,768]{1,0:T(8,128)(2,1)S(1)}, bf16[256,768]{1,0:T(8,128)(2,1)S(1)}, u32[]{:S(2)}, u32[]{:S(2)}) collective-permute-start(bf16[256,768]{1,0:T(8,128)(2,1)S(1)} %get-tuple-element.34), channel_id=1, source_target_pairs={{0,64},{1,17},{2,66},{3,19},{4,68},{5,21},{6,70},{7,23},{8,72},{9,... | collective-permute-start | bytes 1179656 | tf_op jit(solution)/shard_map/ppermute | solution.py:46
  30.7 3.6 %collective-permute-start.8 = (bf16[256,768]{1,0:T(8,128)(2,1)S(1)}, bf16[256,768]{1,0:T(8,128)(2,1)S(1)}, u32[]{:S(2)}, u32[]{:S(2)}) collective-permute-start(bf16[256,768]{1,0:T(8,128)(2,1)S(1)} %get-tuple-element.35), channel_id=1, source_target_pairs={{17,33},{19,35},{21,37},{23,39},{25,41},{27,43},{29,45},{31,47},{3... | collective-permute-start | bytes 1179656 | tf_op jit(solution)/shard_map/ppermute | solution.py:46
  34.3 5.1 %collective-permute-start.9 = (bf16[256,768]{1,0:T(8,128)(2,1)S(1)}, bf16[256,768]{1,0:T(8,128)(2,1)S(1)}, u32[]{:S(2)}, u32[]{:S(2)}) collective-permute-start(bf16[256,768]{1,0:T(8,128)(2,1)S(1)} %get-tuple-element.38), channel_id=1, source_target_pairs={{0,16},{1,65},{2,18},{3,67},{4,20},{5,69},{6,22},{7,71},{8,24},{9,... | collective-permute-start | bytes 1179656 | tf_op jit(solution)/shard_map/ppermute | solution.py:46
  39.4 1.9 %collective-permute-start.10 = (bf16[256,768]{1,0:T(8,128)(2,1)S(1)}, bf16[256,768]{1,0:T(8,128)(2,1)S(1)}, u32[]{:S(2)}, u32[]{:S(2)}) collective-permute-start(bf16[256,768]{1,0:T(8,128)(2,1)S(1)} %get-tuple-element.39), channel_id=1, source_target_pairs={{16,32},{18,34},{20,36},{22,38},{24,40},{26,42},{28,44},{30,46},{3... | collective-permute-start | bytes 1179656 | tf_op jit(solution)/shard_map/ppermute | solution.py:46
  41.3 0.0 collective-permute-done.6.refs_6_
  41.3 1.9 %collective-permute-start.11 = (bf16[256,768]{1,0:T(8,128)(2,1)S(1)}, bf16[256,768]{1,0:T(8,128)(2,1)S(1)}, u32[]{:S(2)}, u32[]{:S(2)}) collective-permute-start(bf16[256,768]{1,0:T(8,128)(2,1)S(1)} %get-tuple-element.40), channel_id=1, source_target_pairs={{0,1},{1,0},{2,3},{3,2},{4,5},{5,4},{6,7},{7,6},{8,9},{9,8},{10,11... | collective-permute-start | bytes 1179656 | tf_op jit(solution)/shard_map/ppermute | solution.py:46
  43.3 0.0 collective-permute-done.7.refs_7_
  43.3 0.0 collective-permute-done.8.refs_8_
  43.3 1.3 %own.1 = (bf16[128,768]{1,0:T(8,128)(2,1)}, f32[256,768]{1,0:T(8,128)S(1)}) custom-call(bf16[256,768]{1,0:T(8,128)(2,1)S(1)} %get-tuple-element.23.asks, f32[4,128,768]{2,1,0:T(8,128)S(1)} %get-tuple-element.25.early_weights, f32[4,128,768]{2,1,0:T(8,128)S(1)} %get-tuple-element.26.early_grads, f32[8,768]{1,0:T(8,128)S(1)} %get-tuple-element.31.final, ...), custom_call_target="tpu_custom_call" | custom-call | tf_op jit(solution)/shard_map/own/pallas_call | solution.py:316
  44.6 0.3 collective-permute-done.9.refs_0_
  44.8 3.1 %collective-permute-done.10.refs_1_ = bf16[256,768]{1,0:T(8,128)(2,1)S(1)} collective-permute-done((bf16[256,768]{1,0:T(8,128)(2,1)S(1)}, bf16[256,768]{1,0:T(8,128)(2,1)S(1)}, u32[]{:S(2)}, u32[]{:S(2)}) %collective-permute-start.10) | collective-permute-done | bytes 393248 | tf_op jit(solution)/shard_map/ppermute | solution.py:46
  47.9 0.0 collective-permute-done.11.refs_2_
  47.9 0.9 %sums.1 = (bf16[128,768]{1,0:T(8,128)(2,1)}, bf16[128,768]{1,0:T(8,128)(2,1)}) custom-call(f32[256,768]{1,0:T(8,128)S(1)} %get-tuple-element.37.own, bf16[256,768]{1,0:T(8,128)(2,1)S(1)} %collective-permute-done.9.refs_0_, bf16[256,768]{1,0:T(8,128)(2,1)S(1)} %collective-permute-done.10.refs_1_, bf16[256,768]{1,0:T(8,128)(2,1)S(1)} %collective-permute-done.11.refs_2_), custom_call_target="tpu_custom_call" | custom-call | tf_op jit(solution)/shard_map/sums/pallas_call | solution.py:319
Async XLA Ops:
  1.7 16.9 %collective-permute-start.2 = (bf16[256,768]{1,0:T(8,128)(2,1)S(1)}, bf16[256,768]{1,0:T(8,128)(2,1)S(1)}, u32[]{:S(2)}, u32[]{:S(2)}) collective-permute-start(bf16[256,768]{1,0:T(8,128)(2,1)S(1)} %pack.1.own), channel_id=1, source_target_pairs={{1,2},{2,1},{3,4},{4,3},{5,6},{6,5},{7,8},{8,7},{9,10},{10,9},{11,... | collective-permute-start | bytes 1179656 | tf_op jit(solution)/shard_map/ppermute | solution.py:46
  7.5 14.1 %collective-permute-start.1 = (bf16[256,768]{1,0:T(8,128)(2,1)S(1)}, bf16[256,768]{1,0:T(8,128)(2,1)S(1)}, u32[]{:S(2)}, u32[]{:S(2)}) collective-permute-start(bf16[256,768]{1,0:T(8,128)(2,1)S(1)} %pack.1.own), channel_id=1, source_target_pairs={{0,64},{1,17},{2,66},{3,19},{4,68},{5,21},{6,70},{7,23},{8,72},{9,... | collective-permute-start | bytes 1179656 | tf_op jit(solution)/shard_map/ppermute | solution.py:46
  9.6 11.9 %collective-permute-start = (bf16[256,768]{1,0:T(8,128)(2,1)S(1)}, bf16[256,768]{1,0:T(8,128)(2,1)S(1)}, u32[]{:S(2)}, u32[]{:S(2)}) collective-permute-start(bf16[256,768]{1,0:T(8,128)(2,1)S(1)} %pack.1.own), channel_id=1, source_target_pairs={{17,33},{19,35},{21,37},{23,39},{25,41},{27,43},{29,45},{31,47},{3... | collective-permute-start | bytes 1179656 | tf_op jit(solution)/shard_map/ppermute | solution.py:46
  13.4 9.4 %collective-permute-start.3 = (bf16[256,768]{1,0:T(8,128)(2,1)S(1)}, bf16[256,768]{1,0:T(8,128)(2,1)S(1)}, u32[]{:S(2)}, u32[]{:S(2)}) collective-permute-start(bf16[256,768]{1,0:T(8,128)(2,1)S(1)} %pack.1.own), channel_id=1, source_target_pairs={{0,16},{1,65},{2,18},{3,67},{4,20},{5,69},{6,22},{7,71},{8,24},{9,... | collective-permute-start | bytes 1179656 | tf_op jit(solution)/shard_map/ppermute | solution.py:46
  16.6 8.5 %collective-permute-start.5 = (bf16[256,768]{1,0:T(8,128)(2,1)S(1)}, bf16[256,768]{1,0:T(8,128)(2,1)S(1)}, u32[]{:S(2)}, u32[]{:S(2)}) collective-permute-start(bf16[256,768]{1,0:T(8,128)(2,1)S(1)} %pack.1.own), channel_id=1, source_target_pairs={{16,32},{18,34},{20,36},{22,38},{24,40},{26,42},{28,44},{30,46},{3... | collective-permute-start | bytes 1179656 | tf_op jit(solution)/shard_map/ppermute | solution.py:46
  18.6 6.6 %collective-permute-start.4 = (bf16[256,768]{1,0:T(8,128)(2,1)S(1)}, bf16[256,768]{1,0:T(8,128)(2,1)S(1)}, u32[]{:S(2)}, u32[]{:S(2)}) collective-permute-start(bf16[256,768]{1,0:T(8,128)(2,1)S(1)} %pack.1.own), channel_id=1, source_target_pairs={{0,1},{1,0},{2,3},{3,2},{4,5},{5,4},{6,7},{7,6},{8,9},{9,8},{10,11... | collective-permute-start | bytes 1179656 | tf_op jit(solution)/shard_map/ppermute | solution.py:46
  26.8 14.5 %collective-permute-start.6 = (bf16[256,768]{1,0:T(8,128)(2,1)S(1)}, bf16[256,768]{1,0:T(8,128)(2,1)S(1)}, u32[]{:S(2)}, u32[]{:S(2)}) collective-permute-start(bf16[256,768]{1,0:T(8,128)(2,1)S(1)} %get-tuple-element.33), channel_id=1, source_target_pairs={{1,2},{2,1},{3,4},{4,3},{5,6},{6,5},{7,8},{8,7},{9,10},{10,9},{11,... | collective-permute-start | bytes 1179656 | tf_op jit(solution)/shard_map/ppermute | solution.py:46
  28.7 14.5 %collective-permute-start.7 = (bf16[256,768]{1,0:T(8,128)(2,1)S(1)}, bf16[256,768]{1,0:T(8,128)(2,1)S(1)}, u32[]{:S(2)}, u32[]{:S(2)}) collective-permute-start(bf16[256,768]{1,0:T(8,128)(2,1)S(1)} %get-tuple-element.34), channel_id=1, source_target_pairs={{0,64},{1,17},{2,66},{3,19},{4,68},{5,21},{6,70},{7,23},{8,72},{9,... | collective-permute-start | bytes 1179656 | tf_op jit(solution)/shard_map/ppermute | solution.py:46
  30.7 12.6 %collective-permute-start.8 = (bf16[256,768]{1,0:T(8,128)(2,1)S(1)}, bf16[256,768]{1,0:T(8,128)(2,1)S(1)}, u32[]{:S(2)}, u32[]{:S(2)}) collective-permute-start(bf16[256,768]{1,0:T(8,128)(2,1)S(1)} %get-tuple-element.35), channel_id=1, source_target_pairs={{17,33},{19,35},{21,37},{23,39},{25,41},{27,43},{29,45},{31,47},{3... | collective-permute-start | bytes 1179656 | tf_op jit(solution)/shard_map/ppermute | solution.py:46
  34.3 10.5 %collective-permute-start.9 = (bf16[256,768]{1,0:T(8,128)(2,1)S(1)}, bf16[256,768]{1,0:T(8,128)(2,1)S(1)}, u32[]{:S(2)}, u32[]{:S(2)}) collective-permute-start(bf16[256,768]{1,0:T(8,128)(2,1)S(1)} %get-tuple-element.38), channel_id=1, source_target_pairs={{0,16},{1,65},{2,18},{3,67},{4,20},{5,69},{6,22},{7,71},{8,24},{9,... | collective-permute-start | bytes 1179656 | tf_op jit(solution)/shard_map/ppermute | solution.py:46
  39.4 8.5 %collective-permute-start.10 = (bf16[256,768]{1,0:T(8,128)(2,1)S(1)}, bf16[256,768]{1,0:T(8,128)(2,1)S(1)}, u32[]{:S(2)}, u32[]{:S(2)}) collective-permute-start(bf16[256,768]{1,0:T(8,128)(2,1)S(1)} %get-tuple-element.39), channel_id=1, source_target_pairs={{16,32},{18,34},{20,36},{22,38},{24,40},{26,42},{28,44},{30,46},{3... | collective-permute-start | bytes 1179656 | tf_op jit(solution)/shard_map/ppermute | solution.py:46
  41.3 6.6 %collective-permute-start.11 = (bf16[256,768]{1,0:T(8,128)(2,1)S(1)}, bf16[256,768]{1,0:T(8,128)(2,1)S(1)}, u32[]{:S(2)}, u32[]{:S(2)}) collective-permute-start(bf16[256,768]{1,0:T(8,128)(2,1)S(1)} %get-tuple-element.40), channel_id=1, source_target_pairs={{0,1},{1,0},{2,3},{3,2},{4,5},{5,4},{6,7},{7,6},{8,9},{9,8},{10,11... | collective-permute-start | bytes 1179656 | tf_op jit(solution)/shard_map/ppermute | solution.py:46

commit v6 on v4

--- a/solution.py
+++ b/solution.py
@@ -19,10 +19,10 @@
 BLOCKS = 512
 ROUTES = (
     (("z", 1), ("z", 1)),
+    (("x", 0), ("y", 0)),
+    (("x", 1), ("y", 1)),
     (("y", 0), ("x", 0)),
     (("y", 1), ("x", 1)),
-    (("x", 0), ("y", 0)),
-    (("x", 1), ("y", 1)),
     (("z", 0), ("z", 0)),
 )
 GROUPS = ((0, 1, 2, 3, 4, 5),)

time: 49.2 us -> 49.2 us (level)
  the two profiles are of different devices: /device:TPU:211 before, /device:TPU:219 now
where the time goes in v6:
time: 49.2 us; the launch traced here: 48.7 us
  starting transfers between devices  36.6 us (74%)
  Pallas kernels  7.47 us (15%)
  waiting for transfers between devices  3.79 us (8%)
  between operations  0.81 us (2%)
    ppermute x12, starting transfers between devices, swapped(): return lax.ppermute(message, AXES, route_pairs(ROUTES[index]))  36.6 us
    ppermute x12, waiting for transfers between devices, swapped(): return lax.ppermute(message, AXES, route_pairs(ROUTES[index]))  3.79 us
    pallas_call x1, Pallas kernels, on_device(): call(late_kernel, [VM] * (5 + 6 - EARLY), [(NEAR, WIDE, low)] * 6 + [(NEA...  1.66 us
    pallas_call x1, Pallas kernels, on_device(): call(early_kernel, [VM] * (3 + EARLY), [(NEAR, (EARLY + 1,) + NARROW, ful...  1.58 us
    pallas_call x1, Pallas kernels, on_device(): call(own_kernel, [VM] * (12 + SUMMED), [(PLAIN, NARROW, low), (NEAR, WIDE...  1.27 us
    pallas_call x1, Pallas kernels, on_device(): call(load_kernel, [FAR] * 3, [(NEAR, WIDE, low), stats_row], 'load', [plt...  1.05 us
    pallas_call x1, Pallas kernels, on_device(): call(pack_kernel, [FAR] * 2, [(NEAR, WIDE, low)], 'pack', [pltpu.Semaphor...  1.04 us
  transfers between devices with their start and end apart: 12, of which 3 were waited for; matrix products, arithmetic and copies ran while one was open for 0% of the time, Pallas kernels for 8%

profile of v6, /device:TPU:219, one launch (start us, length us, event | category | flops | bytes accessed | tf_op | source)
XLA Modules:
  0.0 48.7 jit_solution(5264053700649894725)
XLA Ops:
  0.6 1.0 %pack.1.own = bf16[256,768]{1,0:T(8,128)(2,1)S(1)} custom-call(bf16[128,768]{1,0:T(8,128)(2,1)} %keys.1, bf16[128,768]{1,0:T(8,128)(2,1)} %values.1), custom_call_target="tpu_custom_call" | custom-call | tf_op jit(solution)/shard_map/pack/pallas_call | solution.py:256
  1.7 5.8 %collective-permute-start.3 = (bf16[256,768]{1,0:T(8,128)(2,1)S(1)}, bf16[256,768]{1,0:T(8,128)(2,1)S(1)}, u32[]{:S(2)}, u32[]{:S(2)}) collective-permute-start(bf16[256,768]{1,0:T(8,128)(2,1)S(1)} %pack.1.own), channel_id=1, source_target_pairs={{1,2},{2,1},{3,4},{4,3},{5,6},{6,5},{7,8},{8,7},{9,10},{10,9},{11,... | collective-permute-start | bytes 1179656 | tf_op jit(solution)/shard_map/ppermute | solution.py:46
  7.5 2.1 %collective-permute-start.2 = (bf16[256,768]{1,0:T(8,128)(2,1)S(1)}, bf16[256,768]{1,0:T(8,128)(2,1)S(1)}, u32[]{:S(2)}, u32[]{:S(2)}) collective-permute-start(bf16[256,768]{1,0:T(8,128)(2,1)S(1)} %pack.1.own), channel_id=1, source_target_pairs={{0,16},{1,65},{2,18},{3,67},{4,20},{5,69},{6,22},{7,71},{8,24},{9,... | collective-permute-start | bytes 1179656 | tf_op jit(solution)/shard_map/ppermute | solution.py:46
  9.5 4.6 %collective-permute-start.1 = (bf16[256,768]{1,0:T(8,128)(2,1)S(1)}, bf16[256,768]{1,0:T(8,128)(2,1)S(1)}, u32[]{:S(2)}, u32[]{:S(2)}) collective-permute-start(bf16[256,768]{1,0:T(8,128)(2,1)S(1)} %pack.1.own), channel_id=1, source_target_pairs={{16,32},{18,34},{20,36},{22,38},{24,40},{26,42},{28,44},{30,46},{3... | collective-permute-start | bytes 1179656 | tf_op jit(solution)/shard_map/ppermute | solution.py:46
  14.2 2.2 %collective-permute-start = (bf16[256,768]{1,0:T(8,128)(2,1)S(1)}, bf16[256,768]{1,0:T(8,128)(2,1)S(1)}, u32[]{:S(2)}, u32[]{:S(2)}) collective-permute-start(bf16[256,768]{1,0:T(8,128)(2,1)S(1)} %pack.1.own), channel_id=1, source_target_pairs={{0,64},{1,17},{2,66},{3,19},{4,68},{5,21},{6,70},{7,23},{8,72},{9,... | collective-permute-start | bytes 1179656 | tf_op jit(solution)/shard_map/ppermute | solution.py:46
  16.4 3.8 %collective-permute-start.5 = (bf16[256,768]{1,0:T(8,128)(2,1)S(1)}, bf16[256,768]{1,0:T(8,128)(2,1)S(1)}, u32[]{:S(2)}, u32[]{:S(2)}) collective-permute-start(bf16[256,768]{1,0:T(8,128)(2,1)S(1)} %pack.1.own), channel_id=1, source_target_pairs={{17,33},{19,35},{21,37},{23,39},{25,41},{27,43},{29,45},{31,47},{3... | collective-permute-start | bytes 1179656 | tf_op jit(solution)/shard_map/ppermute | solution.py:46
  20.2 0.0 collective-permute-done.3.refs_3_.refs_0_
  20.2 1.9 %collective-permute-start.4 = (bf16[256,768]{1,0:T(8,128)(2,1)S(1)}, bf16[256,768]{1,0:T(8,128)(2,1)S(1)}, u32[]{:S(2)}, u32[]{:S(2)}) collective-permute-start(bf16[256,768]{1,0:T(8,128)(2,1)S(1)} %pack.1.own), channel_id=1, source_target_pairs={{0,1},{1,0},{2,3},{3,2},{4,5},{5,4},{6,7},{7,6},{8,9},{9,8},{10,11... | collective-permute-start | bytes 1179656 | tf_op jit(solution)/shard_map/ppermute | solution.py:46
  22.1 1.1 %load.1 = (bf16[256,768]{1,0:T(8,128)(2,1)S(1)}, f32[8,768]{1,0:T(8,128)S(1)}) custom-call(s32[1,7]{1,0:T(1,128)} %partners.1, bf16[128,768]{1,0:T(8,128)(2,1)} %query.1, bf16[128,768]{1,0:T(8,128)(2,1)} %dout.1), custom_call_target="tpu_custom_call" | custom-call | tf_op jit(solution)/shard_map/load/pallas_call | solution.py:259
  23.2 0.0 collective-permute-done.2.refs_2_.refs_1_
  23.2 0.0 collective-permute-done.1.refs_1_.refs_2_
  23.2 0.0 collective-permute-done.refs_0_.refs_3_
  23.2 1.6 %early.1 = (f32[5,128,768]{2,1,0:T(8,128)S(1)}, f32[5,128,768]{2,1,0:T(8,128)S(1)}, f32[8,768]{1,0:T(8,128)S(1)}) custom-call(bf16[256,768]{1,0:T(8,128)(2,1)S(1)} %get-tuple-element.20.asks, f32[8,768]{1,0:T(8,128)S(1)} %get-tuple-element.21.biases, bf16[256,768]{1,0:T(8,128)(2,1)S(1)} %pack.1.own, ...), custom_call_target="tpu_custom_call" | custom-call | tf_op jit(solution)/shard_map/early/pallas_call | solution.py:267
  24.8 0.5 %collective-permute-done.5.refs_1_.refs_4_ = bf16[256,768]{1,0:T(8,128)(2,1)S(1)} collective-permute-done((bf16[256,768]{1,0:T(8,128)(2,1)S(1)}, bf16[256,768]{1,0:T(8,128)(2,1)S(1)}, u32[]{:S(2)}, u32[]{:S(2)}) %collective-permute-start.5) | collective-permute-done | bytes 393248 | tf_op jit(solution)/shard_map/ppermute | solution.py:46
  25.3 0.0 collective-permute-done.4.refs_0_.refs_5_
  25.3 1.7 %late.1 = (bf16[256,768]{1,0:T(8,128)(2,1)S(1)}, bf16[256,768]{1,0:T(8,128)(2,1)S(1)}, bf16[256,768]{1,0:T(8,128)(2,1)S(1)}, bf16[256,768]{1,0:T(8,128)(2,1)S(1)...) custom-call(bf16[256,768]{1,0:T(8,128)(2,1)S(1)} %get-tuple-element., ...), custom_call_target="tpu_custom_call" | custom-call | tf_op jit(solution)/shard_map/late/pallas_call | solution.py:273
  27.0 3.8 %collective-permute-start.6 = (bf16[256,768]{1,0:T(8,128)(2,1)S(1)}, bf16[256,768]{1,0:T(8,128)(2,1)S(1)}, u32[]{:S(2)}, u32[]{:S(2)}) collective-permute-start(bf16[256,768]{1,0:T(8,128)(2,1)S(1)} %get-tuple-element.27), channel_id=1, source_target_pairs={{1,2},{2,1},{3,4},{4,3},{5,6},{6,5},{7,8},{8,7},{9,10},{10,9},{11,... | collective-permute-start | bytes 1179656 | tf_op jit(solution)/shard_map/ppermute | solution.py:46
  30.8 2.0 %collective-permute-start.7 = (bf16[256,768]{1,0:T(8,128)(2,1)S(1)}, bf16[256,768]{1,0:T(8,128)(2,1)S(1)}, u32[]{:S(2)}, u32[]{:S(2)}) collective-permute-start(bf16[256,768]{1,0:T(8,128)(2,1)S(1)} %get-tuple-element.28), channel_id=1, source_target_pairs={{0,16},{1,65},{2,18},{3,67},{4,20},{5,69},{6,22},{7,71},{8,24},{9,... | collective-permute-start | bytes 1179656 | tf_op jit(solution)/shard_map/ppermute | solution.py:46
  32.8 4.6 %collective-permute-start.8 = (bf16[256,768]{1,0:T(8,128)(2,1)S(1)}, bf16[256,768]{1,0:T(8,128)(2,1)S(1)}, u32[]{:S(2)}, u32[]{:S(2)}) collective-permute-start(bf16[256,768]{1,0:T(8,128)(2,1)S(1)} %get-tuple-element.29), channel_id=1, source_target_pairs={{16,32},{18,34},{20,36},{22,38},{24,40},{26,42},{28,44},{30,46},{3... | collective-permute-start | bytes 1179656 | tf_op jit(solution)/shard_map/ppermute | solution.py:46
  37.4 1.9 %collective-permute-start.9 = (bf16[256,768]{1,0:T(8,128)(2,1)S(1)}, bf16[256,768]{1,0:T(8,128)(2,1)S(1)}, u32[]{:S(2)}, u32[]{:S(2)}) collective-permute-start(bf16[256,768]{1,0:T(8,128)(2,1)S(1)} %get-tuple-element.32), channel_id=1, source_target_pairs={{0,64},{1,17},{2,66},{3,19},{4,68},{5,21},{6,70},{7,23},{8,72},{9,... | collective-permute-start | bytes 1179656 | tf_op jit(solution)/shard_map/ppermute | solution.py:46
  39.3 2.0 %collective-permute-start.10 = (bf16[256,768]{1,0:T(8,128)(2,1)S(1)}, bf16[256,768]{1,0:T(8,128)(2,1)S(1)}, u32[]{:S(2)}, u32[]{:S(2)}) collective-permute-start(bf16[256,768]{1,0:T(8,128)(2,1)S(1)} %get-tuple-element.33), channel_id=1, source_target_pairs={{17,33},{19,35},{21,37},{23,39},{25,41},{27,43},{29,45},{31,47},{3... | collective-permute-start | bytes 1179656 | tf_op jit(solution)/shard_map/ppermute | solution.py:46
  41.4 0.0 collective-permute-done.6.refs_6_
  41.4 1.9 %collective-permute-start.11 = (bf16[256,768]{1,0:T(8,128)(2,1)S(1)}, bf16[256,768]{1,0:T(8,128)(2,1)S(1)}, u32[]{:S(2)}, u32[]{:S(2)}) collective-permute-start(bf16[256,768]{1,0:T(8,128)(2,1)S(1)} %get-tuple-element.34), channel_id=1, source_target_pairs={{0,1},{1,0},{2,3},{3,2},{4,5},{5,4},{6,7},{7,6},{8,9},{9,8},{10,11... | collective-permute-start | bytes 1179656 | tf_op jit(solution)/shard_map/ppermute | solution.py:46
  43.3 0.0 collective-permute-done.7.refs_7_
  43.3 0.0 collective-permute-done.8.refs_8_
  43.3 1.3 %own.1 = (bf16[128,768]{1,0:T(8,128)(2,1)}, f32[256,768]{1,0:T(8,128)S(1)}) custom-call(bf16[256,768]{1,0:T(8,128)(2,1)S(1)} %get-tuple-element.20.asks, f32[5,128,768]{2,1,0:T(8,128)S(1)} %get-tuple-element.22.early_weights, f32[5,128,768]{2,1,0:T(8,128)S(1)} %get-tuple-element.23.early_grads, f32[8,768]{1,0:T(8,128)S(1)} %get-tuple-element.25.final, ...), custom_call_target="tpu_custom_call" | custom-call | tf_op jit(solution)/shard_map/own/pallas_call | solution.py:281
  44.6 1.6 %collective-permute-done.9.refs_0_ = bf16[256,768]{1,0:T(8,128)(2,1)S(1)} collective-permute-done((bf16[256,768]{1,0:T(8,128)(2,1)S(1)}, bf16[256,768]{1,0:T(8,128)(2,1)S(1)}, u32[]{:S(2)}, u32[]{:S(2)}) %collective-permute-start.9) | collective-permute-done | bytes 393248 | tf_op jit(solution)/shard_map/ppermute | solution.py:46
  46.2 1.6 %collective-permute-done.10.refs_1_ = bf16[256,768]{1,0:T(8,128)(2,1)S(1)} collective-permute-done((bf16[256,768]{1,0:T(8,128)(2,1)S(1)}, bf16[256,768]{1,0:T(8,128)(2,1)S(1)}, u32[]{:S(2)}, u32[]{:S(2)}) %collective-permute-start.10) | collective-permute-done | bytes 393248 | tf_op jit(solution)/shard_map/ppermute | solution.py:46
  47.9 0.0 collective-permute-done.11.refs_2_
  47.9 0.9 %sums.1 = (bf16[128,768]{1,0:T(8,128)(2,1)}, bf16[128,768]{1,0:T(8,128)(2,1)}) custom-call(f32[256,768]{1,0:T(8,128)S(1)} %get-tuple-element.31.own, bf16[256,768]{1,0:T(8,128)(2,1)S(1)} %collective-permute-done.9.refs_0_, bf16[256,768]{1,0:T(8,128)(2,1)S(1)} %collective-permute-done.10.refs_1_, bf16[256,768]{1,0:T(8,128)(2,1)S(1)} %collective-permute-done.11.refs_2_), custom_call_target="tpu_custom_call" | custom-call | tf_op jit(solution)/shard_map/sums/pallas_call | solution.py:284
Async XLA Ops:
  1.7 18.5 %collective-permute-start.3 = (bf16[256,768]{1,0:T(8,128)(2,1)S(1)}, bf16[256,768]{1,0:T(8,128)(2,1)S(1)}, u32[]{:S(2)}, u32[]{:S(2)}) collective-permute-start(bf16[256,768]{1,0:T(8,128)(2,1)S(1)} %pack.1.own), channel_id=1, source_target_pairs={{1,2},{2,1},{3,4},{4,3},{5,6},{6,5},{7,8},{8,7},{9,10},{10,9},{11,... | collective-permute-start | bytes 1179656 | tf_op jit(solution)/shard_map/ppermute | solution.py:46
  7.5 15.7 %collective-permute-start.2 = (bf16[256,768]{1,0:T(8,128)(2,1)S(1)}, bf16[256,768]{1,0:T(8,128)(2,1)S(1)}, u32[]{:S(2)}, u32[]{:S(2)}) collective-permute-start(bf16[256,768]{1,0:T(8,128)(2,1)S(1)} %pack.1.own), channel_id=1, source_target_pairs={{0,16},{1,65},{2,18},{3,67},{4,20},{5,69},{6,22},{7,71},{8,24},{9,... | collective-permute-start | bytes 1179656 | tf_op jit(solution)/shard_map/ppermute | solution.py:46
  9.5 13.6 %collective-permute-start.1 = (bf16[256,768]{1,0:T(8,128)(2,1)S(1)}, bf16[256,768]{1,0:T(8,128)(2,1)S(1)}, u32[]{:S(2)}, u32[]{:S(2)}) collective-permute-start(bf16[256,768]{1,0:T(8,128)(2,1)S(1)} %pack.1.own), channel_id=1, source_target_pairs={{16,32},{18,34},{20,36},{22,38},{24,40},{26,42},{28,44},{30,46},{3... | collective-permute-start | bytes 1179656 | tf_op jit(solution)/shard_map/ppermute | solution.py:46
  14.2 9.0 %collective-permute-start = (bf16[256,768]{1,0:T(8,128)(2,1)S(1)}, bf16[256,768]{1,0:T(8,128)(2,1)S(1)}, u32[]{:S(2)}, u32[]{:S(2)}) collective-permute-start(bf16[256,768]{1,0:T(8,128)(2,1)S(1)} %pack.1.own), channel_id=1, source_target_pairs={{0,64},{1,17},{2,66},{3,19},{4,68},{5,21},{6,70},{7,23},{8,72},{9,... | collective-permute-start | bytes 1179656 | tf_op jit(solution)/shard_map/ppermute | solution.py:46
  16.4 8.9 %collective-permute-start.5 = (bf16[256,768]{1,0:T(8,128)(2,1)S(1)}, bf16[256,768]{1,0:T(8,128)(2,1)S(1)}, u32[]{:S(2)}, u32[]{:S(2)}) collective-permute-start(bf16[256,768]{1,0:T(8,128)(2,1)S(1)} %pack.1.own), channel_id=1, source_target_pairs={{17,33},{19,35},{21,37},{23,39},{25,41},{27,43},{29,45},{31,47},{3... | collective-permute-start | bytes 1179656 | tf_op jit(solution)/shard_map/ppermute | solution.py:46
  20.2 5.1 %collective-permute-start.4 = (bf16[256,768]{1,0:T(8,128)(2,1)S(1)}, bf16[256,768]{1,0:T(8,128)(2,1)S(1)}, u32[]{:S(2)}, u32[]{:S(2)}) collective-permute-start(bf16[256,768]{1,0:T(8,128)(2,1)S(1)} %pack.1.own), channel_id=1, source_target_pairs={{0,1},{1,0},{2,3},{3,2},{4,5},{5,4},{6,7},{7,6},{8,9},{9,8},{10,11... | collective-permute-start | bytes 1179656 | tf_op jit(solution)/shard_map/ppermute | solution.py:46
  27.0 14.4 %collective-permute-start.6 = (bf16[256,768]{1,0:T(8,128)(2,1)S(1)}, bf16[256,768]{1,0:T(8,128)(2,1)S(1)}, u32[]{:S(2)}, u32[]{:S(2)}) collective-permute-start(bf16[256,768]{1,0:T(8,128)(2,1)S(1)} %get-tuple-element.27), channel_id=1, source_target_pairs={{1,2},{2,1},{3,4},{4,3},{5,6},{6,5},{7,8},{8,7},{9,10},{10,9},{11,... | collective-permute-start | bytes 1179656 | tf_op jit(solution)/shard_map/ppermute | solution.py:46
  30.8 12.5 %collective-permute-start.7 = (bf16[256,768]{1,0:T(8,128)(2,1)S(1)}, bf16[256,768]{1,0:T(8,128)(2,1)S(1)}, u32[]{:S(2)}, u32[]{:S(2)}) collective-permute-start(bf16[256,768]{1,0:T(8,128)(2,1)S(1)} %get-tuple-element.28), channel_id=1, source_target_pairs={{0,16},{1,65},{2,18},{3,67},{4,20},{5,69},{6,22},{7,71},{8,24},{9,... | collective-permute-start | bytes 1179656 | tf_op jit(solution)/shard_map/ppermute | solution.py:46
  32.8 10.5 %collective-permute-start.8 = (bf16[256,768]{1,0:T(8,128)(2,1)S(1)}, bf16[256,768]{1,0:T(8,128)(2,1)S(1)}, u32[]{:S(2)}, u32[]{:S(2)}) collective-permute-start(bf16[256,768]{1,0:T(8,128)(2,1)S(1)} %get-tuple-element.29), channel_id=1, source_target_pairs={{16,32},{18,34},{20,36},{22,38},{24,40},{26,42},{28,44},{30,46},{3... | collective-permute-start | bytes 1179656 | tf_op jit(solution)/shard_map/ppermute | solution.py:46
  37.4 8.8 %collective-permute-start.9 = (bf16[256,768]{1,0:T(8,128)(2,1)S(1)}, bf16[256,768]{1,0:T(8,128)(2,1)S(1)}, u32[]{:S(2)}, u32[]{:S(2)}) collective-permute-start(bf16[256,768]{1,0:T(8,128)(2,1)S(1)} %get-tuple-element.32), channel_id=1, source_target_pairs={{0,64},{1,17},{2,66},{3,19},{4,68},{5,21},{6,70},{7,23},{8,72},{9,... | collective-permute-start | bytes 1179656 | tf_op jit(solution)/shard_map/ppermute | solution.py:46
  39.3 8.5 %collective-permute-start.10 = (bf16[256,768]{1,0:T(8,128)(2,1)S(1)}, bf16[256,768]{1,0:T(8,128)(2,1)S(1)}, u32[]{:S(2)}, u32[]{:S(2)}) collective-permute-start(bf16[256,768]{1,0:T(8,128)(2,1)S(1)} %get-tuple-element.33), channel_id=1, source_target_pairs={{17,33},{19,35},{21,37},{23,39},{25,41},{27,43},{29,45},{31,47},{3... | collective-permute-start | bytes 1179656 | tf_op jit(solution)/shard_map/ppermute | solution.py:46
  41.4 6.5 %collective-permute-start.11 = (bf16[256,768]{1,0:T(8,128)(2,1)S(1)}, bf16[256,768]{1,0:T(8,128)(2,1)S(1)}, u32[]{:S(2)}, u32[]{:S(2)}) collective-permute-start(bf16[256,768]{1,0:T(8,128)(2,1)S(1)} %get-tuple-element.34), channel_id=1, source_target_pairs={{0,1},{1,0},{2,3},{3,2},{4,5},{5,4},{6,7},{7,6},{8,9},{9,8},{10,11... | collective-permute-start | bytes 1179656 | tf_op jit(solution)/shard_map/ppermute | solution.py:46
